TPU v7x, 32 devices: a whole 2x2x4 slice. The times are simulated.
32 devices in a mesh: dp: 4 (over x, core), fsdp: 8 (over z, y).
Axes of the slice: x: 2, y: 2, z: 4, core: 2. Of those that a mesh axis runs over, the one named last changes fastest.
Arguments:
- inputs: bfloat16 [16384, 768], P(('dp', 'fsdp')), may hold values from -6 to 6
- cotangent: bfloat16 [16384, 768], P(('dp', 'fsdp')), may hold values from -6 to 6
- lengths: int32 [128], P(('dp', 'fsdp')), may hold values from 96 to 128, as said below
- tags: int32 [128, 1], P(('dp', 'fsdp')), may hold values from 0 to 1; in each aligned block of 4 rows (0 to 3, 4 to 7, ...) at most 3 rows name the same one
- query_weight: bfloat16 [2, 768, 768], P(None, ('dp', 'fsdp')), may hold values from -0.21875 to 0.21875
- query_bias: bfloat16 [2, 768], P(None, ('dp', 'fsdp')), may hold values from -3 to 3
- key_weight: bfloat16 [2, 768, 768], P(None, ('dp', 'fsdp')), may hold values from -0.21875 to 0.21875
- value_weight: bfloat16 [2, 768, 768], P(None, ('dp', 'fsdp')), may hold values from -0.21875 to 0.21875
- value_bias: bfloat16 [2, 768], P(None, ('dp', 'fsdp')), may hold values from -1.75 to 1.75
- output_projection_weight: bfloat16 [2, 768, 768], P(None, ('dp', 'fsdp')), may hold values from -0.875 to 0.875
- out_bias: bfloat16 [2, 768], P(None, ('dp', 'fsdp')), may hold values from -1.75 to 1.75
- first_gain: bfloat16 [2, 768], P(None, ('dp', 'fsdp')), may hold values from 0.099609375 to 1.8984375
- first_shift: bfloat16 [2, 768], P(None, ('dp', 'fsdp')), may hold values from -1.75 to 1.75
- up_weight: bfloat16 [2, 768, 3072], P(None, ('dp', 'fsdp')), may hold values from -0.21875 to 0.21875
- up_bias: bfloat16 [2, 3072], P(None, ('dp', 'fsdp')), may hold values from -1.75 to 1.75
- down_weight: bfloat16 [2, 3072, 768], P(None, ('dp', 'fsdp')), may hold values from -0.109375 to 0.109375
- down_bias: bfloat16 [2, 768], P(None, ('dp', 'fsdp')), may hold values from -1.75 to 1.75
- second_gain: bfloat16 [2, 768], P(None, ('dp', 'fsdp')), may hold values from 0.099609375 to 1.8984375
- second_shift: bfloat16 [2, 768], P(None, ('dp', 'fsdp')), may hold values from -1.75 to 1.75
Outputs:
- output: bfloat16 [16384, 768], P(('dp', 'fsdp'))
- input_grad: bfloat16 [16384, 768], P(('dp', 'fsdp'))
- grad_query_weight: float32 [2, 768, 768], P(None, ('dp', 'fsdp'))
- grad_query_bias: float32 [2, 768], P(None, ('dp', 'fsdp'))
- grad_key_weight: float32 [2, 768, 768], P(None, ('dp', 'fsdp'))
- grad_value_weight: float32 [2, 768, 768], P(None, ('dp', 'fsdp'))
- grad_value_bias: float32 [2, 768], P(None, ('dp', 'fsdp'))
- grad_out_weight: float32 [2, 768, 768], P(None, ('dp', 'fsdp'))
- grad_out_bias: float32 [2, 768], P(None, ('dp', 'fsdp'))
- grad_first_gain: float32 [2, 768], P(None, ('dp', 'fsdp'))
- grad_first_shift: float32 [2, 768], P(None, ('dp', 'fsdp'))
- grad_up_weight: float32 [2, 768, 3072], P(None, ('dp', 'fsdp'))
- grad_up_bias: float32 [2, 3072], P(None, ('dp', 'fsdp'))
- grad_down_weight: float32 [2, 3072, 768], P(None, ('dp', 'fsdp'))
- grad_down_bias: float32 [2, 768], P(None, ('dp', 'fsdp'))
- grad_second_gain: float32 [2, 768], P(None, ('dp', 'fsdp'))
- grad_second_shift: float32 [2, 768], P(None, ('dp', 'fsdp'))
Inputs may be any that keep to these rules, and one draw needn't show every extreme that they name: `lengths`: some chain has exactly 128 live slots and some exactly 96. `tags`: among the 4 chains of one device at most 3 carry either tag, and some device holds exactly 3 of one tag.
All inputs are finite; a program needn't handle non-finite values.
Results may differ from a plain program's by a relative error of at most 0.02.
Values may be sent and summed in bfloat16 or wider, within the bound.
No kernel may reach another device: no remote copies, remote signals or barrier semaphores. Data moves between devices by JAX's collectives and lax.ppermute only.
A program may use at most 192 MiB of HBM per device.

v0:
```python
import functools

import jax
import jax.numpy as jnp
import numpy as np
from jax import lax
from jax.experimental import pallas as pl
from jax.experimental.pallas import tpu as pltpu
from jax.sharding import Mesh
from jax.sharding import PartitionSpec as P

HEADS = 12
HEAD_DIM = 64
CAP = 3
MIN_LEN = 96
LANES = 128
PAIRS = 3
BF16 = jnp.bfloat16
F32 = jnp.float32
NN = (((1,), (0,)), ((), ()))
NT = (((1,), (1,)), ((), ()))
TN = (((0,), (0,)), ((), ()))
SWAP = [(0, 1), (1, 0)]
VMEM_LIMIT = 56 * 2**20
VMEM_MOST = 56 * 2**20
SMALL = 12


def dot(a, b, dims=NN):
    return lax.dot_general(a, b, dims, preferred_element_type=F32)


def tie(*values):
    return lax.optimization_barrier(values)


def params(limit=VMEM_LIMIT):
    return pltpu.CompilerParams(vmem_limit_bytes=limit)


def taking(micros):
    return pl.CostEstimate(flops=int(micros * 1.1e9), bytes_accessed=1, transcendentals=0)


def whole_spec(shape):
    return pl.BlockSpec(shape, lambda *_: (0,) * len(shape), pipeline_mode=pl.Buffered(1))


def fixed(shape):
    return pl.BlockSpec(shape, lambda *_: (0,) * len(shape))


def head_masks(value=1.0):
    lane = lax.broadcasted_iota(jnp.int32, (1, LANES), 1)
    first = jnp.where(lane < HEAD_DIM, value, 0.0).astype(BF16)
    second = jnp.where(lane >= HEAD_DIM, value, 0.0).astype(BF16)
    return first, second


def stacked(two_heads, masks):
    return jnp.concatenate([two_heads * masks[0], two_heads * masks[1]], axis=0)


def side_by_side(rows):
    half = rows.shape[0] // 2
    return jnp.concatenate([rows[:half], rows[half:]], axis=1)


def probs_of(scores, length):
    keys = scores.shape[0] // 2
    scores = scores.reshape(2, keys, scores.shape[1])
    rest = scores[:, MIN_LEN:]
    slot = lax.broadcasted_iota(jnp.int32, rest.shape, 1) + MIN_LEN
    rest = jnp.where(slot < length, rest, -1000000000.0)
    scores = jnp.concatenate([scores[:, :MIN_LEN], rest], axis=1)
    exponent = jnp.exp(scores - jnp.max(scores, axis=1, keepdims=True))
    return exponent * (1.0 / jnp.sum(exponent, axis=1, keepdims=True))


def as_rows(probs):
    return probs.astype(BF16).reshape(-1, probs.shape[-1])


def in_groups(width, pairs):
    starts = list(range(0, width, LANES))
    return [starts[i : i + pairs] for i in range(0, len(starts), pairs)]


def attention_rows(length, qkv_ref, ctx_ref, base, rows, width):
    masks, scaled = head_masks(), head_masks(HEAD_DIM**-0.5)
    at = slice(base, base + rows)

    def part(index, start):
        return qkv_ref[at, index * width + start : index * width + start + LANES]

    for starts in in_groups(width, 1):
        scores = [dot(stacked(part(1, s), scaled), part(0, s), NT) for s in starts]
        probs = [as_rows(probs_of(s, length)) for s in scores]
        for start, low in zip(starts, probs):
            context = dot(low, stacked(part(2, start), masks), TN)
            ctx_ref[at, start : start + LANES] = context.astype(BF16)


def attention_kernel(
    lens_ref,
    rows_ref,
    weight_ref,
    vec_ref,
    qkv_ref,
    unit_ref,
    root_ref,
    low_ref,
    rows_t_ref,
    ctx_t_ref,
    low_t_ref,
    out_weight_ref,
    ctx_ref,
):
    width = ctx_ref.shape[1]
    rows_t_ref[...] = rows_ref[...].T

    @pl.when(pl.program_id(0) == 0)
    def _():
        out_weight_ref[...] = weight_ref[:, 3 * width : 4 * width]

    rows = qkv_ref.shape[0] // 2
    for part in range(3):
        columns = slice(part * width, (part + 1) * width)
        product = dot(rows_ref[...], weight_ref[:, columns])
        if part != 1:
            product = product + vec_ref[part // 2 : part // 2 + 1, :]
        qkv_ref[:, columns] = product.astype(BF16)
    for chain in range(2):
        length = lens_ref[2 * pl.program_id(0) + chain]
        attention_rows(length, qkv_ref, ctx_ref, chain * rows, rows, width)
    branch = dot(ctx_ref[...], weight_ref[:, 3 * width : 4 * width]) + vec_ref[2:3, :]
    unit, root = normed(rows_ref[...].astype(F32) + branch)
    unit_ref[...] = unit.astype(BF16)
    root_ref[...] = root
    low = (unit * vec_ref[3:4, :] + vec_ref[4:5, :]).astype(BF16)
    low_ref[...] = low
    low_t_ref[...] = low.T
    ctx_t_ref[...] = ctx_ref[...].T


def attention(rows_in, lens, whole_a, vectors):
    total, width = rows_in.shape
    rows = 2 * total // lens.shape[0]

    def tokens(lanes):
        return pl.BlockSpec((rows, lanes), lambda i, _: (i, 0))

    return pl.pallas_call(
        attention_kernel,
        out_shape=[
            jax.ShapeDtypeStruct((total, 3 * width), BF16),
            jax.ShapeDtypeStruct((total, width), BF16),
            jax.ShapeDtypeStruct((total, 1), F32),
            jax.ShapeDtypeStruct((total, width), BF16),
        ]
        + [jax.ShapeDtypeStruct((width, total), BF16)] * 3
        + [jax.ShapeDtypeStruct((width, width), BF16)],
        grid_spec=pltpu.PrefetchScalarGridSpec(
            num_scalar_prefetch=1,
            grid=(total // rows,),
            in_specs=[tokens(width), whole_spec(whole_a.shape), whole_spec(vectors.shape)],
            out_specs=[tokens(3 * width), tokens(width), tokens(1), tokens(width)]
            + [pl.BlockSpec((width, rows), lambda i, _: (0, i))] * 3
            + [fixed((width, width))],
            scratch_shapes=[pltpu.VMEM((rows, width), BF16)],
        ),
        compiler_params=params(20 * 2**20),
        cost_estimate=taking(14),
        name="attention_forward",
    )(lens, rows_in, whole_a, vectors)


def attention_back_kernel(lens_ref, qkv_ref, da_ref, out_weight_ref, dqkv_ref, sum_ref):
    width = da_ref.shape[1]
    length = lens_ref[pl.program_id(0)]
    masks, scaled = head_masks(), head_masks(HEAD_DIM**-0.5)
    dctx = dot(da_ref[...], out_weight_ref[...], NT).astype(BF16)

    @pl.when(pl.program_id(0) == 0)
    def _():
        sum_ref[...] = jnp.zeros_like(sum_ref)

    def store(column, value):
        low = value.astype(BF16)
        dqkv_ref[:, column : column + LANES] = low
        sum_ref[:, column : column + LANES] += jnp.sum(low.astype(F32), axis=0, keepdims=True)

    def part(index, start):
        return qkv_ref[:, index * width + start : index * width + start + LANES]

    for starts in in_groups(width, PAIRS):
        queries = [part(0, s) for s in starts]
        keys = [stacked(part(1, s), scaled) for s in starts]
        grads = [dctx[:, s : s + LANES] for s in starts]
        scores = [dot(k, q, NT) for k, q in zip(keys, queries)]
        dprobs = [dot(stacked(part(2, s), masks), d, NT) for s, d in zip(starts, grads)]
        probs = [probs_of(s, length) for s in scores]
        dprobs = [d.reshape(p.shape) for d, p in zip(dprobs, probs)]
        dscores = [
            as_rows(p * (d - jnp.sum(d * p, axis=1, keepdims=True)))
            for p, d in zip(probs, dprobs)
        ]
        for start, p, d in zip(starts, probs, grads):
            store(2 * width + start, dot(side_by_side(as_rows(p)), stacked(d, masks)))
        for start, d, q in zip(starts, dscores, queries):
            store(width + start, dot(side_by_side(d), stacked(q, scaled)))
        for start, d, k in zip(starts, dscores, keys):
            store(start, dot(d, k, TN))


def attention_back(qkv, da, out_weight, lens):
    total, width = da.shape
    rows = total // lens.shape[0]

    def tokens(lanes):
        return pl.BlockSpec((rows, lanes), lambda i, _: (i, 0))

    return pl.pallas_call(
        attention_back_kernel,
        out_shape=[
            jax.ShapeDtypeStruct((total, 3 * width), BF16),
            jax.ShapeDtypeStruct((1, 3 * width), F32),
        ],
        grid_spec=pltpu.PrefetchScalarGridSpec(
            num_scalar_prefetch=1,
            grid=(lens.shape[0],),
            in_specs=[tokens(3 * width), tokens(width), whole_spec((width, width))],
            out_specs=[tokens(3 * width), fixed((1, 3 * width))],
        ),
        compiler_params=params(12 * 2**20),
        cost_estimate=taking(11),
        name="attention_backward",
    )(lens, qkv, da, out_weight)


def up_kernel(low_ref, up_ref, small_ref, active_ref, slope_ref):
    weight = up_ref[...]
    block = weight.shape[1]
    rows = small_ref.shape[0]
    fold = block // rows
    column = lax.broadcasted_iota(jnp.int32, (LANES, block), 0)
    lane = lax.broadcasted_iota(jnp.int32, (LANES, block), 1)
    spread = (column == SMALL - 4 + lane % fold).astype(F32).astype(BF16)
    row = lax.broadcasted_iota(jnp.int32, (rows, block), 0)
    at = lax.broadcasted_iota(jnp.int32, (rows, block), 1)
    bias = jnp.sum(
        jnp.where(at // fold == row, dot(small_ref[...], spread), 0.0), axis=0, keepdims=True
    )
    step = LANES
    for start in range(0, low_ref.shape[0], step):
        hidden = dot(low_ref[start : start + step, :], weight) + bias
        cdf = 0.5 * (1.0 + lax.erf(hidden * (2.0**-0.5)))
        active_ref[start : start + step, :] = (hidden * cdf).astype(BF16)
        density = jnp.exp(-0.5 * hidden * hidden) * ((2.0 * np.pi) ** -0.5)
        slope_ref[start : start + step, :] = (cdf + hidden * density).astype(BF16)


def up_and_gelu(low, up, whole_a):
    rows, width = low.shape
    ff = up.shape[1]
    block = 512
    return pl.pallas_call(
        up_kernel,
        out_shape=[jax.ShapeDtypeStruct((rows, ff), BF16)] * 2,
        grid=(ff // block,),
        in_specs=[
            whole_spec((rows, width)),
            pl.BlockSpec((width, block), lambda i: (0, i)),
            pl.BlockSpec(
                (width * block // ff, LANES), lambda i: (i, whole_a.shape[1] // LANES - 1)
            ),
        ],
        out_specs=[pl.BlockSpec((rows, block), lambda i: (0, i))] * 2,
        cost_estimate=taking(10),
        compiler_params=params(12 * 2**20),
        name="up_gelu",
    )(low, up, whole_a)


def down_kernel(
    active_ref, down_ref, unit_ref, cot_ref, vec_ref, out_ref, df_ref, sum_ref
):
    @pl.when(pl.program_id(0) == 0)
    def _():
        sum_ref[...] = jnp.zeros_like(sum_ref)

    bias, gain, shift = vec_ref[5:6, :], vec_ref[6:7, :], vec_ref[7:8, :]
    hidden = unit_ref[...].astype(F32) * vec_ref[3:4, :] + vec_ref[4:5, :]
    total = hidden + dot(active_ref[...], down_ref[...]) + bias
    unit, root = normed(total)
    out_ref[...] = (unit * gain + shift).astype(BF16)
    grad = cot_ref[...].astype(F32)
    df = norm_back(grad, unit, root, gain).astype(BF16)
    df_ref[...] = df
    sum_ref[0:1, :] += jnp.sum(df.astype(F32), axis=0, keepdims=True)
    sum_ref[1:2, :] += jnp.sum(grad * unit, axis=0, keepdims=True)
    sum_ref[2:3, :] += jnp.sum(grad, axis=0, keepdims=True)


def down_and_norm(active, down, unit, cot, vectors):
    rows, ff = active.shape
    width = down.shape[1]
    block = 256
    tokens = pl.BlockSpec((block, width), lambda i: (i, 0))
    return pl.pallas_call(
        down_kernel,
        out_shape=[
            jax.ShapeDtypeStruct((rows, width), BF16),
            jax.ShapeDtypeStruct((rows, width), BF16),
            jax.ShapeDtypeStruct((8, width), F32),
        ],
        grid=(rows // block,),
        in_specs=[
            pl.BlockSpec((block, ff), lambda i: (i, 0)),
            whole_spec((ff, width)),
            tokens,
            tokens,
            whole_spec(vectors.shape),
        ],
        out_specs=[tokens, tokens, fixed((8, width))],
        compiler_params=params(18 * 2**20),
        cost_estimate=taking(10),
        name="down_norm",
    )(active, down, unit, cot, vectors)


def back_kernel(
    core_ref,
    df_ref,
    down_ref,
    slope_ref,
    up_ref,
    low_t_ref,
    unit_ref,
    root_ref,
    vec_ref,
    send_ref,
    own_ref,
    da_ref,
    bias_ref,
    sum_ref,
    total,
    grad,
):
    at = pl.program_id(0)
    step = 384

    @pl.when(at == 0)
    def _():
        total[...] = df_ref[...].astype(F32)
        sum_ref[...] = jnp.zeros_like(sum_ref)

    bias = jnp.zeros(bias_ref.shape, F32)
    for start in range(0, df_ref.shape[0], step):
        rows = slice(start, start + step)
        du = dot(df_ref[rows, :], down_ref[...], NT) * slope_ref[rows, :].astype(F32)
        du = du.astype(BF16)
        grad[rows, :] = du
        bias += jnp.sum(du.astype(F32), axis=0, keepdims=True)
        total[rows, :] += dot(du, up_ref[...], NT)
    bias_ref[...] = bias
    halves_kernel(core_ref[0], low_t_ref, grad, send_ref, own_ref)

    @pl.when(at == pl.num_programs(0) - 1)
    def _():
        for start in range(0, df_ref.shape[0], step):
            rows = slice(start, start + step)
            dh1, unit = total[rows, :], unit_ref[rows, :].astype(F32)
            da = norm_back(dh1, unit, root_ref[rows, :], vec_ref[3:4, :]).astype(BF16)
            da_ref[rows, :] = da
            sum_ref[0:1, :] += jnp.sum(da.astype(F32), axis=0, keepdims=True)
            sum_ref[1:2, :] += jnp.sum(dh1 * unit, axis=0, keepdims=True)
            sum_ref[2:3, :] += jnp.sum(dh1, axis=0, keepdims=True)


def halves_kernel(core, left_ref, right_ref, send_ref, own_ref):
    parts, _, run, tokens = left_ref.shape
    for half, out_ref in ((1 - core, send_ref), (core, own_ref)):
        left = left_ref[:, half].reshape(parts * run, tokens)
        out_ref[...] = dot(left, right_ref[...]).astype(BF16).reshape(out_ref.shape)


def feed_back(df, down, slope, up, low_t, unit, root, vectors, core1, parts):
    rows, width = df.shape
    ff = up.shape[1]
    block = 768
    run = width // (2 * parts)
    tokens = whole_spec((rows, width))
    half = pl.BlockSpec((parts, run, block), lambda i, _: (0, 0, i))
    return pl.pallas_call(
        back_kernel,
        out_shape=[
            jax.ShapeDtypeStruct((parts, run, ff), BF16),
            jax.ShapeDtypeStruct((parts, run, ff), BF16),
            jax.ShapeDtypeStruct((rows, width), BF16),
            jax.ShapeDtypeStruct((1, ff), F32),
            jax.ShapeDtypeStruct((8, width), F32),
        ],
        grid_spec=pltpu.PrefetchScalarGridSpec(
            num_scalar_prefetch=1,
            grid=(ff // block,),
            in_specs=[
                tokens,
                pl.BlockSpec((block, width), lambda i, _: (i, 0)),
                pl.BlockSpec((rows, block), lambda i, _: (0, i)),
                pl.BlockSpec((width, block), lambda i, _: (0, i)),
                whole_spec((parts, 2, run, rows)),
                tokens,
                whole_spec(root.shape),
                whole_spec(vectors.shape),
            ],
            out_specs=[
                half,
                half,
                fixed((rows, width)),
                pl.BlockSpec((1, block), lambda i, _: (0, i)),
                fixed((8, width)),
            ],
            scratch_shapes=[pltpu.VMEM((rows, width), F32), pltpu.VMEM((rows, block), BF16)],
        ),
        compiler_params=params(30 * 2**20),
        cost_estimate=taking(21),
        name="feed_forward_back",
    )(core1, df, down, slope, up, low_t.reshape(parts, 2, run, rows), unit, root, vectors)


def normed(values):
    centre = values - jnp.mean(values, axis=-1, keepdims=True)
    root = lax.rsqrt(jnp.mean(centre * centre, axis=-1, keepdims=True) + 1e-05)
    return centre * root, root


def norm_back(grad, unit, root, gain):
    scaled = grad * gain
    inner = jnp.mean(scaled * unit, axis=-1, keepdims=True)
    return root * (scaled - jnp.mean(scaled, axis=-1, keepdims=True) - unit * inner)


def transposed_rows(vectors):
    count, size = vectors.shape
    padded = jnp.concatenate([vectors, jnp.zeros((LANES - count, size), vectors.dtype)], axis=0)
    row = lax.broadcasted_iota(jnp.int32, (size, size), 0)
    column = lax.broadcasted_iota(jnp.int32, (size, size), 1)
    unit = (row == column).astype(F32).astype(BF16)
    return dot(unit, padded.astype(BF16), NT)


def folded(values, rows):
    size = values.shape[1]
    fold = size // rows
    row = lax.broadcasted_iota(jnp.int32, (rows, size), 0)
    at = lax.broadcasted_iota(jnp.int32, (rows, size), 1)
    spread = jnp.where(at // fold == row, values.astype(F32), 0.0).astype(BF16)
    column = lax.broadcasted_iota(jnp.int32, (LANES, size), 0)
    lane = lax.broadcasted_iota(jnp.int32, (LANES, size), 1)
    place = (column == SMALL - 4 + lane % fold).astype(F32).astype(BF16)
    return dot(spread, place, NT)


def pack_kernel(*refs):
    matrices, vectors, up_bias_ref, out_ref = refs[:4], refs[4:12], refs[12], refs[13]
    rows = out_ref.shape[1]
    for model in range(2):
        start = 0
        for matrix in matrices:
            out_ref[model, :, start : start + matrix.shape[2]] = matrix[model]
            start += matrix.shape[2]
        eight = jnp.concatenate([v[model : model + 1, :].astype(F32) for v in vectors], axis=0)
        small = transposed_rows(eight) + folded(up_bias_ref[model : model + 1, :].astype(F32), rows)
        out_ref[model, :, start:] = small.astype(BF16)


def pack(matrices, vectors, up_bias):
    models, rows, _ = matrices[0].shape
    lanes = sum(m.shape[2] for m in matrices) + LANES
    if rows % 8:
        parts = [v[..., None] for v in vectors] + [up_bias.reshape(models, rows, -1)]
        small = jnp.concatenate(parts, axis=-1)
        small = jnp.pad(small, [(0, 0), (0, 0), (0, LANES - small.shape[-1])])
        return jnp.concatenate(list(matrices) + [small], axis=-1)
    return pl.pallas_call(
        pack_kernel,
        out_shape=jax.ShapeDtypeStruct((models, rows, lanes), BF16),
        compiler_params=params(VMEM_MOST),
        name="pack_shard",
    )(*matrices, *vectors, up_bias)


def small_grads_kernel(down_ref, back_ref, bias_ref, qkv_ref, out_ref):
    rows = out_ref.shape[0]
    width = down_ref.shape[1]
    eight = jnp.concatenate(
        [
            qkv_ref[:, :width],
            qkv_ref[:, 2 * width :],
            back_ref[0:3, :],
            down_ref[0:3, :],
        ],
        axis=0,
    )
    out_ref[...] = transposed_rows(eight).astype(BF16)
    step = LANES
    fold = bias_ref.shape[1] // rows
    for start in range(0, rows, step):
        values = bias_ref[:, start * fold : (start + step) * fold]
        here = slice(start, start + step)
        out_ref[here, :] = (out_ref[here, :].astype(F32) + folded(values, step)).astype(BF16)


def small_grads(down_sums, back_sums, bias_sums, qkv_sums):
    width = down_sums.shape[1]
    return pl.pallas_call(
        small_grads_kernel,
        out_shape=jax.ShapeDtypeStruct((width, LANES), BF16),
        compiler_params=params(8 * 2**20),
        name="small_gradients",
    )(down_sums, back_sums, bias_sums, qkv_sums)


class Ring:
    def __init__(self, count):
        depth = 4 if count % 4 == 0 else 2
        wide = count // depth
        order = []
        if wide > 1:
            for z in range(depth):
                ys = range(1, wide) if z % 2 == 0 else reversed(range(1, wide))
                order += [z * wide + y for y in ys]
            order += [z * wide for z in reversed(range(depth))]
        else:
            order = list(range(count))
        self.count, self.depth, self.wide = count, depth, wide
        self.long = count // 2
        self.short = count - 1 - self.long
        self.ahead, self.behind = [], []
        for core in range(2):
            sign = 1 if core == 0 else -1
            here = core * count
            for place, chip in enumerate(order):
                self.ahead.append((here + chip, here + order[(place + sign) % count]))
                self.behind.append((here + chip, here + order[(place - sign) % count]))

    def origins(self, core, chip):
        depth, turn = self.depth, self.wide - 1
        if turn == 0:
            place = chip
        else:
            z, y = lax.div(chip, self.wide), lax.rem(chip, self.wide)
            along = jnp.where(lax.rem(z, 2) == 0, y - 1, turn - y)
            place = jnp.where(y == 0, depth * turn + depth - 1 - z, z * turn + along)
        sign = 1 - 2 * core
        chips = []
        for k in range(self.count):
            off = -k if k <= self.long else k - self.long
            at = lax.rem(place + sign * off + self.count, self.count)
            if turn > 0:
                z, j = lax.div(at, turn), lax.rem(at, turn)
                y = jnp.where(lax.rem(z, 2) == 0, 1 + j, turn - j)
                at = jnp.where(
                    at < depth * turn, z * self.wide + y, (depth * (turn + 1) - 1 - at) * self.wide
                )
            chips.append(at)
        return chips

    def forth(self, block):
        return lax.ppermute(block, ("core", "f"), self.ahead)

    def back(self, block):
        return lax.ppermute(block, ("core", "f"), self.behind)


def swap(value, axis):
    return lax.ppermute(value, axis, SWAP)


def pick(value, index, axis):
    return lax.dynamic_index_in_dim(value, index, axis, keepdims=False)


def two_sides(own, other, side, groups):
    place = lax.broadcasted_iota(jnp.int32, (2, 1, 1), 0)
    block = jnp.where(place == side, own[None], other[None])
    if groups > 1:
        return lax.all_gather(block, "r", axis=0, tiled=False)
    return block[None]


class Gather:
    def __init__(self, ring, block):
        self.ring, self.step = ring, 0
        self.forth, self.back = [block], [block]
        self.theirs_forth, self.theirs_back = [swap(block, "core")], []

    def launch(self):
        self.step += 1
        sent = [self.ring.forth(self.forth[-1])]
        if self.step <= self.ring.short:
            sent.append(self.ring.back(self.back[-1]))
        return sent

    def now(self):
        return self.forth[-1]

    def land(self, sent):
        self.forth.append(sent[0])
        self.theirs_forth.append(swap(sent[0], "core"))
        if len(sent) > 1:
            self.back.append(sent[1])
            self.theirs_back.append(swap(sent[1], "core"))

    def settle(self, values):
        for kept, value in zip((self.theirs_forth, self.theirs_back), values):
            kept[:] = value

    def blocks(self):
        return self.forth + self.back[1:], self.theirs_forth + self.theirs_back


class Scatter:
    def __init__(self, ring, own, other, origins):
        self.ring, self.step = ring, 0
        self.own, self.other, self.origins = own, other, origins
        self.far = self.term(ring.long).astype(BF16)
        self.near = self.term(ring.long + ring.short).astype(BF16)
        self.total = None

    def term(self, k):
        a, b = pick(self.own, self.origins[k], 2), pick(self.other, self.origins[k], 2)
        return a.astype(F32) + b.astype(F32)

    def launch(self):
        self.step += 1
        sent = [self.ring.back(self.far)]
        if self.step > self.ring.long - self.ring.short:
            sent.append(self.ring.forth(self.near))
        return sent

    def now(self):
        return self.far

    def land(self, sent):
        left = self.ring.long - self.step
        if left:
            self.far = (sent[0].astype(F32) + self.term(left)).astype(BF16)
            if len(sent) > 1:
                near = sent[1].astype(F32) + self.term(self.ring.long + left)
                self.near = near.astype(BF16)
        else:
            self.total = sent[0].astype(F32) + sent[1].astype(F32) + self.term(0)


class Trip:
    def __init__(self, value, axis):
        self.value, self.axis, self.got = value, axis, None

    def launch(self):
        return [swap(self.value, self.axis)]

    def now(self):
        return self.value

    def land(self, sent):
        self.got = sent[0]


def slot(movers, work=None):
    now = [m.now() for m in movers]
    sent = [m.launch() for m in movers]
    gathers = [m for m in movers if isinstance(m, Gather)]
    before = [(m.theirs_forth, m.theirs_back) for m in gathers]
    done = None if work is None else work((now, before))
    sent, done, before = tie(sent, done, before)
    for mover, settled in zip(gathers, before):
        mover.settle(settled)
    for mover, arrived in zip(movers, sent):
        mover.land(arrived)
    return done


def assemble_kernel(ring, with_vectors, at_ref, *refs):
    count = ring.count
    blocks, out_ref = refs[: 2 * count], refs[2 * count]
    held, sems_in, sems_out = refs[-3:]
    core, chip = at_ref[0], at_ref[1]
    here, there = ring.origins(core, chip), ring.origins(1 - core, chip)
    incoming, outgoing = [], []
    for i, (block, at) in enumerate(zip(blocks, here + there)):
        half = core if i < count else 1 - core
        for r in range(block.shape[0]):
            inside, outside = held.at[r, :, half, at], out_ref.at[r, :, half, at]
            n = len(incoming)
            incoming.append(pltpu.make_async_copy(block.at[r], inside, sems_in.at[n]))
            outgoing.append(pltpu.make_async_copy(inside, outside, sems_out.at[n]))
    for copy in incoming:
        copy.start()
    for copy, after in zip(incoming, outgoing):
        copy.wait()
        after.start()
    if with_vectors:
        rows = held[:, :, :, :, :, held.shape[-1] - LANES :]
        small = rows.astype(F32).reshape(-1, LANES)
        refs[2 * count + 1][...] = small.T[:16]
    for copy in outgoing:
        copy.wait()


def assemble(ring, mine, theirs, core, with_vectors=False):
    groups, _, rows, lanes = mine[0].shape
    count = ring.count
    chip = lax.axis_index("f")
    shape = (groups, 2, 2, count, rows, lanes)
    width = shape[1] * shape[2] * groups * count * rows
    if rows % 8:
        whole = jnp.zeros(shape, BF16)
        at = ring.origins(core, chip) + ring.origins(1 - core, chip)
        for i, block in enumerate(mine + theirs):
            half = core if i < count else 1 - core
            where = (0, 0, half, at[i], 0, 0)
            whole = lax.dynamic_update_slice(whole, block[:, :, None, None], where)
        whole = whole.reshape(-1, lanes)
        return whole, (whole[:, lanes - LANES :].astype(F32).T[:16] if with_vectors else None)
    out_shape = [jax.ShapeDtypeStruct(shape, BF16)]
    if with_vectors:
        out_shape.append(jax.ShapeDtypeStruct((16, width), F32))
    out = pl.pallas_call(
        functools.partial(assemble_kernel, ring, with_vectors),
        out_shape=out_shape,
        in_specs=[pl.BlockSpec(memory_space=pltpu.SMEM)]
        + [pl.BlockSpec(memory_space=pl.ANY)] * (2 * count),
        out_specs=[pl.BlockSpec(memory_space=pl.ANY)]
        + [pl.BlockSpec(memory_space=pltpu.VMEM)] * with_vectors,
        scratch_shapes=[
            pltpu.VMEM(shape, BF16),
            pltpu.SemaphoreType.DMA((2 * count * groups,)),
            pltpu.SemaphoreType.DMA((2 * count * groups,)),
        ],
        cost_estimate=taking(4),
        compiler_params=params((36 if with_vectors else 8) * 2**20),
        name="assemble",
    )(jnp.stack([core, chip]).astype(jnp.int32), *mine, *theirs)
    return out[0].reshape(-1, lanes), out[1] if with_vectors else None


class Owners:
    def __init__(self, total, side, groups):
        if groups > 1:
            total = lax.psum_scatter(total.astype(BF16), "r", scatter_dimension=0, tiled=True)
        self.side, self.own = side, pick(total[0], side, 0).astype(F32)
        self.trip = Trip(pick(total[0], 1 - side, 0).astype(BF16), "t")

    def by_model(self):
        place = lax.broadcasted_iota(jnp.int32, (2, 1, 1), 0)
        return jnp.where(place == self.side, self.own[None], self.trip.got.astype(F32)[None])


def mixed_kernel(core_ref, left_ref, ctx_ref, dqkv_ref, da_ref, small_ref, send_ref, own_ref):
    at, core = pl.program_id(0), core_ref[0]

    @pl.when(at < 3)
    def _():
        halves_kernel(core, left_ref, dqkv_ref, send_ref, own_ref)

    @pl.when(at == 3)
    def _():
        halves_kernel(core, ctx_ref, da_ref, send_ref, own_ref)

    @pl.when(at == 4)
    def _():
        send_ref[:, :, :LANES] = small_ref[:, 1 - core]
        own_ref[:, :, :LANES] = small_ref[:, core]


def mixed_grad(rows_t, ctx_t, dqkv, da, small, core1, parts):
    size, tokens = rows_t.shape
    run = size // (2 * parts)
    width = da.shape[1]
    small = small.reshape(parts, 2, run, LANES)
    lanes = 4 * width + LANES
    if run % 16:
        full = [dot(rows_t, dqkv), dot(ctx_t, da)]
        full = [f.astype(BF16).reshape(parts, 2, run, -1) for f in full] + [small]
        full = jnp.concatenate(full, axis=-1)
        return pick(full, 1 - core1[0], 1), pick(full, core1[0], 1)
    left = whole_spec((parts, 2, run, tokens))
    half = pl.BlockSpec((parts, run, width), lambda j, _: (0, 0, j))
    return pl.pallas_call(
        mixed_kernel,
        out_shape=[jax.ShapeDtypeStruct((parts, run, lanes), BF16)] * 2,
        grid_spec=pltpu.PrefetchScalarGridSpec(
            num_scalar_prefetch=1,
            grid=(5,),
            in_specs=[
                left,
                left,
                pl.BlockSpec((tokens, width), lambda j, _: (0, jnp.minimum(j, 2))),
                whole_spec(da.shape),
                whole_spec(small.shape),
            ],
            out_specs=[half, half],
        ),
        compiler_params=params(16 * 2**20),
        cost_estimate=taking(8),
        name="attention_gradients",
    )(
        core1,
        rows_t.reshape(parts, 2, run, tokens),
        ctx_t.reshape(parts, 2, run, tokens),
        dqkv,
        da,
        small,
    )


def wide_kernel(core_ref, left_ref, right_ref, send_ref, own_ref):
    out = dot(left_ref[...], right_ref[...], TN).astype(BF16)

    @pl.when(pl.program_id(0) == 0)
    def _():
        send_ref[...] = out.reshape(send_ref.shape)

    @pl.when(pl.program_id(0) == 1)
    def _():
        own_ref[...] = out.reshape(own_ref.shape)


def wide_grad(left, right, core1, parts):
    tokens, size = left.shape
    run = size // (2 * parts)
    n = right.shape[1]
    if run % LANES:
        full = dot(left, right, TN).astype(BF16).reshape(parts, 2, run, n)
        return pick(full, 1 - core1[0], 1), pick(full, core1[0], 1)

    def columns(h, i, core_ref):
        return (0, 2 * i + jnp.where(h == 0, 1 - core_ref[0], core_ref[0]))

    return pl.pallas_call(
        wide_kernel,
        out_shape=[jax.ShapeDtypeStruct((parts, run, n), BF16)] * 2,
        grid_spec=pltpu.PrefetchScalarGridSpec(
            num_scalar_prefetch=1,
            grid=(2, parts),
            in_specs=[pl.BlockSpec((tokens, run), columns), whole_spec((tokens, n))],
            out_specs=[
                pl.BlockSpec((1, run, n), lambda h, i, _: (jnp.where(h == 0, i, parts - 1), 0, 0)),
                pl.BlockSpec((1, run, n), lambda h, i, _: (jnp.where(h == 0, 0, i), 0, 0)),
            ],
        ),
        compiler_params=params(14 * 2**20),
        cost_estimate=taking(5),
        name="down_gradient",
    )(core1, left, right)


def places(tags, model):
    member = tags[:, 0] == model
    count = member.shape[0]
    before = lax.broadcasted_iota(jnp.int32, (count, count), 0) < lax.broadcasted_iota(
        jnp.int32, (count, count), 1
    )
    ranking = jnp.sum(jnp.where(before & member[:, None], 1, 0), axis=0)
    slots = lax.broadcasted_iota(jnp.int32, (CAP, count), 0)
    return (slots == ranking[None, :]) & member[None, :]


def route(chosen, chains):
    marked = jnp.where(chosen[:, :, None, None], chains[None], jnp.zeros((), chains.dtype))
    return jnp.sum(marked.astype(F32), axis=1).astype(chains.dtype)


def body(ring, groups, *args):
    (
        inputs,
        cotangent,
        lengths,
        tags,
        query_weight,
        query_bias,
        key_weight,
        value_weight,
        value_bias,
        output_projection_weight,
        out_bias,
        first_gain,
        first_shift,
        up_weight,
        up_bias,
        down_weight,
        down_bias,
        second_gain,
        second_shift,
    ) = args
    side, core = lax.axis_index("t"), lax.axis_index("core")
    core1 = core.astype(jnp.int32)[None]
    chains = lengths.shape[0]
    width = inputs.shape[1]
    ff = up_weight.shape[2]
    slots = inputs.shape[0] // chains
    tokens = 2 * CAP * slots
    parts = 2 * groups

    shard_a = pack(
        (query_weight, key_weight, value_weight, output_projection_weight),
        (
            query_bias,
            value_bias,
            out_bias,
            first_gain,
            first_shift,
            down_bias,
            second_gain,
            second_shift,
        ),
        up_bias,
    )
    block_a = two_sides(
        pick(shard_a, side, 0), swap(pick(shard_a, 1 - side, 0), "t"), side, groups
    )

    own_places, other_places = places(tags, side), places(tags, 1 - side)
    own_len = jnp.sum(jnp.where(own_places, lengths[None, :], 0), axis=1)
    other_len = jnp.sum(jnp.where(other_places, lengths[None, :], 0), axis=1)
    chain_rows = inputs.reshape(chains, slots, width)
    sent_lens = jnp.broadcast_to(other_len[:, None, None], (CAP, 16, width)).astype(BF16)
    sent = jnp.concatenate([route(other_places, chain_rows), sent_lens], axis=1)

    def other_side(weight):
        return Trip(pick(weight, 1 - side, 0), "t")

    def joined(weight, trip):
        return two_sides(pick(weight, side, 0), trip.got, side, groups)

    ring_a, trip = Gather(ring, block_a), other_side(up_weight)
    message = slot([ring_a, trip], lambda now: tie(now, sent)[1])
    ring_u = Gather(ring, joined(up_weight, trip))
    down_weight = slot([ring_a], lambda now: tie(now, down_weight)[1])
    trip_rows, trip = Trip(message, "t"), other_side(down_weight)
    slot([ring_a, ring_u, trip_rows])

    def make_rows(now):
        _, got, cots = tie(now, trip_rows.got, cotangent.reshape(chains, slots, width))
        rows = jnp.concatenate([route(own_places, chain_rows), got[:, :slots]], axis=0)
        lens = jnp.concatenate([own_len, got[:, slots, 0].astype(jnp.int32)])
        return rows.reshape(tokens, width), lens, route(other_places, cots), cots

    rows_in, lens, other_cot, cot_rows = slot([ring_a, ring_u, trip], make_rows)
    ring_d, trip_cot = Gather(ring, joined(down_weight, trip)), Trip(other_cot, "t")
    for _ in range(ring.long - 4):
        slot([ring_a, ring_u, ring_d])

    def join_attention(now):
        _, blocks = tie(now, ring_a.blocks())
        return assemble(ring, *blocks, core, True)

    whole_a, vectors = slot([ring_u, ring_d, trip_cot], join_attention)

    def do_attention(now):
        _, whole = tie(now, whole_a)
        return attention(rows_in, lens, whole, vectors)

    qkv, unit1, root1, low1, rows_t, ctx_t, low_t, out_weight = slot([ring_u, ring_d], do_attention)

    def join_up(now):
        _, blocks, own, other = tie(now, ring_u.blocks(), cot_rows, trip_cot.got)
        cot = jnp.concatenate([route(own_places, own), other], axis=0)
        return assemble(ring, *blocks, core)[0], cot.reshape(tokens, width)

    whole_u, cot = slot([ring_d], join_up)

    def do_up(now):
        _, whole = tie(now, whole_u)
        return up_and_gelu(low1, whole, whole_a)

    active, slope = slot([ring_d], do_up)
    whole_d, _ = assemble(ring, *ring_d.blocks(), core)
    gain1 = vectors[3:4]

    result, df, down_sums = down_and_norm(active, whole_d, unit1, cot, vectors)

    origins = ring.origins(core, lax.axis_index("f"))

    def blocks_of(half):
        return half.reshape(groups, 2, ring.count, -1, half.shape[-1])

    def scatter(own, arrived):
        return Scatter(ring, blocks_of(own), blocks_of(arrived), origins)

    send_d, own_d = wide_grad(active, df, core1, parts)
    trip = Trip(send_d, "core")

    def do_feed_back(now):
        _, df_now = tie(now, df)
        return feed_back(
            df_now, whole_d, slope, whole_u, low_t, unit1, root1, vectors, core1, parts
        )

    send_u, own_u, da, bias_sums, back_sums = slot([trip], do_feed_back)
    ring_d = scatter(own_d, trip.got)

    def do_attention_back(now):
        _, da_now = tie(now, da)
        return attention_back(qkv, da_now, out_weight, lens)

    def second_half(values):
        return values.reshape(2, CAP, slots, width)[1]

    trip, trip_result = Trip(send_u, "core"), Trip(second_half(tie(result, da)[0]), "t")
    dqkv, qkv_sums = slot([ring_d, trip, trip_result], do_attention_back)
    ring_u = scatter(own_u, trip.got)

    def attention_grads(now):
        _, dqkv_now = tie(now, dqkv)
        small = small_grads(down_sums, back_sums, bias_sums, qkv_sums)
        return mixed_grad(rows_t, ctx_t, dqkv_now, da, small, core1, parts)

    send_a, own_a = slot([ring_d, ring_u], attention_grads)
    def do_rows(now):
        _, dq = tie(now, dqkv)
        rows = (da.astype(F32) + dot(dq, whole_a[:, : 3 * width], NT)).astype(BF16)
        return rows, second_half(rows)

    trip = Trip(send_a, "core")
    rows_grad, rows = slot([ring_d, ring_u, trip], do_rows)
    trip_rows = Trip(rows, "t")
    to_home = jnp.concatenate([own_places, other_places], axis=0).T

    def home(values, back):
        both = jnp.concatenate([values.reshape(2, CAP, slots, width)[0], back], axis=0)
        return route(to_home, both).reshape(-1, width)

    def outputs(now):
        _, values, back = tie(now, result, trip_result.got)
        return home(values, back)

    output = slot([ring_d, ring_u, trip_rows], outputs)
    for _ in range(ring.long - 4):
        slot([ring_d, ring_u])
    ring_a = scatter(own_a, trip.got)
    owners_d = Owners(ring_d.total, side, groups)

    def input_grads(now):
        _, values, back = tie(now, rows_grad, trip_rows.got)
        return home(values, back)

    input_grad = slot([ring_u, ring_a, owners_d.trip], input_grads)
    owners_u = Owners(ring_u.total, side, groups)
    grads_d = slot([ring_a, owners_u.trip], lambda now: owners_d.by_model())
    grads_u = slot([ring_a], lambda now: owners_u.by_model())
    for _ in range(ring.long - 3):
        slot([ring_a])

    owners_a = Owners(ring_a.total, side, groups)
    slot([owners_a.trip])
    grads_a = owners_a.by_model()
    columns = jnp.swapaxes(grads_a[:, :, 4 * width : 4 * width + 16], 1, 2)
    return (
        output,
        input_grad,
        grads_a[:, :, :width],
        columns[:, 0],
        grads_a[:, :, width : 2 * width],
        grads_a[:, :, 2 * width : 3 * width],
        columns[:, 1],
        grads_a[:, :, 3 * width : 4 * width],
        columns[:, 2],
        columns[:, 3],
        columns[:, 4],
        grads_u,
        jnp.swapaxes(columns[:, 8:12], 1, 2).reshape(2, -1),
        grads_d,
        columns[:, 5],
        columns[:, 6],
        columns[:, 7],
    )


def solution(mesh):
    dp, fsdp = mesh.shape["dp"], mesh.shape["fsdp"]
    groups = dp // 4
    inner = Mesh(mesh.devices.reshape(groups, 2, 2, fsdp), ("r", "t", "core", "f"))
    every = ("r", "t", "core", "f")
    rows, vector, matrix = P(every, None), P(None, every), P(None, every, None)
    weights = (
        matrix,
        vector,
        matrix,
        matrix,
        vector,
        matrix,
        vector,
        vector,
        vector,
        matrix,
        vector,
        matrix,
        vector,
        vector,
        vector,
    )
    return jax.shard_map(
        functools.partial(body, Ring(fsdp), groups),
        mesh=inner,
        in_specs=(rows, rows, P(every), rows) + weights,
        out_specs=(rows, rows) + weights,
        check_vma=False,
    )
```

profile of v0, /device:TPU:0, one launch (start us, length us, event | category | flops | bytes accessed | tf_op | source)
XLA Modules:
  0.0 283.7 jit_solution(8853949083308490450)
XLA Ops:
  0.7 2.0 pack_shard.1
  3.7 3.0 %collective-permute-start = (bf16[24,3200]{1,0:T(8,128)(2,1)S(1)}, bf16[24,3200]{1,0:T(8,128)(2,1)S(1)}, u32[]{:S(2)}, u32[]{:S(2)}) collective-permute-start(bf16[24,3200]{1,0:T(8,128)(2,1)S(1)} %get-tuple-element.476), channel_id=1, source_target_pairs={{0,16},{16,0},{1,17},{17,1},{2,18},{18,2},{3,19},{19,3},{4,20},{20... | collective-permute-start | bytes 460808 | tf_op jit(solution)/shard_map/ppermute | solution.py:578
  9.4 2.0 collective-permute-done
  11.6 2.1 collective-permute-start.1
  15.2 5.7 %collective-permute-done.1.refs_1_ = bf16[1,2,24,3200]{3,2,1,0:T(8,128)(2,1)S(1)} collective-permute-done((bf16[1,2,24,3200]{3,2,1,0:T(8,128)(2,1)S(1)}, bf16[1,2,24,3200]{3,2,1,0:T(8,128)(2,1)S(1)}, u32[]{:S(2)}, u32[]{:S(2)}) %collective-permute-start.1) | collective-permute-done | bytes 307232 | tf_op jit(solution)/shard_map/ppermute | solution.py:571
  21.7 1.7 collective-permute-start.5
  23.6 1.6 collective-permute-start.6
  25.2 1.7 collective-permute-start.13
  28.3 1.6 collective-permute-start.12
  30.6 2.5 collective-permute-done.6.refs_6_
  33.2 2.3 collective-permute-start.10
  35.4 1.5 collective-permute-done.11.refs_1_
  39.0 1.7 collective-permute-start.9
  42.9 3.7 %collective-permute-done.9.refs_3_ = bf16[1,2,24,3200]{3,2,1,0:T(8,128)(2,1)S(1)} collective-permute-done((bf16[1,2,24,3200]{3,2,1,0:T(8,128)(2,1)S(1)}, bf16[1,2,24,3200]{3,2,1,0:T(8,128)(2,1)S(1)}, u32[]{:S(2)}, u32[]{:S(2)}) %collective-permute-start.9) | collective-permute-done | bytes 307232 | tf_op jit(solution)/shard_map/ppermute | solution.py:571
  48.4 1.7 collective-permute-start.20
  53.5 1.5 collective-permute-start.18
  60.0 2.6 collective-permute-done.18.refs_2_
  65.8 1.7 collective-permute-start.27
  79.2 2.8 assemble.3
  83.2 1.4 collective-permute-start.34
  84.6 2.0 collective-permute-start.35
  86.6 10.4 %attention_forward.1 = (bf16[768,2304]{1,0:T(8,128)(2,1)S(1)}, bf16[768,768]{1,0:T(8,128)(2,1)S(1)}, f32[768,1]{1,0:T(8,128)S(1)}, bf16[768,768]{1,0:T(8,128)(2,...) custom-call(s32[6]{0:T(128)S(1)} %pad_add_fusion.lens_ref, ...), custom_call_target="tpu_custom_call" | custom-call | flops 15399999488 | bytes 1 | tf_op jit(solution)/shard_map/attention_forward/pallas_call | solution.py:153
  97.1 1.9 copy-done.48
  100.7 2.0 collective-permute-start.41
  104.7 2.6 assemble.4
  107.3 2.9 %collective-permute-done.41.refs_3_ = bf16[1,2,96,768]{3,2,1,0:T(8,128)(2,1)S(1)} collective-permute-done((bf16[1,2,96,768]{3,2,1,0:T(8,128)(2,1)S(1)}, bf16[1,2,96,768]{3,2,1,0:T(8,128)(2,1)S(1)}, u32[]{:S(2)}, u32[]{:S(2)}) %collective-permute-start.41) | collective-permute-done | bytes 294944 | tf_op jit(solution)/shard_map/ppermute | solution.py:571
  110.8 2.0 collective-permute-start.46
  112.8 7.5 %up_gelu.1 = (bf16[768,3072]{1,0:T(8,128)(2,1)S(1)}, bf16[768,3072]{1,0:T(8,128)(2,1)S(1)}) custom-call(bf16[768,768]{1,0:T(8,128)(2,1)S(1)} %get-tuple-element.344.low_ref, bf16[768,3072]{1,0:T(8,128)(2,1)S(1)} %bitcast.243, bf16[768,3200]{1,0:T(8,128)(2,1)S(1)} %bitcast.241), custom_call_target="tpu_custom_call" | custom-call | flops 11000000512 | bytes 1 | tf_op jit(solution)/shard_map/up_gelu/pallas_call | solution.py:267
  120.4 1.6 collective-permute-done.49.refs_12_
  121.9 2.6 assemble.5
  124.5 6.3 %down_norm.1 = (bf16[768,768]{1,0:T(8,128)(2,1)S(1)}, bf16[768,768]{1,0:T(8,128)(2,1)S(1)}, f32[8,768]{1,0:T(8,128)S(1)}) custom-call(bf16[768,3072]{1,0:T(8,128)(2,1)S(1)} %get-tuple-element.355.active_ref.left_ref, bf16[3072,768]{1,0:T(8,128)(2,1)S(1)} %bitcast.245, bf16[768,768]{1,0:T(8,128)(2,1)S(1)} %get-tuple-element.364.unit_ref, ...), custom_call_target="tpu_custom_call" | custom-call | flops 11000000512 | bytes 1 | tf_op jit(solution)/shard_map/down_norm/pallas_call | solution.py:310
  130.9 5.4 %down_gradient.1 = (bf16[2,768,768]{2,1,0:T(8,128)(2,1)S(1)}, bf16[2,768,768]{2,1,0:T(8,128)(2,1)S(1)}) custom-call(s32[1]{0:T(128)} %bitcast.core_ref, bf16[768,3072]{1,0:T(8,128)(2,1)S(1)} %get-tuple-element.355.active_ref.left_ref, bf16[768,768]{1,0:T(8,128)(2,1)S(1)} %get-tuple-element.369.right_ref.df_ref), custom_call_target="tpu_custom_call" | custom-call | flops 5500000256 | bytes 1 | tf_op jit(solution)/shard_map/down_gradient/pallas_call | solution.py:842
  136.3 1.4 copy-done.2
  137.8 15.9 %feed_forward_back.1 = (bf16[2,192,3072]{2,1,0:T(8,128)(2,1)}, bf16[2,192,3072]{2,1,0:T(8,128)(2,1)S(1)}, bf16[768,768]{1,0:T(8,128)(2,1)S(1)}, f32[1,3072]{1,0:T(1,128)S(1)}, f32[8,768]{1,0:T(8,128)S(1)}) custom-call(s32[1]{0:T(128)} %bitcast.core_ref, bf16[768,768]{1,0:T(8,128)(2,1)S(1)} %get-tuple-element.369.right_ref.df_ref, ...), custom_call_target="tpu_custom_call" | custom-call | flops 23100000256 | bytes 1 | tf_op jit(solution)/shard_map/feed_forward_back/pallas_call | solution.py:395
  155.4 1.5 copy-done.54
  158.4 1.4 fusion.20
  160.3 10.8 %collective-permute-start.55 = (bf16[1,2,96,768]{3,2,1,0:T(8,128)(2,1)S(1)}, bf16[1,2,96,768]{3,2,1,0:T(8,128)(2,1)S(1)}, u32[]{:S(2)}, u32[]{:S(2)}) collective-permute-start(bf16[1,2,96,768]{3,2,1,0:T(8,128)(2,1)S(1)} %get-tuple-element.469), channel_id=1, source_target_pairs={{1,3},{3,5},{5,7},{7,6},{6,4},{4,2},{2,0},{0,1},{9,8},{11,9},{13,1... | collective-permute-start | bytes 884744 | tf_op jit(solution)/shard_map/ppermute | solution.py:571
  171.1 2.0 copy-done.49
  173.1 10.3 %attention_backward.1 = (bf16[768,2304]{1,0:T(8,128)(2,1)S(1)}, f32[1,2304]{1,0:T(1,128)S(1)}) custom-call(s32[6]{0:T(128)S(1)} %pad_add_fusion.lens_ref, bf16[768,2304]{1,0:T(8,128)(2,1)S(1)} %copy-done.49, bf16[768,768]{1,0:T(8,128)(2,1)S(1)} %copy-done.47, bf16[768,768]{1,0:T(8,128)(2,1)S(1)} %copy-done.51), custom_call_target="tpu_custom_call" | custom-call | flops 12099999744 | bytes 1 | tf_op jit(solution)/shard_map/attention_backward/pallas_call | solution.py:223
  183.5 2.8 fusion.22
  187.9 1.8 collective-permute-start.54
  190.4 5.8 %attention_gradients.1 = (bf16[2,192,3200]{2,1,0:T(8,128)(2,1)}, bf16[2,192,3200]{2,1,0:T(8,128)(2,1)S(1)}) custom-call(s32[1]{0:T(128)} %bitcast.core_ref, bf16[2,2,192,768]{3,2,1,0:T(8,128)(2,1)S(1)} %bitcast.247, bf16[2,2,192,768]{3,2,1,0:T(8,128)(2,1)S(1)} %bitcast.248, bf16[768,2304]{1,0:T(8,128)(2,1)S(1)} %get-tuple-element.405.dqkv_ref, ...), custom_call_target="tpu_custom_call" | custom-call | flops 8800000000 | bytes 1 | tf_op jit(solution)/shard_map/attention_gradients/pallas_call | solution.py:791
  196.6 1.6 collective-permute-start.60
  200.1 1.5 fusion.14
  201.6 2.0 collective-permute-start.57
  203.7 5.4 %add_convert_fusion = bf16[768,768]{1,0:T(8,128)(2,1)S(1)} fusion(bf16[768,768]{1,0:T(8,128)(2,1)} %copy-done.46, bf16[768,2304]{1,0:T(8,128)(2,1)S(1)} %copy-done.45, bf16[768,3200]{1,0:T(8,128)(2,1)} %bitcast.242), kind=kOutput, calls=%fused_computation.4 | convolution fusion | flops 2719678464 | bytes 9437184 | tf_op jit(solution)/shard_map/dot_general | solution.py:30
  209.2 3.4 %collective-permute-done.57 = bf16[1,2,96,768]{3,2,1,0:T(8,128)(2,1)S(1)} collective-permute-done((bf16[1,2,96,768]{3,2,1,0:T(8,128)(2,1)S(1)}, bf16[1,2,96,768]{3,2,1,0:T(8,128)(2,1)S(1)}, u32[]{:S(2)}, u32[]{:S(2)}) %collective-permute-start.57) | collective-permute-done | bytes 294944 | tf_op jit(solution)/shard_map/ppermute | solution.py:574
  214.3 1.8 collective-permute-start.64
  216.4 1.5 fusion.11
  217.8 1.8 collective-permute-start.62
  222.4 1.6 select_reduce_fusion.1
  224.0 1.9 collective-permute-start.69
  226.3 4.0 %collective-permute-done.62 = bf16[1,2,96,768]{3,2,1,0:T(8,128)(2,1)S(1)} collective-permute-done((bf16[1,2,96,768]{3,2,1,0:T(8,128)(2,1)S(1)}, bf16[1,2,96,768]{3,2,1,0:T(8,128)(2,1)S(1)}, u32[]{:S(2)}, u32[]{:S(2)}) %collective-permute-start.62) | collective-permute-done | bytes 294944 | tf_op jit(solution)/shard_map/ppermute | solution.py:574
  230.3 2.0 collective-permute-done.63
  232.4 1.9 collective-permute-done.66
  237.7 1.7 collective-permute-start.67
  240.0 1.6 select_reduce_fusion
  241.7 4.2 %collective-permute-done.67 = bf16[1,2,24,3072]{3,2,1,0:T(8,128)(2,1)S(1)} collective-permute-done((bf16[1,2,24,3072]{3,2,1,0:T(8,128)(2,1)S(1)}, bf16[1,2,24,3072]{3,2,1,0:T(8,128)(2,1)S(1)}, u32[]{:S(2)}, u32[]{:S(2)}) %collective-permute-start.67) | collective-permute-done | bytes 294944 | tf_op jit(solution)/shard_map/ppermute | solution.py:574
  247.4 1.7 collective-permute-start.71
  251.9 3.6 %collective-permute-done.73 = bf16[24,3072]{1,0:T(8,128)(2,1)S(1)} collective-permute-done((bf16[24,3072]{1,0:T(8,128)(2,1)S(1)}, bf16[24,3072]{1,0:T(8,128)(2,1)S(1)}, u32[]{:S(2)}, u32[]{:S(2)}) %collective-permute-start.73) | collective-permute-done | bytes 147488 | tf_op jit(solution)/shard_map/ppermute | solution.py:578
  256.9 1.3 collective-permute-start.74
  259.9 4.2 %collective-permute-done.74 = bf16[1,2,24,3200]{3,2,1,0:T(8,128)(2,1)S(1)} collective-permute-done((bf16[1,2,24,3200]{3,2,1,0:T(8,128)(2,1)S(1)}, bf16[1,2,24,3200]{3,2,1,0:T(8,128)(2,1)S(1)}, u32[]{:S(2)}, u32[]{:S(2)}) %collective-permute-start.74) | collective-permute-done | bytes 307232 | tf_op jit(solution)/shard_map/ppermute | solution.py:574
  268.4 4.8 %collective-permute-done.76 = bf16[1,2,24,3200]{3,2,1,0:T(8,128)(2,1)S(1)} collective-permute-done((bf16[1,2,24,3200]{3,2,1,0:T(8,128)(2,1)S(1)}, bf16[1,2,24,3200]{3,2,1,0:T(8,128)(2,1)S(1)}, u32[]{:S(2)}, u32[]{:S(2)}) %collective-permute-start.76) | collective-permute-done | bytes 307232 | tf_op jit(solution)/shard_map/ppermute | solution.py:574
  276.9 4.2 %collective-permute-done.78 = bf16[24,3200]{1,0:T(8,128)(2,1)S(1)} collective-permute-done((bf16[24,3200]{1,0:T(8,128)(2,1)S(1)}, bf16[24,3200]{1,0:T(8,128)(2,1)S(1)}, u32[]{:S(2)}, u32[]{:S(2)}) %collective-permute-start.78) | collective-permute-done | bytes 153632 | tf_op jit(solution)/shard_map/ppermute | solution.py:578
  (297 shorter events, 78.8 us)
Async XLA Ops:
  3.7 7.7 %collective-permute-start = (bf16[24,3200]{1,0:T(8,128)(2,1)S(1)}, bf16[24,3200]{1,0:T(8,128)(2,1)S(1)}, u32[]{:S(2)}, u32[]{:S(2)}) collective-permute-start(bf16[24,3200]{1,0:T(8,128)(2,1)S(1)} %get-tuple-element.476), channel_id=1, source_target_pairs={{0,16},{16,0},{1,17},{17,1},{2,18},{18,2},{3,19},{19,3},{4,20},{20... | collective-permute-start | bytes 460808 | tf_op jit(solution)/shard_map/ppermute | solution.py:578
  7.7 7.5 %collective-permute-start.3 = (bf16[24,3072]{1,0:T(8,128)(2,1)S(1)}, bf16[24,3072]{1,0:T(8,128)(2,1)S(1)}, u32[]{:S(2)}, u32[]{:S(2)}) collective-permute-start(bf16[24,3072]{1,0:T(8,128)(2,1)S(1)} %get-tuple-element.480), channel_id=1, source_target_pairs={{0,16},{16,0},{1,17},{17,1},{2,18},{18,2},{3,19},{19,3},{4,20},{20... | collective-permute-start | bytes 442376 | tf_op jit(solution)/shard_map/ppermute | solution.py:578
  11.6 9.3 %collective-permute-start.1 = (bf16[1,2,24,3200]{3,2,1,0:T(8,128)(2,1)S(1)}, bf16[1,2,24,3200]{3,2,1,0:T(8,128)(2,1)S(1)}, u32[]{:S(2)}, u32[]{:S(2)}) collective-permute-start(bf16[1,2,24,3200]{3,2,1,0:T(8,128)(2,1)S(1)} %broadcast_select_fusion.1.refs_0_), channel_id=1, source_target_pairs={{1,3},{3,5},{5,7},{7,6},{6,4},{4,2},{2,0},{0,1},{9,8},{11,9},{13,1... | collective-permute-start | bytes 921608 | tf_op jit(solution)/shard_map/ppermute | solution.py:571
  13.7 7.9 %collective-permute-start.2 = (bf16[1,2,24,3200]{3,2,1,0:T(8,128)(2,1)S(1)}, bf16[1,2,24,3200]{3,2,1,0:T(8,128)(2,1)S(1)}, u32[]{:S(2)}, u32[]{:S(2)}) collective-permute-start(bf16[1,2,24,3200]{3,2,1,0:T(8,128)(2,1)S(1)} %broadcast_select_fusion.1.refs_0_), channel_id=1, source_target_pairs={{1,0},{3,1},{5,3},{7,5},{6,7},{4,6},{2,4},{0,2},{9,11},{11,13},{13... | collective-permute-start | bytes 921608 | tf_op jit(solution)/shard_map/ppermute | solution.py:574
  21.6 5.4 %collective-permute-start.7 = (bf16[1,2,24,3200]{3,2,1,0:T(8,128)(2,1)S(1)}, bf16[1,2,24,3200]{3,2,1,0:T(8,128)(2,1)S(1)}, u32[]{:S(2)}, u32[]{:S(2)}) collective-permute-start(bf16[1,2,24,3200]{3,2,1,0:T(8,128)(2,1)S(1)} %collective-permute-done.1.refs_1_), channel_id=1, source_target_pairs={{0,8},{8,0},{1,9},{9,1},{2,10},{10,2},{3,11},{11,3},{4,12},{12,4},... | collective-permute-start | bytes 921608 | tf_op jit(solution)/shard_map/ppermute | solution.py:578
  21.7 8.9 %collective-permute-start.5 = (bf16[1,2,24,3200]{3,2,1,0:T(8,128)(2,1)S(1)}, bf16[1,2,24,3200]{3,2,1,0:T(8,128)(2,1)S(1)}, u32[]{:S(2)}, u32[]{:S(2)}) collective-permute-start(bf16[1,2,24,3200]{3,2,1,0:T(8,128)(2,1)S(1)} %collective-permute-done.1.refs_1_), channel_id=1, source_target_pairs={{1,3},{3,5},{5,7},{7,6},{6,4},{4,2},{2,0},{0,1},{9,8},{11,9},{13,1... | collective-permute-start | bytes 921608 | tf_op jit(solution)/shard_map/ppermute | solution.py:571
  23.4 4.1 %collective-permute-start.8 = (bf16[1,2,24,3200]{3,2,1,0:T(8,128)(2,1)S(1)}, bf16[1,2,24,3200]{3,2,1,0:T(8,128)(2,1)S(1)}, u32[]{:S(2)}, u32[]{:S(2)}) collective-permute-start(bf16[1,2,24,3200]{3,2,1,0:T(8,128)(2,1)S(1)} %collective-permute-done.2.refs_5_), channel_id=1, source_target_pairs={{0,8},{8,0},{1,9},{9,1},{2,10},{10,2},{3,11},{11,3},{4,12},{12,4},... | collective-permute-start | bytes 921608 | tf_op jit(solution)/shard_map/ppermute | solution.py:578
  23.6 9.5 %collective-permute-start.6 = (bf16[1,2,24,3200]{3,2,1,0:T(8,128)(2,1)S(1)}, bf16[1,2,24,3200]{3,2,1,0:T(8,128)(2,1)S(1)}, u32[]{:S(2)}, u32[]{:S(2)}) collective-permute-start(bf16[1,2,24,3200]{3,2,1,0:T(8,128)(2,1)S(1)} %collective-permute-done.2.refs_5_), channel_id=1, source_target_pairs={{1,0},{3,1},{5,3},{7,5},{6,7},{4,6},{2,4},{0,2},{9,11},{11,13},{13... | collective-permute-start | bytes 921608 | tf_op jit(solution)/shard_map/ppermute | solution.py:574
  25.2 21.4 %collective-permute-start.13 = (bf16[3,144,768]{2,1,0:T(8,128)(2,1)S(1)}, bf16[3,144,768]{2,1,0:T(8,128)(2,1)S(1)}, u32[]{:S(2)}, u32[]{:S(2)}) collective-permute-start(bf16[3,144,768]{2,1,0:T(8,128)(2,1)S(1)} %pad_maximum_fusion.4), channel_id=1, source_target_pairs={{0,16},{16,0},{1,17},{17,1},{2,18},{18,2},{3,19},{19,3},{4,20},{20... | collective-permute-start | bytes 1990664 | tf_op jit(solution)/shard_map/ppermute | solution.py:578
  27.0 10.0 %collective-permute-start.11 = (bf16[1,2,24,3072]{3,2,1,0:T(8,128)(2,1)S(1)}, bf16[1,2,24,3072]{3,2,1,0:T(8,128)(2,1)S(1)}, u32[]{:S(2)}, u32[]{:S(2)}) collective-permute-start(bf16[1,2,24,3072]{3,2,1,0:T(8,128)(2,1)S(1)} %broadcast_select_fusion.5.refs_0_), channel_id=1, source_target_pairs={{1,3},{3,5},{5,7},{7,6},{6,4},{4,2},{2,0},{0,1},{9,8},{11,9},{13,1... | collective-permute-start | bytes 884744 | tf_op jit(solution)/shard_map/ppermute | solution.py:571
  28.3 9.4 %collective-permute-start.12 = (bf16[1,2,24,3072]{3,2,1,0:T(8,128)(2,1)S(1)}, bf16[1,2,24,3072]{3,2,1,0:T(8,128)(2,1)S(1)}, u32[]{:S(2)}, u32[]{:S(2)}) collective-permute-start(bf16[1,2,24,3072]{3,2,1,0:T(8,128)(2,1)S(1)} %broadcast_select_fusion.5.refs_0_), channel_id=1, source_target_pairs={{1,0},{3,1},{5,3},{7,5},{6,7},{4,6},{2,4},{0,2},{9,11},{11,13},{13... | collective-permute-start | bytes 884744 | tf_op jit(solution)/shard_map/ppermute | solution.py:574
  30.6 7.7 %collective-permute-start.16 = (bf16[1,2,24,3072]{3,2,1,0:T(8,128)(2,1)S(1)}, bf16[1,2,24,3072]{3,2,1,0:T(8,128)(2,1)S(1)}, u32[]{:S(2)}, u32[]{:S(2)}) collective-permute-start(bf16[1,2,24,3072]{3,2,1,0:T(8,128)(2,1)S(1)} %broadcast_select_fusion.5.refs_0_), channel_id=1, source_target_pairs={{0,8},{8,0},{1,9},{9,1},{2,10},{10,2},{3,11},{11,3},{4,12},{12,4},... | collective-permute-start | bytes 884744 | tf_op jit(solution)/shard_map/ppermute | solution.py:578
  33.2 8.3 %collective-permute-start.10 = (bf16[1,2,24,3200]{3,2,1,0:T(8,128)(2,1)S(1)}, bf16[1,2,24,3200]{3,2,1,0:T(8,128)(2,1)S(1)}, u32[]{:S(2)}, u32[]{:S(2)}) collective-permute-start(bf16[1,2,24,3200]{3,2,1,0:T(8,128)(2,1)S(1)} %collective-permute-done.6.refs_6_), channel_id=1, source_target_pairs={{1,0},{3,1},{5,3},{7,5},{6,7},{4,6},{2,4},{0,2},{9,11},{11,13},{13... | collective-permute-start | bytes 921608 | tf_op jit(solution)/shard_map/ppermute | solution.py:574
  36.9 5.2 %collective-permute-start.15 = (bf16[1,2,24,3200]{3,2,1,0:T(8,128)(2,1)S(1)}, bf16[1,2,24,3200]{3,2,1,0:T(8,128)(2,1)S(1)}, u32[]{:S(2)}, u32[]{:S(2)}) collective-permute-start(bf16[1,2,24,3200]{3,2,1,0:T(8,128)(2,1)S(1)} %collective-permute-done.6.refs_6_), channel_id=1, source_target_pairs={{0,8},{8,0},{1,9},{9,1},{2,10},{10,2},{3,11},{11,3},{4,12},{12,4},... | collective-permute-start | bytes 921608 | tf_op jit(solution)/shard_map/ppermute | solution.py:578
  39.0 7.5 %collective-permute-start.9 = (bf16[1,2,24,3200]{3,2,1,0:T(8,128)(2,1)S(1)}, bf16[1,2,24,3200]{3,2,1,0:T(8,128)(2,1)S(1)}, u32[]{:S(2)}, u32[]{:S(2)}) collective-permute-start(bf16[1,2,24,3200]{3,2,1,0:T(8,128)(2,1)S(1)} %collective-permute-done.5.refs_2_), channel_id=1, source_target_pairs={{1,3},{3,5},{5,7},{7,6},{6,4},{4,2},{2,0},{0,1},{9,8},{11,9},{13,1... | collective-permute-start | bytes 921608 | tf_op jit(solution)/shard_map/ppermute | solution.py:571
  46.6 9.1 %collective-permute-start.21 = (bf16[1,2,24,3200]{3,2,1,0:T(8,128)(2,1)S(1)}, bf16[1,2,24,3200]{3,2,1,0:T(8,128)(2,1)S(1)}, u32[]{:S(2)}, u32[]{:S(2)}) collective-permute-start(bf16[1,2,24,3200]{3,2,1,0:T(8,128)(2,1)S(1)} %collective-permute-done.9.refs_3_), channel_id=1, source_target_pairs={{0,8},{8,0},{1,9},{9,1},{2,10},{10,2},{3,11},{11,3},{4,12},{12,4},... | collective-permute-start | bytes 921608 | tf_op jit(solution)/shard_map/ppermute | solution.py:578
  46.6 11.0 %collective-permute-start.22 = (bf16[1,2,24,3200]{3,2,1,0:T(8,128)(2,1)S(1)}, bf16[1,2,24,3200]{3,2,1,0:T(8,128)(2,1)S(1)}, u32[]{:S(2)}, u32[]{:S(2)}) collective-permute-start(bf16[1,2,24,3200]{3,2,1,0:T(8,128)(2,1)S(1)} %collective-permute-done.10.refs_7_), channel_id=1, source_target_pairs={{0,8},{8,0},{1,9},{9,1},{2,10},{10,2},{3,11},{11,3},{4,12},{12,4},... | collective-permute-start | bytes 921608 | tf_op jit(solution)/shard_map/ppermute | solution.py:578
  47.8 4.9 %collective-permute-start.24 = (bf16[1,2,24,3072]{3,2,1,0:T(8,128)(2,1)S(1)}, bf16[1,2,24,3072]{3,2,1,0:T(8,128)(2,1)S(1)}, u32[]{:S(2)}, u32[]{:S(2)}) collective-permute-start(bf16[1,2,24,3072]{3,2,1,0:T(8,128)(2,1)S(1)} %collective-permute-done.12.refs_5_), channel_id=1, source_target_pairs={{0,8},{8,0},{1,9},{9,1},{2,10},{10,2},{3,11},{11,3},{4,12},{12,4},... | collective-permute-start | bytes 884744 | tf_op jit(solution)/shard_map/ppermute | solution.py:578
  48.4 11.6 %collective-permute-start.20 = (bf16[96,768]{1,0:T(8,128)(2,1)S(1)}, bf16[96,768]{1,0:T(8,128)(2,1)S(1)}, u32[]{:S(2)}, u32[]{:S(2)}) collective-permute-start(bf16[96,768]{1,0:T(8,128)(2,1)S(1)} %get-tuple-element.478), channel_id=1, source_target_pairs={{0,16},{16,0},{1,17},{17,1},{2,18},{18,2},{3,19},{19,3},{4,20},{20... | collective-permute-start | bytes 442376 | tf_op jit(solution)/shard_map/ppermute | solution.py:578
  50.8 12.4 %collective-permute-start.17 = (bf16[1,2,24,3200]{3,2,1,0:T(8,128)(2,1)S(1)}, bf16[1,2,24,3200]{3,2,1,0:T(8,128)(2,1)}, u32[]{:S(2)}, u32[]{:S(2)}) collective-permute-start(bf16[1,2,24,3200]{3,2,1,0:T(8,128)(2,1)S(1)} %collective-permute-done.9.refs_3_), channel_id=1, source_target_pairs={{1,3},{3,5},{5,7},{7,6},{6,4},{4,2},{2,0},{0,1},{9,8},{11,9},{13,1... | collective-permute-start | bytes 921608 | tf_op jit(solution)/shard_map/ppermute | solution.py:571
  53.5 9.2 %collective-permute-start.18 = (bf16[1,2,24,3072]{3,2,1,0:T(8,128)(2,1)S(1)}, bf16[1,2,24,3072]{3,2,1,0:T(8,128)(2,1)}, u32[]{:S(2)}, u32[]{:S(2)}) collective-permute-start(bf16[1,2,24,3072]{3,2,1,0:T(8,128)(2,1)S(1)} %collective-permute-done.11.refs_1_), channel_id=1, source_target_pairs={{1,3},{3,5},{5,7},{7,6},{6,4},{4,2},{2,0},{0,1},{9,8},{11,9},{13,1... | collective-permute-start | bytes 884744 | tf_op jit(solution)/shard_map/ppermute | solution.py:571
  56.4 6.8 %collective-permute-start.19 = (bf16[1,2,24,3072]{3,2,1,0:T(8,128)(2,1)S(1)}, bf16[1,2,24,3072]{3,2,1,0:T(8,128)(2,1)}, u32[]{:S(2)}, u32[]{:S(2)}) collective-permute-start(bf16[1,2,24,3072]{3,2,1,0:T(8,128)(2,1)S(1)} %collective-permute-done.12.refs_5_), channel_id=1, source_target_pairs={{1,0},{3,1},{5,3},{7,5},{6,7},{4,6},{2,4},{0,2},{9,11},{11,13},{13... | collective-permute-start | bytes 884744 | tf_op jit(solution)/shard_map/ppermute | solution.py:574
  63.2 6.4 %collective-permute-start.33 = (bf16[1,2,24,3200]{3,2,1,0:T(8,128)(2,1)}, bf16[1,2,24,3200]{3,2,1,0:T(8,128)(2,1)}, u32[]{:S(2)}, u32[]{:S(2)}) collective-permute-start(bf16[1,2,24,3200]{3,2,1,0:T(8,128)(2,1)} %collective-permute-done.17.refs_4_), channel_id=1, source_target_pairs={{0,8},{8,0},{1,9},{9,1},{2,10},{10,2},{3,11},{11,3},{4,12},{12,4},... | collective-permute-start | bytes 921608 | tf_op jit(solution)/shard_map/ppermute | solution.py:578
  64.7 17.4 %collective-permute-start.29 = (bf16[3,128,768]{2,1,0:T(8,128)(2,1)}, bf16[3,128,768]{2,1,0:T(8,128)(2,1)}, u32[]{:S(2)}, u32[]{:S(2)}) collective-permute-start(bf16[3,128,768]{2,1,0:T(8,128)(2,1)} %select_reduce_fusion.3), channel_id=1, source_target_pairs={{0,16},{16,0},{1,17},{17,1},{2,18},{18,2},{3,19},{19,3},{4,20},{20... | collective-permute-start | bytes 1769480 | tf_op jit(solution)/shard_map/ppermute | solution.py:578
  65.8 16.2 %collective-permute-start.27 = (bf16[1,2,96,768]{3,2,1,0:T(8,128)(2,1)S(1)}, bf16[1,2,96,768]{3,2,1,0:T(8,128)(2,1)S(1)}, u32[]{:S(2)}, u32[]{:S(2)}) collective-permute-start(bf16[1,2,96,768]{3,2,1,0:T(8,128)(2,1)S(1)} %broadcast_select_fusion.4.refs_0_), channel_id=1, source_target_pairs={{1,3},{3,5},{5,7},{7,6},{6,4},{4,2},{2,0},{0,1},{9,8},{11,9},{13,1... | collective-permute-start | bytes 884744 | tf_op jit(solution)/shard_map/ppermute | solution.py:571
  67.5 14.6 %collective-permute-start.28 = (bf16[1,2,96,768]{3,2,1,0:T(8,128)(2,1)S(1)}, bf16[1,2,96,768]{3,2,1,0:T(8,128)(2,1)S(1)}, u32[]{:S(2)}, u32[]{:S(2)}) collective-permute-start(bf16[1,2,96,768]{3,2,1,0:T(8,128)(2,1)S(1)} %broadcast_select_fusion.4.refs_0_), channel_id=1, source_target_pairs={{1,0},{3,1},{5,3},{7,5},{6,7},{4,6},{2,4},{0,2},{9,11},{11,13},{13... | collective-permute-start | bytes 884744 | tf_op jit(solution)/shard_map/ppermute | solution.py:574
  68.5 13.6 %collective-permute-start.25 = (bf16[1,2,24,3072]{3,2,1,0:T(8,128)(2,1)}, bf16[1,2,24,3072]{3,2,1,0:T(8,128)(2,1)S(1)}, u32[]{:S(2)}, u32[]{:S(2)}) collective-permute-start(bf16[1,2,24,3072]{3,2,1,0:T(8,128)(2,1)} %collective-permute-done.18.refs_2_), channel_id=1, source_target_pairs={{1,3},{3,5},{5,7},{7,6},{6,4},{4,2},{2,0},{0,1},{9,8},{11,9},{13,1... | collective-permute-start | bytes 884744 | tf_op jit(solution)/shard_map/ppermute | solution.py:571
  69.6 12.5 %collective-permute-start.26 = (bf16[1,2,24,3072]{3,2,1,0:T(8,128)(2,1)}, bf16[1,2,24,3072]{3,2,1,0:T(8,128)(2,1)S(1)}, u32[]{:S(2)}, u32[]{:S(2)}) collective-permute-start(bf16[1,2,24,3072]{3,2,1,0:T(8,128)(2,1)} %collective-permute-done.19.refs_6_), channel_id=1, source_target_pairs={{1,0},{3,1},{5,3},{7,5},{6,7},{4,6},{2,4},{0,2},{9,11},{11,13},{13... | collective-permute-start | bytes 884744 | tf_op jit(solution)/shard_map/ppermute | solution.py:574
  82.2 4.4 %collective-permute-start.38 = (bf16[1,2,24,3072]{3,2,1,0:T(8,128)(2,1)S(1)}, bf16[1,2,24,3072]{3,2,1,0:T(8,128)(2,1)S(1)}, u32[]{:S(2)}, u32[]{:S(2)}) collective-permute-start(bf16[1,2,24,3072]{3,2,1,0:T(8,128)(2,1)S(1)} %collective-permute-done.26.refs_7_), channel_id=1, source_target_pairs={{0,8},{8,0},{1,9},{9,1},{2,10},{10,2},{3,11},{11,3},{4,12},{12,4},... | collective-permute-start | bytes 884744 | tf_op jit(solution)/shard_map/ppermute | solution.py:578
  83.2 16.8 %collective-permute-start.34 = (bf16[1,2,24,3072]{3,2,1,0:T(8,128)(2,1)S(1)}, bf16[1,2,24,3072]{3,2,1,0:T(8,128)(2,1)S(1)}, u32[]{:S(2)}, u32[]{:S(2)}) collective-permute-start(bf16[1,2,24,3072]{3,2,1,0:T(8,128)(2,1)S(1)} %collective-permute-done.25.refs_3_), channel_id=1, source_target_pairs={{1,3},{3,5},{5,7},{7,6},{6,4},{4,2},{2,0},{0,1},{9,8},{11,9},{13,1... | collective-permute-start | bytes 884744 | tf_op jit(solution)/shard_map/ppermute | solution.py:571
  84.6 15.4 %collective-permute-start.35 = (bf16[1,2,96,768]{3,2,1,0:T(8,128)(2,1)S(1)}, bf16[1,2,96,768]{3,2,1,0:T(8,128)(2,1)S(1)}, u32[]{:S(2)}, u32[]{:S(2)}) collective-permute-start(bf16[1,2,96,768]{3,2,1,0:T(8,128)(2,1)S(1)} %collective-permute-done.27.refs_1_), channel_id=1, source_target_pairs={{1,3},{3,5},{5,7},{7,6},{6,4},{4,2},{2,0},{0,1},{9,8},{11,9},{13,1... | collective-permute-start | bytes 884744 | tf_op jit(solution)/shard_map/ppermute | solution.py:571
  86.6 13.4 %collective-permute-start.36 = (bf16[1,2,96,768]{3,2,1,0:T(8,128)(2,1)S(1)}, bf16[1,2,96,768]{3,2,1,0:T(8,128)(2,1)S(1)}, u32[]{:S(2)}, u32[]{:S(2)}) collective-permute-start(bf16[1,2,96,768]{3,2,1,0:T(8,128)(2,1)S(1)} %collective-permute-done.28.refs_5_), channel_id=1, source_target_pairs={{1,0},{3,1},{5,3},{7,5},{6,7},{4,6},{2,4},{0,2},{9,11},{11,13},{13... | collective-permute-start | bytes 884744 | tf_op jit(solution)/shard_map/ppermute | solution.py:574
  100.7 9.5 %collective-permute-start.41 = (bf16[1,2,96,768]{3,2,1,0:T(8,128)(2,1)S(1)}, bf16[1,2,96,768]{3,2,1,0:T(8,128)(2,1)S(1)}, u32[]{:S(2)}, u32[]{:S(2)}) collective-permute-start(bf16[1,2,96,768]{3,2,1,0:T(8,128)(2,1)S(1)} %collective-permute-done.35.refs_2_), channel_id=1, source_target_pairs={{1,3},{3,5},{5,7},{7,6},{6,4},{4,2},{2,0},{0,1},{9,8},{11,9},{13,1... | collective-permute-start | bytes 884744 | tf_op jit(solution)/shard_map/ppermute | solution.py:571
  102.7 7.6 %collective-permute-start.42 = (bf16[1,2,96,768]{3,2,1,0:T(8,128)(2,1)S(1)}, bf16[1,2,96,768]{3,2,1,0:T(8,128)(2,1)S(1)}, u32[]{:S(2)}, u32[]{:S(2)}) collective-permute-start(bf16[1,2,96,768]{3,2,1,0:T(8,128)(2,1)S(1)} %collective-permute-done.36.refs_6_), channel_id=1, source_target_pairs={{1,0},{3,1},{5,3},{7,5},{6,7},{4,6},{2,4},{0,2},{9,11},{11,13},{13... | collective-permute-start | bytes 884744 | tf_op jit(solution)/shard_map/ppermute | solution.py:574
  110.8 9.5 %collective-permute-start.46 = (bf16[1,2,96,768]{3,2,1,0:T(8,128)(2,1)S(1)}, bf16[1,2,96,768]{3,2,1,0:T(8,128)(2,1)S(1)}, u32[]{:S(2)}, u32[]{:S(2)}) collective-permute-start(bf16[1,2,96,768]{3,2,1,0:T(8,128)(2,1)S(1)} %collective-permute-done.41.refs_3_), channel_id=1, source_target_pairs={{1,3},{3,5},{5,7},{7,6},{6,4},{4,2},{2,0},{0,1},{9,8},{11,9},{13,1... | collective-permute-start | bytes 884744 | tf_op jit(solution)/shard_map/ppermute | solution.py:571
  137.7 17.7 %collective-permute-start.50 = (bf16[2,768,768]{2,1,0:T(8,128)(2,1)S(1)}, bf16[2,768,768]{2,1,0:T(8,128)(2,1)S(1)}, u32[]{:S(2)}, u32[]{:S(2)}) collective-permute-start(bf16[2,768,768]{2,1,0:T(8,128)(2,1)S(1)} %get-tuple-element.368), channel_id=1, source_target_pairs={{0,8},{8,0},{1,9},{9,1},{2,10},{10,2},{3,11},{11,3},{4,12},{12,4},... | collective-permute-start | bytes 7077896 | tf_op jit(solution)/shard_map/ppermute | solution.py:578
  156.9 26.6 %collective-permute-start.52 = (bf16[2,192,3072]{2,1,0:T(8,128)(2,1)}, bf16[2,192,3072]{2,1,0:T(8,128)(2,1)}, u32[]{:S(2)}, u32[]{:S(2)}) collective-permute-start(bf16[2,192,3072]{2,1,0:T(8,128)(2,1)} %get-tuple-element.379), channel_id=1, source_target_pairs={{0,8},{8,0},{1,9},{9,1},{2,10},{10,2},{3,11},{11,3},{4,12},{12,4},... | collective-permute-start | bytes 7077896 | tf_op jit(solution)/shard_map/ppermute | solution.py:578
  157.3 26.2 %collective-permute-start.53 = (bf16[3,128,768]{2,1,0:T(8,128)(2,1)S(1)}, bf16[3,128,768]{2,1,0:T(8,128)(2,1)S(1)}, u32[]{:S(2)}, u32[]{:S(2)}) collective-permute-start(bf16[3,128,768]{2,1,0:T(8,128)(2,1)S(1)} %bitcast.263), channel_id=1, source_target_pairs={{0,16},{16,0},{1,17},{17,1},{2,18},{18,2},{3,19},{19,3},{4,20},{20... | collective-permute-start | bytes 1769480 | tf_op jit(solution)/shard_map/ppermute | solution.py:578
  159.7 23.7 %collective-permute-start.51 = (bf16[1,2,96,768]{3,2,1,0:T(8,128)(2,1)S(1)}, bf16[1,2,96,768]{3,2,1,0:T(8,128)(2,1)S(1)}, u32[]{:S(2)}, u32[]{:S(2)}) collective-permute-start(bf16[1,2,96,768]{3,2,1,0:T(8,128)(2,1)S(1)} %get-tuple-element.470), channel_id=1, source_target_pairs={{1,0},{3,1},{5,3},{7,5},{6,7},{4,6},{2,4},{0,2},{9,11},{11,13},{13... | collective-permute-start | bytes 884744 | tf_op jit(solution)/shard_map/ppermute | solution.py:574
  160.3 36.0 %collective-permute-start.55 = (bf16[1,2,96,768]{3,2,1,0:T(8,128)(2,1)S(1)}, bf16[1,2,96,768]{3,2,1,0:T(8,128)(2,1)S(1)}, u32[]{:S(2)}, u32[]{:S(2)}) collective-permute-start(bf16[1,2,96,768]{3,2,1,0:T(8,128)(2,1)S(1)} %get-tuple-element.469), channel_id=1, source_target_pairs={{1,3},{3,5},{5,7},{7,6},{6,4},{4,2},{2,0},{0,1},{9,8},{11,9},{13,1... | collective-permute-start | bytes 884744 | tf_op jit(solution)/shard_map/ppermute | solution.py:571
  186.3 10.0 %collective-permute-start.56 = (bf16[1,2,24,3072]{3,2,1,0:T(8,128)(2,1)S(1)}, bf16[1,2,24,3072]{3,2,1,0:T(8,128)(2,1)}, u32[]{:S(2)}, u32[]{:S(2)}) collective-permute-start(bf16[1,2,24,3072]{3,2,1,0:T(8,128)(2,1)S(1)} %get-tuple-element.466), channel_id=1, source_target_pairs={{1,0},{3,1},{5,3},{7,5},{6,7},{4,6},{2,4},{0,2},{9,11},{11,13},{13... | collective-permute-start | bytes 884744 | tf_op jit(solution)/shard_map/ppermute | solution.py:574
  187.9 8.4 %collective-permute-start.54 = (bf16[1,2,96,768]{3,2,1,0:T(8,128)(2,1)S(1)}, bf16[1,2,96,768]{3,2,1,0:T(8,128)(2,1)}, u32[]{:S(2)}, u32[]{:S(2)}) collective-permute-start(bf16[1,2,96,768]{3,2,1,0:T(8,128)(2,1)S(1)} %fusion.16), channel_id=1, source_target_pairs={{1,0},{3,1},{5,3},{7,5},{6,7},{4,6},{2,4},{0,2},{9,11},{11,13},{13... | collective-permute-start | bytes 884744 | tf_op jit(solution)/shard_map/ppermute | solution.py:574
  196.3 16.7 %collective-permute-start.61 = (bf16[2,192,3200]{2,1,0:T(8,128)(2,1)}, bf16[2,192,3200]{2,1,0:T(8,128)(2,1)}, u32[]{:S(2)}, u32[]{:S(2)}) collective-permute-start(bf16[2,192,3200]{2,1,0:T(8,128)(2,1)} %get-tuple-element.404), channel_id=1, source_target_pairs={{0,8},{8,0},{1,9},{9,1},{2,10},{10,2},{3,11},{11,3},{4,12},{12,4},... | collective-permute-start | bytes 7372808 | tf_op jit(solution)/shard_map/ppermute | solution.py:578
  196.6 12.6 %collective-permute-start.60 = (bf16[1,2,24,3072]{3,2,1,0:T(8,128)(2,1)}, bf16[1,2,24,3072]{3,2,1,0:T(8,128)(2,1)S(1)}, u32[]{:S(2)}, u32[]{:S(2)}) collective-permute-start(bf16[1,2,24,3072]{3,2,1,0:T(8,128)(2,1)} %get-tuple-element.465), channel_id=1, source_target_pairs={{1,3},{3,5},{5,7},{7,6},{6,4},{4,2},{2,0},{0,1},{9,8},{11,9},{13,1... | collective-permute-start | bytes 884744 | tf_op jit(solution)/shard_map/ppermute | solution.py:571
  199.5 9.7 %collective-permute-start.59 = (bf16[1,2,24,3072]{3,2,1,0:T(8,128)(2,1)S(1)}, bf16[1,2,24,3072]{3,2,1,0:T(8,128)(2,1)S(1)}, u32[]{:S(2)}, u32[]{:S(2)}) collective-permute-start(bf16[1,2,24,3072]{3,2,1,0:T(8,128)(2,1)S(1)} %fusion.13), channel_id=1, source_target_pairs={{1,0},{3,1},{5,3},{7,5},{6,7},{4,6},{2,4},{0,2},{9,11},{11,13},{13... | collective-permute-start | bytes 884744 | tf_op jit(solution)/shard_map/ppermute | solution.py:574
  201.6 11.0 %collective-permute-start.57 = (bf16[1,2,96,768]{3,2,1,0:T(8,128)(2,1)S(1)}, bf16[1,2,96,768]{3,2,1,0:T(8,128)(2,1)S(1)}, u32[]{:S(2)}, u32[]{:S(2)}) collective-permute-start(bf16[1,2,96,768]{3,2,1,0:T(8,128)(2,1)S(1)} %get-tuple-element.468), channel_id=1, source_target_pairs={{1,0},{3,1},{5,3},{7,5},{6,7},{4,6},{2,4},{0,2},{9,11},{11,13},{13... | collective-permute-start | bytes 884744 | tf_op jit(solution)/shard_map/ppermute | solution.py:574
  203.6 9.4 %collective-permute-start.58 = (bf16[1,2,96,768]{3,2,1,0:T(8,128)(2,1)S(1)}, bf16[1,2,96,768]{3,2,1,0:T(8,128)(2,1)S(1)}, u32[]{:S(2)}, u32[]{:S(2)}) collective-permute-start(bf16[1,2,96,768]{3,2,1,0:T(8,128)(2,1)S(1)} %get-tuple-element.467), channel_id=1, source_target_pairs={{1,3},{3,5},{5,7},{7,6},{6,4},{4,2},{2,0},{0,1},{9,8},{11,9},{13,1... | collective-permute-start | bytes 884744 | tf_op jit(solution)/shard_map/ppermute | solution.py:571
  214.3 9.7 %collective-permute-start.64 = (bf16[1,2,24,3072]{3,2,1,0:T(8,128)(2,1)S(1)}, bf16[1,2,24,3072]{3,2,1,0:T(8,128)(2,1)S(1)}, u32[]{:S(2)}, u32[]{:S(2)}) collective-permute-start(bf16[1,2,24,3072]{3,2,1,0:T(8,128)(2,1)S(1)} %get-tuple-element.462), channel_id=1, source_target_pairs={{1,0},{3,1},{5,3},{7,5},{6,7},{4,6},{2,4},{0,2},{9,11},{11,13},{13... | collective-permute-start | bytes 884744 | tf_op jit(solution)/shard_map/ppermute | solution.py:574
  216.1 9.9 %collective-permute-start.65 = (bf16[1,2,24,3072]{3,2,1,0:T(8,128)(2,1)S(1)}, bf16[1,2,24,3072]{3,2,1,0:T(8,128)(2,1)S(1)}, u32[]{:S(2)}, u32[]{:S(2)}) collective-permute-start(bf16[1,2,24,3072]{3,2,1,0:T(8,128)(2,1)S(1)} %get-tuple-element.461), channel_id=1, source_target_pairs={{1,3},{3,5},{5,7},{7,6},{6,4},{4,2},{2,0},{0,1},{9,8},{11,9},{13,1... | collective-permute-start | bytes 884744 | tf_op jit(solution)/shard_map/ppermute | solution.py:571
  217.8 12.5 %collective-permute-start.62 = (bf16[1,2,96,768]{3,2,1,0:T(8,128)(2,1)S(1)}, bf16[1,2,96,768]{3,2,1,0:T(8,128)(2,1)S(1)}, u32[]{:S(2)}, u32[]{:S(2)}) collective-permute-start(bf16[1,2,96,768]{3,2,1,0:T(8,128)(2,1)S(1)} %get-tuple-element.464), channel_id=1, source_target_pairs={{1,0},{3,1},{5,3},{7,5},{6,7},{4,6},{2,4},{0,2},{9,11},{11,13},{13... | collective-permute-start | bytes 884744 | tf_op jit(solution)/shard_map/ppermute | solution.py:574
  219.6 12.7 %collective-permute-start.63 = (bf16[1,2,96,768]{3,2,1,0:T(8,128)(2,1)S(1)}, bf16[1,2,96,768]{3,2,1,0:T(8,128)(2,1)S(1)}, u32[]{:S(2)}, u32[]{:S(2)}) collective-permute-start(bf16[1,2,96,768]{3,2,1,0:T(8,128)(2,1)S(1)} %get-tuple-element.463), channel_id=1, source_target_pairs={{1,3},{3,5},{5,7},{7,6},{6,4},{4,2},{2,0},{0,1},{9,8},{11,9},{13,1... | collective-permute-start | bytes 884744 | tf_op jit(solution)/shard_map/ppermute | solution.py:571
  219.9 14.3 %collective-permute-start.66 = (bf16[3,128,768]{2,1,0:T(8,128)(2,1)S(1)}, bf16[3,128,768]{2,1,0:T(8,128)(2,1)S(1)}, u32[]{:S(2)}, u32[]{:S(2)}) collective-permute-start(bf16[3,128,768]{2,1,0:T(8,128)(2,1)S(1)} %bitcast.262), channel_id=1, source_target_pairs={{0,16},{16,0},{1,17},{17,1},{2,18},{18,2},{3,19},{19,3},{4,20},{20... | collective-permute-start | bytes 1769480 | tf_op jit(solution)/shard_map/ppermute | solution.py:578
  224.0 17.6 %collective-permute-start.69 = (bf16[1,2,24,3200]{3,2,1,0:T(8,128)(2,1)S(1)}, bf16[1,2,24,3200]{3,2,1,0:T(8,128)(2,1)S(1)}, u32[]{:S(2)}, u32[]{:S(2)}) collective-permute-start(bf16[1,2,24,3200]{3,2,1,0:T(8,128)(2,1)S(1)} %get-tuple-element.458), channel_id=1, source_target_pairs={{1,0},{3,1},{5,3},{7,5},{6,7},{4,6},{2,4},{0,2},{9,11},{11,13},{13... | collective-permute-start | bytes 921608 | tf_op jit(solution)/shard_map/ppermute | solution.py:574
  226.0 25.9 %collective-permute-start.72 = (bf16[1,2,24,3200]{3,2,1,0:T(8,128)(2,1)S(1)}, bf16[1,2,24,3200]{3,2,1,0:T(8,128)(2,1)S(1)}, u32[]{:S(2)}, u32[]{:S(2)}) collective-permute-start(bf16[1,2,24,3200]{3,2,1,0:T(8,128)(2,1)S(1)} %get-tuple-element.457), channel_id=1, source_target_pairs={{1,3},{3,5},{5,7},{7,6},{6,4},{4,2},{2,0},{0,1},{9,8},{11,9},{13,1... | collective-permute-start | bytes 921608 | tf_op jit(solution)/shard_map/ppermute | solution.py:571
  235.4 6.2 %collective-permute-start.70 = (bf16[96,768]{1,0:T(8,128)(2,1)S(1)}, bf16[96,768]{1,0:T(8,128)(2,1)S(1)}, u32[]{:S(2)}, u32[]{:S(2)}) collective-permute-start(bf16[96,768]{1,0:T(8,128)(2,1)S(1)} %fusion.24), channel_id=1, source_target_pairs={{0,16},{16,0},{1,17},{17,1},{2,18},{18,2},{3,19},{19,3},{4,20},{20... | collective-permute-start | bytes 442376 | tf_op jit(solution)/shard_map/ppermute | solution.py:578
  237.7 8.1 %collective-permute-start.67 = (bf16[1,2,24,3072]{3,2,1,0:T(8,128)(2,1)S(1)}, bf16[1,2,24,3072]{3,2,1,0:T(8,128)(2,1)S(1)}, u32[]{:S(2)}, u32[]{:S(2)}) collective-permute-start(bf16[1,2,24,3072]{3,2,1,0:T(8,128)(2,1)S(1)} %get-tuple-element.460), channel_id=1, source_target_pairs={{1,0},{3,1},{5,3},{7,5},{6,7},{4,6},{2,4},{0,2},{9,11},{11,13},{13... | collective-permute-start | bytes 884744 | tf_op jit(solution)/shard_map/ppermute | solution.py:574
  239.5 6.8 %collective-permute-start.68 = (bf16[1,2,24,3072]{3,2,1,0:T(8,128)(2,1)S(1)}, bf16[1,2,24,3072]{3,2,1,0:T(8,128)(2,1)S(1)}, u32[]{:S(2)}, u32[]{:S(2)}) collective-permute-start(bf16[1,2,24,3072]{3,2,1,0:T(8,128)(2,1)S(1)} %get-tuple-element.459), channel_id=1, source_target_pairs={{1,3},{3,5},{5,7},{7,6},{6,4},{4,2},{2,0},{0,1},{9,8},{11,9},{13,1... | collective-permute-start | bytes 884744 | tf_op jit(solution)/shard_map/ppermute | solution.py:571
  247.4 8.1 %collective-permute-start.71 = (bf16[1,2,24,3200]{3,2,1,0:T(8,128)(2,1)S(1)}, bf16[1,2,24,3200]{3,2,1,0:T(8,128)(2,1)S(1)}, u32[]{:S(2)}, u32[]{:S(2)}) collective-permute-start(bf16[1,2,24,3200]{3,2,1,0:T(8,128)(2,1)S(1)} %fusion.6), channel_id=1, source_target_pairs={{1,0},{3,1},{5,3},{7,5},{6,7},{4,6},{2,4},{0,2},{9,11},{11,13},{13... | collective-permute-start | bytes 921608 | tf_op jit(solution)/shard_map/ppermute | solution.py:574
  250.3 5.2 %collective-permute-start.73 = (bf16[24,3072]{1,0:T(8,128)(2,1)S(1)}, bf16[24,3072]{1,0:T(8,128)(2,1)S(1)}, u32[]{:S(2)}, u32[]{:S(2)}) collective-permute-start(bf16[24,3072]{1,0:T(8,128)(2,1)S(1)} %fusion.25), channel_id=1, source_target_pairs={{0,16},{16,0},{1,17},{17,1},{2,18},{18,2},{3,19},{19,3},{4,20},{20... | collective-permute-start | bytes 442376 | tf_op jit(solution)/shard_map/ppermute | solution.py:578
  256.9 7.2 %collective-permute-start.74 = (bf16[1,2,24,3200]{3,2,1,0:T(8,128)(2,1)S(1)}, bf16[1,2,24,3200]{3,2,1,0:T(8,128)(2,1)S(1)}, u32[]{:S(2)}, u32[]{:S(2)}) collective-permute-start(bf16[1,2,24,3200]{3,2,1,0:T(8,128)(2,1)S(1)} %get-tuple-element.456), channel_id=1, source_target_pairs={{1,0},{3,1},{5,3},{7,5},{6,7},{4,6},{2,4},{0,2},{9,11},{11,13},{13... | collective-permute-start | bytes 921608 | tf_op jit(solution)/shard_map/ppermute | solution.py:574
  258.2 6.9 %collective-permute-start.75 = (bf16[1,2,24,3200]{3,2,1,0:T(8,128)(2,1)S(1)}, bf16[1,2,24,3200]{3,2,1,0:T(8,128)(2,1)S(1)}, u32[]{:S(2)}, u32[]{:S(2)}) collective-permute-start(bf16[1,2,24,3200]{3,2,1,0:T(8,128)(2,1)S(1)} %get-tuple-element.455), channel_id=1, source_target_pairs={{1,3},{3,5},{5,7},{7,6},{6,4},{4,2},{2,0},{0,1},{9,8},{11,9},{13,1... | collective-permute-start | bytes 921608 | tf_op jit(solution)/shard_map/ppermute | solution.py:571
  266.4 6.9 %collective-permute-start.76 = (bf16[1,2,24,3200]{3,2,1,0:T(8,128)(2,1)S(1)}, bf16[1,2,24,3200]{3,2,1,0:T(8,128)(2,1)S(1)}, u32[]{:S(2)}, u32[]{:S(2)}) collective-permute-start(bf16[1,2,24,3200]{3,2,1,0:T(8,128)(2,1)S(1)} %get-tuple-element.454), channel_id=1, source_target_pairs={{1,0},{3,1},{5,3},{7,5},{6,7},{4,6},{2,4},{0,2},{9,11},{11,13},{13... | collective-permute-start | bytes 921608 | tf_op jit(solution)/shard_map/ppermute | solution.py:574
  267.5 7.1 %collective-permute-start.77 = (bf16[1,2,24,3200]{3,2,1,0:T(8,128)(2,1)S(1)}, bf16[1,2,24,3200]{3,2,1,0:T(8,128)(2,1)S(1)}, u32[]{:S(2)}, u32[]{:S(2)}) collective-permute-start(bf16[1,2,24,3200]{3,2,1,0:T(8,128)(2,1)S(1)} %get-tuple-element.453), channel_id=1, source_target_pairs={{1,3},{3,5},{5,7},{7,6},{6,4},{4,2},{2,0},{0,1},{9,8},{11,9},{13,1... | collective-permute-start | bytes 921608 | tf_op jit(solution)/shard_map/ppermute | solution.py:571
  275.7 5.3 %collective-permute-start.78 = (bf16[24,3200]{1,0:T(8,128)(2,1)S(1)}, bf16[24,3200]{1,0:T(8,128)(2,1)S(1)}, u32[]{:S(2)}, u32[]{:S(2)}) collective-permute-start(bf16[24,3200]{1,0:T(8,128)(2,1)S(1)} %fusion.23), channel_id=1, source_target_pairs={{0,16},{16,0},{1,17},{17,1},{2,18},{18,2},{3,19},{19,3},{4,20},{20... | collective-permute-start | bytes 460808 | tf_op jit(solution)/shard_map/ppermute | solution.py:578
  (78 other events, 646.0 us)
where the time goes:
time: 288 us; the launch traced here: 284 us
  starting transfers between devices  78.2 us (27%)
  Pallas kernels  72.2 us (25%)
  waiting for transfers between devices  60.3 us (21%)
  local copies, waits for them, and re-layouts  33.3 us (12%)
  other arithmetic  32.3 us (11%)
  matrix products  5.41 us (2%)
    ppermute x21, starting transfers between devices, forth(): return lax.ppermute(block, ('core', 'f'), self.ahead)  34.4 us
    unnamed x126, local copies, waits for them, and re-layouts  28.4 us
    ppermute x21, starting transfers between devices, back(): return lax.ppermute(block, ('core', 'f'), self.behind)  25 us
    ppermute x21, waiting for transfers between devices, back(): return lax.ppermute(block, ('core', 'f'), self.behind)  24.5 us
    ppermute x21, waiting for transfers between devices, forth(): return lax.ppermute(block, ('core', 'f'), self.ahead)  22.5 us
    ppermute x37, starting transfers between devices, swap(): return lax.ppermute(value, axis, SWAP)  18.8 us
    pallas_call x1, Pallas kernels, feed_back(): pl.pallas_call(back_kernel, out_shape=[jax.ShapeDtypeStruct((parts, run,...  15.9 us
    ppermute x37, waiting for transfers between devices, swap(): return lax.ppermute(value, axis, SWAP)  13.3 us
  transfers between devices with their start and end apart: 79, of which 28 were waited for; matrix products, arithmetic and copies ran while one was open for 12% of the time, Pallas kernels for 20%

commit v1 on v0

--- a/solution.py
+++ b/solution.py
@@ -110,19 +110,11 @@
     unit_ref,
     root_ref,
     low_ref,
-    rows_t_ref,
     ctx_t_ref,
     low_t_ref,
-    out_weight_ref,
     ctx_ref,
 ):
     width = ctx_ref.shape[1]
-    rows_t_ref[...] = rows_ref[...].T
-
-    @pl.when(pl.program_id(0) == 0)
-    def _():
-        out_weight_ref[...] = weight_ref[:, 3 * width : 4 * width]
-
     rows = qkv_ref.shape[0] // 2
     for part in range(3):
         columns = slice(part * width, (part + 1) * width)
@@ -143,6 +135,20 @@
     ctx_t_ref[...] = ctx_ref[...].T
 
 
+def turn_kernel(rows_ref, out_ref):
+    out_ref[...] = rows_ref[...].T
+
+
+def turned(rows):
+    return pl.pallas_call(
+        turn_kernel,
+        out_shape=jax.ShapeDtypeStruct(rows.shape[::-1], rows.dtype),
+        compiler_params=params(12 * 2**20),
+        cost_estimate=taking(2),
+        name="turn_rows",
+    )(rows)
+
+
 def attention(rows_in, lens, whole_a, vectors):
     total, width = rows_in.shape
     rows = 2 * total // lens.shape[0]
@@ -158,15 +164,13 @@
             jax.ShapeDtypeStruct((total, 1), F32),
             jax.ShapeDtypeStruct((total, width), BF16),
         ]
-        + [jax.ShapeDtypeStruct((width, total), BF16)] * 3
-        + [jax.ShapeDtypeStruct((width, width), BF16)],
+        + [jax.ShapeDtypeStruct((width, total), BF16)] * 2,
         grid_spec=pltpu.PrefetchScalarGridSpec(
             num_scalar_prefetch=1,
             grid=(total // rows,),
             in_specs=[tokens(width), whole_spec(whole_a.shape), whole_spec(vectors.shape)],
             out_specs=[tokens(3 * width), tokens(width), tokens(1), tokens(width)]
-            + [pl.BlockSpec((width, rows), lambda i, _: (0, i))] * 3
-            + [fixed((width, width))],
+            + [pl.BlockSpec((width, rows), lambda i, _: (0, i))] * 2,
             scratch_shapes=[pltpu.VMEM((rows, width), BF16)],
         ),
         compiler_params=params(20 * 2**20),
@@ -462,33 +466,41 @@
     return dot(spread, place, NT)
 
 
-def pack_kernel(*refs):
-    matrices, vectors, up_bias_ref, out_ref = refs[:4], refs[4:12], refs[12], refs[13]
-    rows = out_ref.shape[1]
-    for model in range(2):
+def pack_kernel(side_ref, *refs):
+    matrices, vectors, up_bias_ref = refs[:4], refs[4:12], refs[12]
+    rows = refs[13].shape[0]
+    for model, out_ref in ((side_ref[0], refs[13]), (1 - side_ref[0], refs[14])):
+
+        def row(vector):
+            both = vector[...].astype(F32)
+            return jnp.where(model == 0, both[0:1, :], both[1:2, :])
+
         start = 0
         for matrix in matrices:
-            out_ref[model, :, start : start + matrix.shape[2]] = matrix[model]
+            out_ref[:, start : start + matrix.shape[2]] = matrix[model]
             start += matrix.shape[2]
-        eight = jnp.concatenate([v[model : model + 1, :].astype(F32) for v in vectors], axis=0)
-        small = transposed_rows(eight) + folded(up_bias_ref[model : model + 1, :].astype(F32), rows)
-        out_ref[model, :, start:] = small.astype(BF16)
-
-
-def pack(matrices, vectors, up_bias):
+        eight = jnp.concatenate([row(v) for v in vectors], axis=0)
+        small = transposed_rows(eight) + folded(row(up_bias_ref), rows)
+        out_ref[:, start:] = small.astype(BF16)
+
+
+def pack(matrices, vectors, up_bias, side):
     models, rows, _ = matrices[0].shape
     lanes = sum(m.shape[2] for m in matrices) + LANES
     if rows % 8:
         parts = [v[..., None] for v in vectors] + [up_bias.reshape(models, rows, -1)]
         small = jnp.concatenate(parts, axis=-1)
         small = jnp.pad(small, [(0, 0), (0, 0), (0, LANES - small.shape[-1])])
-        return jnp.concatenate(list(matrices) + [small], axis=-1)
+        both = jnp.concatenate(list(matrices) + [small], axis=-1)
+        return pick(both, side, 0), pick(both, 1 - side, 0)
     return pl.pallas_call(
         pack_kernel,
-        out_shape=jax.ShapeDtypeStruct((models, rows, lanes), BF16),
+        out_shape=[jax.ShapeDtypeStruct((rows, lanes), BF16)] * 2,
+        in_specs=[pl.BlockSpec(memory_space=pltpu.SMEM)]
+        + [pl.BlockSpec(memory_space=pltpu.VMEM)] * 13,
         compiler_params=params(VMEM_MOST),
         name="pack_shard",
-    )(*matrices, *vectors, up_bias)
+    )(side.astype(jnp.int32)[None], *matrices, *vectors, up_bias)
 
 
 def small_grads_kernel(down_ref, back_ref, bias_ref, qkv_ref, out_ref):
@@ -668,18 +680,27 @@
         self.got = sent[0]
 
 
+class Kept:
+    def __init__(self, small, *rest):
+        self.small, self.rest = small, rest
+
+
 def slot(movers, work=None):
     now = [m.now() for m in movers]
     sent = [m.launch() for m in movers]
     gathers = [m for m in movers if isinstance(m, Gather)]
     before = [(m.theirs_forth, m.theirs_back) for m in gathers]
     done = None if work is None else work((now, before))
+    if isinstance(done, Kept):
+        kept, done = done.rest, done.small
+    else:
+        kept = None
     sent, done, before = tie(sent, done, before)
     for mover, settled in zip(gathers, before):
         mover.settle(settled)
     for mover, arrived in zip(movers, sent):
         mover.land(arrived)
-    return done
+    return done if kept is None else (done,) + tuple(kept)
 
 
 def assemble_kernel(ring, with_vectors, at_ref, *refs):
@@ -705,6 +726,9 @@
         rows = held[:, :, :, :, :, held.shape[-1] - LANES :]
         small = rows.astype(F32).reshape(-1, LANES)
         refs[2 * count + 1][...] = small.T[:16]
+        width = refs[2 * count + 2].shape[0]
+        output = held[:, :, :, :, :, 3 * width : 4 * width]
+        refs[2 * count + 2][...] = output.astype(F32).reshape(-1, width).astype(BF16)
     for copy in outgoing:
         copy.wait()
 
@@ -723,27 +747,32 @@
             where = (0, 0, half, at[i], 0, 0)
             whole = lax.dynamic_update_slice(whole, block[:, :, None, None], where)
         whole = whole.reshape(-1, lanes)
-        return whole, (whole[:, lanes - LANES :].astype(F32).T[:16] if with_vectors else None)
+        if not with_vectors:
+            return whole, None
+        vectors = whole[:, lanes - LANES :].astype(F32).T[:16]
+        return whole, vectors, whole[:, 3 * width : 4 * width]
     out_shape = [jax.ShapeDtypeStruct(shape, BF16)]
     if with_vectors:
         out_shape.append(jax.ShapeDtypeStruct((16, width), F32))
+        out_shape.append(jax.ShapeDtypeStruct((width, width), BF16))
     out = pl.pallas_call(
         functools.partial(assemble_kernel, ring, with_vectors),
         out_shape=out_shape,
         in_specs=[pl.BlockSpec(memory_space=pltpu.SMEM)]
         + [pl.BlockSpec(memory_space=pl.ANY)] * (2 * count),
         out_specs=[pl.BlockSpec(memory_space=pl.ANY)]
-        + [pl.BlockSpec(memory_space=pltpu.VMEM)] * with_vectors,
+        + [pl.BlockSpec(memory_space=pltpu.VMEM)] * (2 * with_vectors),
         scratch_shapes=[
             pltpu.VMEM(shape, BF16),
             pltpu.SemaphoreType.DMA((2 * count * groups,)),
             pltpu.SemaphoreType.DMA((2 * count * groups,)),
         ],
         cost_estimate=taking(4),
-        compiler_params=params((36 if with_vectors else 8) * 2**20),
+        compiler_params=params((56 if with_vectors else 8) * 2**20),
         name="assemble",
     )(jnp.stack([core, chip]).astype(jnp.int32), *mine, *theirs)
-    return out[0].reshape(-1, lanes), out[1] if with_vectors else None
+    whole = out[0].reshape(-1, lanes)
+    return (whole,) + (tuple(out[1:]) if with_vectors else (None,))
 
 
 class Owners:
@@ -904,7 +933,7 @@
     tokens = 2 * CAP * slots
     parts = 2 * groups
 
-    shard_a = pack(
+    own_a, send_a = pack(
         (query_weight, key_weight, value_weight, output_projection_weight),
         (
             query_bias,
@@ -917,10 +946,9 @@
             second_shift,
         ),
         up_bias,
+        side,
     )
-    block_a = two_sides(
-        pick(shard_a, side, 0), swap(pick(shard_a, 1 - side, 0), "t"), side, groups
-    )
+    block_a = two_sides(own_a, swap(send_a, "t"), side, groups)
 
     own_places, other_places = places(tags, side), places(tags, 1 - side)
     own_len = jnp.sum(jnp.where(own_places, lengths[None, :], 0), axis=1)
@@ -954,16 +982,18 @@
         slot([ring_a, ring_u, ring_d])
 
     def join_attention(now):
-        _, blocks = tie(now, ring_a.blocks())
-        return assemble(ring, *blocks, core, True)
-
-    whole_a, vectors = slot([ring_u, ring_d, trip_cot], join_attention)
+        _, blocks, rows = tie(now, ring_a.blocks(), rows_in)
+        whole, small, out_part = assemble(ring, *blocks, core, True)
+        return Kept((small, turned(rows)), whole, out_part)
+
+    (vectors, rows_t), whole_a, out_weight = slot([ring_u, ring_d, trip_cot], join_attention)
 
     def do_attention(now):
-        _, whole = tie(now, whole_a)
-        return attention(rows_in, lens, whole, vectors)
-
-    qkv, unit1, root1, low1, rows_t, ctx_t, low_t, out_weight = slot([ring_u, ring_d], do_attention)
+        _, counts = tie(now, lens)
+        out = attention(rows_in, counts, whole_a, vectors)
+        return Kept(out[2], *out[:2], *out[3:])
+
+    root1, qkv, unit1, low1, ctx_t, low_t = slot([ring_u, ring_d], do_attention)
 
     def join_up(now):
         _, blocks, own, other = tie(now, ring_u.blocks(), cot_rows, trip_cot.got)
@@ -973,8 +1003,8 @@
     whole_u, cot = slot([ring_d], join_up)
 
     def do_up(now):
-        _, whole = tie(now, whole_u)
-        return up_and_gelu(low1, whole, whole_a)
+        _, rows = tie(now, low1)
+        return up_and_gelu(rows, whole_u, whole_a)
 
     active, slope = slot([ring_d], do_up)
     whole_d, _ = assemble(ring, *ring_d.blocks(), core)
@@ -994,34 +1024,34 @@
     trip = Trip(send_d, "core")
 
     def do_feed_back(now):
-        _, df_now = tie(now, df)
-        return feed_back(
-            df_now, whole_d, slope, whole_u, low_t, unit1, root1, vectors, core1, parts
-        )
-
-    send_u, own_u, da, bias_sums, back_sums = slot([trip], do_feed_back)
+        _, rows = tie(now, vectors)
+        out = feed_back(df, whole_d, slope, whole_u, low_t, unit1, root1, rows, core1, parts)
+        return Kept(out[3:], *out[:3])
+
+    (bias_sums, back_sums), send_u, own_u, da = slot([trip], do_feed_back)
     ring_d = scatter(own_d, trip.got)
 
     def do_attention_back(now):
-        _, da_now = tie(now, da)
-        return attention_back(qkv, da_now, out_weight, lens)
+        _, counts = tie(now, lens)
+        out = attention_back(qkv, da, out_weight, counts)
+        return Kept(out[1], out[0])
 
     def second_half(values):
         return values.reshape(2, CAP, slots, width)[1]
 
-    trip, trip_result = Trip(send_u, "core"), Trip(second_half(tie(result, da)[0]), "t")
-    dqkv, qkv_sums = slot([ring_d, trip, trip_result], do_attention_back)
+    trip, trip_result = Trip(send_u, "core"), Trip(second_half(tie(result, back_sums)[0]), "t")
+    qkv_sums, dqkv = slot([ring_d, trip, trip_result], do_attention_back)
     ring_u = scatter(own_u, trip.got)
 
     def attention_grads(now):
-        _, dqkv_now = tie(now, dqkv)
-        small = small_grads(down_sums, back_sums, bias_sums, qkv_sums)
-        return mixed_grad(rows_t, ctx_t, dqkv_now, da, small, core1, parts)
+        _, sums, place = tie(now, qkv_sums, core1)
+        small = small_grads(down_sums, back_sums, bias_sums, sums)
+        return mixed_grad(rows_t, ctx_t, dqkv, da, small, place, parts)
 
     send_a, own_a = slot([ring_d, ring_u], attention_grads)
     def do_rows(now):
-        _, dq = tie(now, dqkv)
-        rows = (da.astype(F32) + dot(dq, whole_a[:, : 3 * width], NT)).astype(BF16)
+        _, base = tie(now, da)
+        rows = (base.astype(F32) + dot(dqkv, whole_a[:, : 3 * width], NT)).astype(BF16)
         return rows, second_half(rows)
 
     trip = Trip(send_a, "core")

time: 288 us -> 286 us (level)
  local copies, waits for them, and re-layouts: 33.3 us -> 13.3 us
  waiting for transfers between devices: 60.3 us -> 73.3 us
  Pallas kernels: 72.2 us -> 76 us
    unnamed x126 -> x100, local copies, waits for them, and re-layouts: 28.4 us -> 9.39 us
    ppermute x21, waiting for transfers between devices: 22.5 us -> 30.4 us  [forth(): return lax.ppermute(block, ('core', 'f'), self.ahead)]
    ppermute x21, starting transfers between devices: 25 us -> 21.5 us  [back(): return lax.ppermute(block, ('core', 'f'), self.behind)]
    ppermute x37, waiting for transfers between devices: 13.3 us -> 16.7 us  [swap(): return lax.ppermute(value, axis, SWAP)]
    pallas_call x3, Pallas kernels: 8.02 us -> 11.3 us  [assemble(): pl.pallas_call(functools.partial(assemble_kernel, ring, with_vectors), ou...]
  transfers between devices with their start and end apart: 79 -> 79, of which waited for: 28 -> 29; matrix products, arithmetic and copies ran while one was open for 12% -> 13% of each run, Pallas kernels for 20% -> 21%
where the time goes in v1:
time: 286 us; the launch traced here: 281 us
  starting transfers between devices  77.3 us (27%)
  Pallas kernels  76 us (27%)
  waiting for transfers between devices  73.3 us (26%)
  other arithmetic  33.8 us (12%)
  local copies, waits for them, and re-layouts  13.3 us (5%)
  matrix products  5.27 us (2%)
    ppermute x21, starting transfers between devices, forth(): return lax.ppermute(block, ('core', 'f'), self.ahead)  36.4 us
    ppermute x21, waiting for transfers between devices, forth(): return lax.ppermute(block, ('core', 'f'), self.ahead)  30.4 us
    ppermute x21, waiting for transfers between devices, back(): return lax.ppermute(block, ('core', 'f'), self.behind)  26.2 us
    ppermute x21, starting transfers between devices, back(): return lax.ppermute(block, ('core', 'f'), self.behind)  21.5 us
    ppermute x37, starting transfers between devices, swap(): return lax.ppermute(value, axis, SWAP)  19.4 us
    ppermute x37, waiting for transfers between devices, swap(): return lax.ppermute(value, axis, SWAP)  16.7 us
    pallas_call x1, Pallas kernels, feed_back(): pl.pallas_call(back_kernel, out_shape=[jax.ShapeDtypeStruct((parts, run,...  15.7 us
    pallas_call x3, Pallas kernels, assemble(): pl.pallas_call(functools.partial(assemble_kernel, ring, with_vectors), ou...  11.3 us
  transfers between devices with their start and end apart: 79, of which 29 were waited for; matrix products, arithmetic and copies ran while one was open for 13% of the time, Pallas kernels for 21%

profile of v1, /device:TPU:0, one launch (start us, length us, event | category | flops | bytes accessed | tf_op | source)
XLA Modules:
  0.0 280.7 jit_solution(623833352882404518)
XLA Ops:
  0.7 1.9 pack_shard.1
  2.6 2.9 %collective-permute-start = (bf16[24,3200]{1,0:T(8,128)(2,1)}, bf16[24,3200]{1,0:T(8,128)(2,1)S(1)}, u32[]{:S(2)}, u32[]{:S(2)}) collective-permute-start(bf16[24,3200]{1,0:T(8,128)(2,1)} %get-tuple-element.221), channel_id=1, source_target_pairs={{0,16},{16,0},{1,17},{17,1},{2,18},{18,2},{3,19},{19,3},{4,20},{20... | collective-permute-start | bytes 460808 | tf_op jit(solution)/shard_map/ppermute | solution.py:590
  8.2 2.3 collective-permute-done
  11.7 2.1 collective-permute-start.1
  14.0 2.3 select_reduce_fusion.4
  16.5 4.6 %collective-permute-done.1.refs_1_ = bf16[1,2,24,3200]{3,2,1,0:T(8,128)(2,1)S(1)} collective-permute-done((bf16[1,2,24,3200]{3,2,1,0:T(8,128)(2,1)S(1)}, bf16[1,2,24,3200]{3,2,1,0:T(8,128)(2,1)S(1)}, u32[]{:S(2)}, u32[]{:S(2)}) %collective-permute-start.1) | collective-permute-done | bytes 307232 | tf_op jit(solution)/shard_map/ppermute | solution.py:583
  21.9 1.8 collective-permute-start.5
  23.8 1.6 collective-permute-start.6
  25.4 1.5 collective-permute-start.13
  27.6 1.5 collective-permute-start.12
  29.1 1.6 collective-permute-done.5.refs_2_
  30.6 2.8 %collective-permute-done.6.refs_6_ = bf16[1,2,24,3200]{3,2,1,0:T(8,128)(2,1)S(1)} collective-permute-done((bf16[1,2,24,3200]{3,2,1,0:T(8,128)(2,1)S(1)}, bf16[1,2,24,3200]{3,2,1,0:T(8,128)(2,1)S(1)}, u32[]{:S(2)}, u32[]{:S(2)}) %collective-permute-start.6) | collective-permute-done | bytes 307232 | tf_op jit(solution)/shard_map/ppermute | solution.py:586
  33.5 2.1 collective-permute-start.10
  35.6 1.4 collective-permute-done.11.refs_1_
  38.5 1.8 collective-permute-start.9
  41.2 4.1 %collective-permute-done.9.refs_3_ = bf16[1,2,24,3200]{3,2,1,0:T(8,128)(2,1)S(1)} collective-permute-done((bf16[1,2,24,3200]{3,2,1,0:T(8,128)(2,1)S(1)}, bf16[1,2,24,3200]{3,2,1,0:T(8,128)(2,1)S(1)}, u32[]{:S(2)}, u32[]{:S(2)}) %collective-permute-start.9) | collective-permute-done | bytes 307232 | tf_op jit(solution)/shard_map/ppermute | solution.py:583
  46.4 2.0 collective-permute-start.20
  48.4 1.5 collective-permute-start.17
  49.9 1.5 collective-permute-start.18
  54.6 7.1 %collective-permute-done.18.refs_2_ = bf16[1,2,24,3072]{3,2,1,0:T(8,128)(2,1)} collective-permute-done((bf16[1,2,24,3072]{3,2,1,0:T(8,128)(2,1)S(1)}, bf16[1,2,24,3072]{3,2,1,0:T(8,128)(2,1)}, u32[]{:S(2)}, u32[]{:S(2)}) %collective-permute-start.18) | collective-permute-done | bytes 294944 | tf_op jit(solution)/shard_map/ppermute | solution.py:583
  63.5 1.5 collective-permute-start.27
  65.5 1.5 collective-permute-start.25
  68.9 6.3 %assemble.3 = (bf16[1,2,2,8,24,3200]{5,4,3,2,1,0:T(8,128)(2,1)}, f32[16,768]{1,0:T(8,128)}, bf16[768,768]{1,0:T(8,128)(2,1)}) custom-call(s32[2]{0:T(128)} %pad_add_fusion.1.at_ref, bf16[1,2,24,3200]{3,2,1,0:T(8,128)(2,1)} %copy-done.29, bf16[1,2,24,3200]{3,2,1,0:T(8,128)(2,1)} %copy-done.38, bf16[1,2,24,3200]{3,2,1,0:T(8,128)(2,1)} %copy-done.41, ...), custom_call_target="tpu_custom_call" | custom-call | flops 4400000000 | bytes 1 | tf_op jit(solution)/shard_map/assemble/pallas_call | solution.py:758
  76.6 2.8 collective-permute-done.25.refs_3_
  79.4 2.8 collective-permute-done.29
  84.8 1.4 collective-permute-start.35
  86.9 9.8 %attention_forward.1 = (bf16[768,2304]{1,0:T(8,128)(2,1)S(1)}, bf16[768,768]{1,0:T(8,128)(2,1)S(1)}, f32[768,1]{1,0:T(8,128)S(1)}, bf16[768,768]{1,0:T(8,128)(2,...) custom-call(s32[6]{0:T(128)S(1)} %pad_add_fusion.lens_ref, bf16[768,768]{1,0:T(8,128)(2,1)S(1)} %bitcast.235, ...), custom_call_target="tpu_custom_call" | custom-call | flops 15399999488 | bytes 1 | tf_op jit(solution)/shard_map/attention_forward/pallas_call | solution.py:159
  96.7 1.8 copy-done.22
  99.2 1.4 collective-permute-start.41
  101.9 2.6 assemble.4
  104.5 4.4 %collective-permute-done.41.refs_3_ = bf16[1,2,96,768]{3,2,1,0:T(8,128)(2,1)S(1)} collective-permute-done((bf16[1,2,96,768]{3,2,1,0:T(8,128)(2,1)S(1)}, bf16[1,2,96,768]{3,2,1,0:T(8,128)(2,1)S(1)}, u32[]{:S(2)}, u32[]{:S(2)}) %collective-permute-start.41) | collective-permute-done | bytes 294944 | tf_op jit(solution)/shard_map/ppermute | solution.py:583
  109.5 1.6 collective-permute-start.46
  111.0 7.5 %up_gelu.1 = (bf16[768,3072]{1,0:T(8,128)(2,1)S(1)}, bf16[768,3072]{1,0:T(8,128)(2,1)S(1)}) custom-call(bf16[768,768]{1,0:T(8,128)(2,1)S(1)} %get-tuple-element.338.low_ref, bf16[768,3072]{1,0:T(8,128)(2,1)S(1)} %bitcast.241, bf16[768,3200]{1,0:T(8,128)(2,1)S(1)} %bitcast.240), custom_call_target="tpu_custom_call" | custom-call | flops 11000000512 | bytes 1 | tf_op jit(solution)/shard_map/up_gelu/pallas_call | solution.py:271
  118.7 1.5 collective-permute-done.49.refs_12_
  120.2 2.4 assemble.5
  122.6 6.2 %down_norm.1 = (bf16[768,768]{1,0:T(8,128)(2,1)S(1)}, bf16[768,768]{1,0:T(8,128)(2,1)S(1)}, f32[8,768]{1,0:T(8,128)S(1)}) custom-call(bf16[768,3072]{1,0:T(8,128)(2,1)S(1)} %get-tuple-element.342.active_ref.left_ref, bf16[3072,768]{1,0:T(8,128)(2,1)S(1)} %bitcast.243, bf16[768,768]{1,0:T(8,128)(2,1)S(1)} %get-tuple-element.351.unit_ref, ...), custom_call_target="tpu_custom_call" | custom-call | flops 11000000512 | bytes 1 | tf_op jit(solution)/shard_map/down_norm/pallas_call | solution.py:314
  128.8 6.5 %down_gradient.1 = (bf16[2,768,768]{2,1,0:T(8,128)(2,1)}, bf16[2,768,768]{2,1,0:T(8,128)(2,1)S(1)}) custom-call(s32[1]{0:T(128)} %bitcast.core_ref, bf16[768,3072]{1,0:T(8,128)(2,1)S(1)} %get-tuple-element.342.active_ref.left_ref, bf16[768,768]{1,0:T(8,128)(2,1)S(1)} %get-tuple-element.353.right_ref.df_ref), custom_call_target="tpu_custom_call" | custom-call | flops 5500000256 | bytes 1 | tf_op jit(solution)/shard_map/down_gradient/pallas_call | solution.py:871
  135.3 1.5 copy-done.2
  136.9 15.7 %feed_forward_back.1 = (bf16[2,192,3072]{2,1,0:T(8,128)(2,1)}, bf16[2,192,3072]{2,1,0:T(8,128)(2,1)S(1)}, bf16[768,768]{1,0:T(8,128)(2,1)S(1)}, f32[1,3072]{1,0:T(1,128)S(1)}, f32[8,768]{1,0:T(8,128)S(1)}) custom-call(s32[1]{0:T(128)} %bitcast.core_ref, bf16[768,768]{1,0:T(8,128)(2,1)S(1)} %get-tuple-element.353.right_ref.df_ref, ...), custom_call_target="tpu_custom_call" | custom-call | flops 23100000256 | bytes 1 | tf_op jit(solution)/shard_map/feed_forward_back/pallas_call | solution.py:399
  154.8 1.4 collective-permute-start.53
  158.3 10.6 %collective-permute-start.55 = (bf16[1,2,96,768]{3,2,1,0:T(8,128)(2,1)S(1)}, bf16[1,2,96,768]{3,2,1,0:T(8,128)(2,1)S(1)}, u32[]{:S(2)}, u32[]{:S(2)}) collective-permute-start(bf16[1,2,96,768]{3,2,1,0:T(8,128)(2,1)S(1)} %get-tuple-element.453), channel_id=1, source_target_pairs={{1,3},{3,5},{5,7},{7,6},{6,4},{4,2},{2,0},{0,1},{9,8},{11,9},{13,1... | collective-permute-start | bytes 884744 | tf_op jit(solution)/shard_map/ppermute | solution.py:583
  168.9 2.0 copy-done.23
  170.9 10.3 %attention_backward.1 = (bf16[768,2304]{1,0:T(8,128)(2,1)S(1)}, f32[1,2304]{1,0:T(1,128)S(1)}) custom-call(s32[6]{0:T(128)S(1)} %pad_add_fusion.lens_ref, bf16[768,2304]{1,0:T(8,128)(2,1)S(1)} %copy-done.23, bf16[768,768]{1,0:T(8,128)(2,1)S(1)} %copy-done.20, bf16[768,768]{1,0:T(8,128)(2,1)S(1)} %copy-done.21), custom_call_target="tpu_custom_call" | custom-call | flops 12099999744 | bytes 1 | tf_op jit(solution)/shard_map/attention_backward/pallas_call | solution.py:227
  181.2 2.8 fusion.24
  187.8 5.8 %attention_gradients.1 = (bf16[2,192,3200]{2,1,0:T(8,128)(2,1)}, bf16[2,192,3200]{2,1,0:T(8,128)(2,1)S(1)}) custom-call(s32[1]{0:T(128)} %bitcast.core_ref, bf16[2,2,192,768]{3,2,1,0:T(8,128)(2,1)S(1)} %bitcast.245, bf16[2,2,192,768]{3,2,1,0:T(8,128)(2,1)S(1)} %bitcast.246, bf16[768,2304]{1,0:T(8,128)(2,1)S(1)} %get-tuple-element.379.dqkv_ref, ...), custom_call_target="tpu_custom_call" | custom-call | flops 8800000000 | bytes 1 | tf_op jit(solution)/shard_map/attention_gradients/pallas_call | solution.py:820
  194.1 1.6 collective-permute-start.60
  197.7 1.5 fusion.16
  201.3 5.3 %add_convert_fusion = bf16[768,768]{1,0:T(8,128)(2,1)S(1)} fusion(bf16[768,768]{1,0:T(8,128)(2,1)} %copy-done.19, bf16[768,2304]{1,0:T(8,128)(2,1)S(1)} %copy-done.18, bf16[768,3200]{1,0:T(8,128)(2,1)} %bitcast.238), kind=kOutput, calls=%fused_computation.4 | convolution fusion | flops 2719678464 | bytes 9437184 | tf_op jit(solution)/shard_map/dot_general | solution.py:30
  206.6 3.4 %collective-permute-done.57 = bf16[1,2,96,768]{3,2,1,0:T(8,128)(2,1)S(1)} collective-permute-done((bf16[1,2,96,768]{3,2,1,0:T(8,128)(2,1)S(1)}, bf16[1,2,96,768]{3,2,1,0:T(8,128)(2,1)S(1)}, u32[]{:S(2)}, u32[]{:S(2)}) %collective-permute-start.57) | collective-permute-done | bytes 294944 | tf_op jit(solution)/shard_map/ppermute | solution.py:586
  213.8 1.5 fusion.13
  220.0 1.6 select_reduce_fusion.1
  223.7 3.9 %collective-permute-done.62 = bf16[1,2,96,768]{3,2,1,0:T(8,128)(2,1)S(1)} collective-permute-done((bf16[1,2,96,768]{3,2,1,0:T(8,128)(2,1)S(1)}, bf16[1,2,96,768]{3,2,1,0:T(8,128)(2,1)S(1)}, u32[]{:S(2)}, u32[]{:S(2)}) %collective-permute-start.62) | collective-permute-done | bytes 294944 | tf_op jit(solution)/shard_map/ppermute | solution.py:586
  227.6 1.7 collective-permute-done.63
  229.3 2.2 collective-permute-done.66
  237.7 1.6 select_reduce_fusion
  239.4 4.0 %collective-permute-done.67 = bf16[1,2,24,3072]{3,2,1,0:T(8,128)(2,1)S(1)} collective-permute-done((bf16[1,2,24,3072]{3,2,1,0:T(8,128)(2,1)S(1)}, bf16[1,2,24,3072]{3,2,1,0:T(8,128)(2,1)S(1)}, u32[]{:S(2)}, u32[]{:S(2)}) %collective-permute-start.67) | collective-permute-done | bytes 294944 | tf_op jit(solution)/shard_map/ppermute | solution.py:586
  244.5 1.6 collective-permute-start.71
  249.0 3.5 %collective-permute-done.73 = bf16[24,3072]{1,0:T(8,128)(2,1)S(1)} collective-permute-done((bf16[24,3072]{1,0:T(8,128)(2,1)S(1)}, bf16[24,3072]{1,0:T(8,128)(2,1)S(1)}, u32[]{:S(2)}, u32[]{:S(2)}) %collective-permute-start.73) | collective-permute-done | bytes 147488 | tf_op jit(solution)/shard_map/ppermute | solution.py:590
  253.9 1.8 collective-permute-start.74
  256.9 4.2 %collective-permute-done.74 = bf16[1,2,24,3200]{3,2,1,0:T(8,128)(2,1)S(1)} collective-permute-done((bf16[1,2,24,3200]{3,2,1,0:T(8,128)(2,1)S(1)}, bf16[1,2,24,3200]{3,2,1,0:T(8,128)(2,1)S(1)}, u32[]{:S(2)}, u32[]{:S(2)}) %collective-permute-start.74) | collective-permute-done | bytes 307232 | tf_op jit(solution)/shard_map/ppermute | solution.py:586
  261.2 1.8 collective-permute-done.75
  264.6 1.8 collective-permute-start.77
  266.3 4.8 %collective-permute-done.76 = bf16[1,2,24,3200]{3,2,1,0:T(8,128)(2,1)S(1)} collective-permute-done((bf16[1,2,24,3200]{3,2,1,0:T(8,128)(2,1)S(1)}, bf16[1,2,24,3200]{3,2,1,0:T(8,128)(2,1)S(1)}, u32[]{:S(2)}, u32[]{:S(2)}) %collective-permute-start.76) | collective-permute-done | bytes 307232 | tf_op jit(solution)/shard_map/ppermute | solution.py:586
  273.8 4.3 %collective-permute-done.78 = bf16[24,3200]{1,0:T(8,128)(2,1)S(1)} collective-permute-done((bf16[24,3200]{1,0:T(8,128)(2,1)S(1)}, bf16[24,3200]{1,0:T(8,128)(2,1)S(1)}, u32[]{:S(2)}, u32[]{:S(2)}) %collective-permute-start.78) | collective-permute-done | bytes 153632 | tf_op jit(solution)/shard_map/ppermute | solution.py:590
  (271 shorter events, 66.2 us)
Async XLA Ops:
  2.6 8.0 %collective-permute-start = (bf16[24,3200]{1,0:T(8,128)(2,1)}, bf16[24,3200]{1,0:T(8,128)(2,1)S(1)}, u32[]{:S(2)}, u32[]{:S(2)}) collective-permute-start(bf16[24,3200]{1,0:T(8,128)(2,1)} %get-tuple-element.221), channel_id=1, source_target_pairs={{0,16},{16,0},{1,17},{17,1},{2,18},{18,2},{3,19},{19,3},{4,20},{20... | collective-permute-start | bytes 460808 | tf_op jit(solution)/shard_map/ppermute | solution.py:590
  6.6 9.9 %collective-permute-start.3 = (bf16[24,3072]{1,0:T(8,128)(2,1)S(1)}, bf16[24,3072]{1,0:T(8,128)(2,1)S(1)}, u32[]{:S(2)}, u32[]{:S(2)}) collective-permute-start(bf16[24,3072]{1,0:T(8,128)(2,1)S(1)} %get-tuple-element.462), channel_id=1, source_target_pairs={{0,16},{16,0},{1,17},{17,1},{2,18},{18,2},{3,19},{19,3},{4,20},{20... | collective-permute-start | bytes 442376 | tf_op jit(solution)/shard_map/ppermute | solution.py:590
  11.7 4.8 %collective-permute-start.4 = (bf16[1,2,24,3200]{3,2,1,0:T(8,128)(2,1)S(1)}, bf16[1,2,24,3200]{3,2,1,0:T(8,128)(2,1)S(1)}, u32[]{:S(2)}, u32[]{:S(2)}) collective-permute-start(bf16[1,2,24,3200]{3,2,1,0:T(8,128)(2,1)S(1)} %broadcast_select_fusion.1.refs_0_), channel_id=1, source_target_pairs={{0,8},{8,0},{1,9},{9,1},{2,10},{10,2},{3,11},{11,3},{4,12},{12,4},... | collective-permute-start | bytes 921608 | tf_op jit(solution)/shard_map/ppermute | solution.py:590
  11.7 9.3 %collective-permute-start.1 = (bf16[1,2,24,3200]{3,2,1,0:T(8,128)(2,1)S(1)}, bf16[1,2,24,3200]{3,2,1,0:T(8,128)(2,1)S(1)}, u32[]{:S(2)}, u32[]{:S(2)}) collective-permute-start(bf16[1,2,24,3200]{3,2,1,0:T(8,128)(2,1)S(1)} %broadcast_select_fusion.1.refs_0_), channel_id=1, source_target_pairs={{1,3},{3,5},{5,7},{7,6},{6,4},{4,2},{2,0},{0,1},{9,8},{11,9},{13,1... | collective-permute-start | bytes 921608 | tf_op jit(solution)/shard_map/ppermute | solution.py:583
  13.9 7.9 %collective-permute-start.2 = (bf16[1,2,24,3200]{3,2,1,0:T(8,128)(2,1)S(1)}, bf16[1,2,24,3200]{3,2,1,0:T(8,128)(2,1)S(1)}, u32[]{:S(2)}, u32[]{:S(2)}) collective-permute-start(bf16[1,2,24,3200]{3,2,1,0:T(8,128)(2,1)S(1)} %broadcast_select_fusion.1.refs_0_), channel_id=1, source_target_pairs={{1,0},{3,1},{5,3},{7,5},{6,7},{4,6},{2,4},{0,2},{9,11},{11,13},{13... | collective-permute-start | bytes 921608 | tf_op jit(solution)/shard_map/ppermute | solution.py:586
  21.8 5.2 %collective-permute-start.7 = (bf16[1,2,24,3200]{3,2,1,0:T(8,128)(2,1)S(1)}, bf16[1,2,24,3200]{3,2,1,0:T(8,128)(2,1)S(1)}, u32[]{:S(2)}, u32[]{:S(2)}) collective-permute-start(bf16[1,2,24,3200]{3,2,1,0:T(8,128)(2,1)S(1)} %collective-permute-done.1.refs_1_), channel_id=1, source_target_pairs={{0,8},{8,0},{1,9},{9,1},{2,10},{10,2},{3,11},{11,3},{4,12},{12,4},... | collective-permute-start | bytes 921608 | tf_op jit(solution)/shard_map/ppermute | solution.py:590
  21.9 8.7 %collective-permute-start.5 = (bf16[1,2,24,3200]{3,2,1,0:T(8,128)(2,1)S(1)}, bf16[1,2,24,3200]{3,2,1,0:T(8,128)(2,1)S(1)}, u32[]{:S(2)}, u32[]{:S(2)}) collective-permute-start(bf16[1,2,24,3200]{3,2,1,0:T(8,128)(2,1)S(1)} %collective-permute-done.1.refs_1_), channel_id=1, source_target_pairs={{1,3},{3,5},{5,7},{7,6},{6,4},{4,2},{2,0},{0,1},{9,8},{11,9},{13,1... | collective-permute-start | bytes 921608 | tf_op jit(solution)/shard_map/ppermute | solution.py:583
  23.8 9.7 %collective-permute-start.6 = (bf16[1,2,24,3200]{3,2,1,0:T(8,128)(2,1)S(1)}, bf16[1,2,24,3200]{3,2,1,0:T(8,128)(2,1)S(1)}, u32[]{:S(2)}, u32[]{:S(2)}) collective-permute-start(bf16[1,2,24,3200]{3,2,1,0:T(8,128)(2,1)S(1)} %collective-permute-done.2.refs_5_), channel_id=1, source_target_pairs={{1,0},{3,1},{5,3},{7,5},{6,7},{4,6},{2,4},{0,2},{9,11},{11,13},{13... | collective-permute-start | bytes 921608 | tf_op jit(solution)/shard_map/ppermute | solution.py:586
  25.4 20.0 %collective-permute-start.13 = (bf16[3,144,768]{2,1,0:T(8,128)(2,1)S(1)}, bf16[3,144,768]{2,1,0:T(8,128)(2,1)S(1)}, u32[]{:S(2)}, u32[]{:S(2)}) collective-permute-start(bf16[3,144,768]{2,1,0:T(8,128)(2,1)S(1)} %pad_maximum_fusion.4), channel_id=1, source_target_pairs={{0,16},{16,0},{1,17},{17,1},{2,18},{18,2},{3,19},{19,3},{4,20},{20... | collective-permute-start | bytes 1990664 | tf_op jit(solution)/shard_map/ppermute | solution.py:590
  27.0 10.0 %collective-permute-start.11 = (bf16[1,2,24,3072]{3,2,1,0:T(8,128)(2,1)S(1)}, bf16[1,2,24,3072]{3,2,1,0:T(8,128)(2,1)S(1)}, u32[]{:S(2)}, u32[]{:S(2)}) collective-permute-start(bf16[1,2,24,3072]{3,2,1,0:T(8,128)(2,1)S(1)} %broadcast_select_fusion.5.refs_0_), channel_id=1, source_target_pairs={{1,3},{3,5},{5,7},{7,6},{6,4},{4,2},{2,0},{0,1},{9,8},{11,9},{13,1... | collective-permute-start | bytes 884744 | tf_op jit(solution)/shard_map/ppermute | solution.py:583
  27.6 10.3 %collective-permute-start.12 = (bf16[1,2,24,3072]{3,2,1,0:T(8,128)(2,1)S(1)}, bf16[1,2,24,3072]{3,2,1,0:T(8,128)(2,1)S(1)}, u32[]{:S(2)}, u32[]{:S(2)}) collective-permute-start(bf16[1,2,24,3072]{3,2,1,0:T(8,128)(2,1)S(1)} %broadcast_select_fusion.5.refs_0_), channel_id=1, source_target_pairs={{1,0},{3,1},{5,3},{7,5},{6,7},{4,6},{2,4},{0,2},{9,11},{11,13},{13... | collective-permute-start | bytes 884744 | tf_op jit(solution)/shard_map/ppermute | solution.py:586
  30.6 7.8 %collective-permute-start.16 = (bf16[1,2,24,3072]{3,2,1,0:T(8,128)(2,1)S(1)}, bf16[1,2,24,3072]{3,2,1,0:T(8,128)(2,1)S(1)}, u32[]{:S(2)}, u32[]{:S(2)}) collective-permute-start(bf16[1,2,24,3072]{3,2,1,0:T(8,128)(2,1)S(1)} %broadcast_select_fusion.5.refs_0_), channel_id=1, source_target_pairs={{0,8},{8,0},{1,9},{9,1},{2,10},{10,2},{3,11},{11,3},{4,12},{12,4},... | collective-permute-start | bytes 884744 | tf_op jit(solution)/shard_map/ppermute | solution.py:590
  33.5 7.7 %collective-permute-start.10 = (bf16[1,2,24,3200]{3,2,1,0:T(8,128)(2,1)S(1)}, bf16[1,2,24,3200]{3,2,1,0:T(8,128)(2,1)S(1)}, u32[]{:S(2)}, u32[]{:S(2)}) collective-permute-start(bf16[1,2,24,3200]{3,2,1,0:T(8,128)(2,1)S(1)} %collective-permute-done.6.refs_6_), channel_id=1, source_target_pairs={{1,0},{3,1},{5,3},{7,5},{6,7},{4,6},{2,4},{0,2},{9,11},{11,13},{13... | collective-permute-start | bytes 921608 | tf_op jit(solution)/shard_map/ppermute | solution.py:586
  37.0 4.2 %collective-permute-start.15 = (bf16[1,2,24,3200]{3,2,1,0:T(8,128)(2,1)S(1)}, bf16[1,2,24,3200]{3,2,1,0:T(8,128)(2,1)S(1)}, u32[]{:S(2)}, u32[]{:S(2)}) collective-permute-start(bf16[1,2,24,3200]{3,2,1,0:T(8,128)(2,1)S(1)} %collective-permute-done.6.refs_6_), channel_id=1, source_target_pairs={{0,8},{8,0},{1,9},{9,1},{2,10},{10,2},{3,11},{11,3},{4,12},{12,4},... | collective-permute-start | bytes 921608 | tf_op jit(solution)/shard_map/ppermute | solution.py:590
  38.5 6.9 %collective-permute-start.9 = (bf16[1,2,24,3200]{3,2,1,0:T(8,128)(2,1)S(1)}, bf16[1,2,24,3200]{3,2,1,0:T(8,128)(2,1)S(1)}, u32[]{:S(2)}, u32[]{:S(2)}) collective-permute-start(bf16[1,2,24,3200]{3,2,1,0:T(8,128)(2,1)S(1)} %collective-permute-done.5.refs_2_), channel_id=1, source_target_pairs={{1,3},{3,5},{5,7},{7,6},{6,4},{4,2},{2,0},{0,1},{9,8},{11,9},{13,1... | collective-permute-start | bytes 921608 | tf_op jit(solution)/shard_map/ppermute | solution.py:583
  45.3 6.1 %collective-permute-start.21 = (bf16[1,2,24,3200]{3,2,1,0:T(8,128)(2,1)S(1)}, bf16[1,2,24,3200]{3,2,1,0:T(8,128)(2,1)S(1)}, u32[]{:S(2)}, u32[]{:S(2)}) collective-permute-start(bf16[1,2,24,3200]{3,2,1,0:T(8,128)(2,1)S(1)} %collective-permute-done.9.refs_3_), channel_id=1, source_target_pairs={{0,8},{8,0},{1,9},{9,1},{2,10},{10,2},{3,11},{11,3},{4,12},{12,4},... | collective-permute-start | bytes 921608 | tf_op jit(solution)/shard_map/ppermute | solution.py:590
  45.4 6.6 %collective-permute-start.22 = (bf16[1,2,24,3200]{3,2,1,0:T(8,128)(2,1)S(1)}, bf16[1,2,24,3200]{3,2,1,0:T(8,128)(2,1)S(1)}, u32[]{:S(2)}, u32[]{:S(2)}) collective-permute-start(bf16[1,2,24,3200]{3,2,1,0:T(8,128)(2,1)S(1)} %collective-permute-done.10.refs_7_), channel_id=1, source_target_pairs={{0,8},{8,0},{1,9},{9,1},{2,10},{10,2},{3,11},{11,3},{4,12},{12,4},... | collective-permute-start | bytes 921608 | tf_op jit(solution)/shard_map/ppermute | solution.py:590
  46.4 8.2 %collective-permute-start.20 = (bf16[96,768]{1,0:T(8,128)(2,1)S(1)}, bf16[96,768]{1,0:T(8,128)(2,1)S(1)}, u32[]{:S(2)}, u32[]{:S(2)}) collective-permute-start(bf16[96,768]{1,0:T(8,128)(2,1)S(1)} %get-tuple-element.460), channel_id=1, source_target_pairs={{0,16},{16,0},{1,17},{17,1},{2,18},{18,2},{3,19},{19,3},{4,20},{20... | collective-permute-start | bytes 442376 | tf_op jit(solution)/shard_map/ppermute | solution.py:590
  48.4 13.3 %collective-permute-start.17 = (bf16[1,2,24,3200]{3,2,1,0:T(8,128)(2,1)S(1)}, bf16[1,2,24,3200]{3,2,1,0:T(8,128)(2,1)}, u32[]{:S(2)}, u32[]{:S(2)}) collective-permute-start(bf16[1,2,24,3200]{3,2,1,0:T(8,128)(2,1)S(1)} %collective-permute-done.9.refs_3_), channel_id=1, source_target_pairs={{1,3},{3,5},{5,7},{7,6},{6,4},{4,2},{2,0},{0,1},{9,8},{11,9},{13,1... | collective-permute-start | bytes 921608 | tf_op jit(solution)/shard_map/ppermute | solution.py:583
  49.9 11.7 %collective-permute-start.18 = (bf16[1,2,24,3072]{3,2,1,0:T(8,128)(2,1)S(1)}, bf16[1,2,24,3072]{3,2,1,0:T(8,128)(2,1)}, u32[]{:S(2)}, u32[]{:S(2)}) collective-permute-start(bf16[1,2,24,3072]{3,2,1,0:T(8,128)(2,1)S(1)} %collective-permute-done.11.refs_1_), channel_id=1, source_target_pairs={{1,3},{3,5},{5,7},{7,6},{6,4},{4,2},{2,0},{0,1},{9,8},{11,9},{13,1... | collective-permute-start | bytes 884744 | tf_op jit(solution)/shard_map/ppermute | solution.py:583
  51.5 10.2 %collective-permute-start.19 = (bf16[1,2,24,3072]{3,2,1,0:T(8,128)(2,1)S(1)}, bf16[1,2,24,3072]{3,2,1,0:T(8,128)(2,1)}, u32[]{:S(2)}, u32[]{:S(2)}) collective-permute-start(bf16[1,2,24,3072]{3,2,1,0:T(8,128)(2,1)S(1)} %collective-permute-done.12.refs_5_), channel_id=1, source_target_pairs={{1,0},{3,1},{5,3},{7,5},{6,7},{4,6},{2,4},{0,2},{9,11},{11,13},{13... | collective-permute-start | bytes 884744 | tf_op jit(solution)/shard_map/ppermute | solution.py:586
  61.7 5.9 %collective-permute-start.33 = (bf16[1,2,24,3200]{3,2,1,0:T(8,128)(2,1)}, bf16[1,2,24,3200]{3,2,1,0:T(8,128)(2,1)}, u32[]{:S(2)}, u32[]{:S(2)}) collective-permute-start(bf16[1,2,24,3200]{3,2,1,0:T(8,128)(2,1)} %collective-permute-done.17.refs_4_), channel_id=1, source_target_pairs={{0,8},{8,0},{1,9},{9,1},{2,10},{10,2},{3,11},{11,3},{4,12},{12,4},... | collective-permute-start | bytes 921608 | tf_op jit(solution)/shard_map/ppermute | solution.py:590
  62.5 4.6 %collective-permute-start.31 = (bf16[1,2,24,3072]{3,2,1,0:T(8,128)(2,1)}, bf16[1,2,24,3072]{3,2,1,0:T(8,128)(2,1)}, u32[]{:S(2)}, u32[]{:S(2)}) collective-permute-start(bf16[1,2,24,3072]{3,2,1,0:T(8,128)(2,1)} %collective-permute-done.19.refs_6_), channel_id=1, source_target_pairs={{0,8},{8,0},{1,9},{9,1},{2,10},{10,2},{3,11},{11,3},{4,12},{12,4},... | collective-permute-start | bytes 884744 | tf_op jit(solution)/shard_map/ppermute | solution.py:590
  63.5 13.1 %collective-permute-start.27 = (bf16[1,2,96,768]{3,2,1,0:T(8,128)(2,1)S(1)}, bf16[1,2,96,768]{3,2,1,0:T(8,128)(2,1)S(1)}, u32[]{:S(2)}, u32[]{:S(2)}) collective-permute-start(bf16[1,2,96,768]{3,2,1,0:T(8,128)(2,1)S(1)} %broadcast_select_fusion.4.refs_0_), channel_id=1, source_target_pairs={{1,3},{3,5},{5,7},{7,6},{6,4},{4,2},{2,0},{0,1},{9,8},{11,9},{13,1... | collective-permute-start | bytes 884744 | tf_op jit(solution)/shard_map/ppermute | solution.py:583
  65.0 11.6 %collective-permute-start.28 = (bf16[1,2,96,768]{3,2,1,0:T(8,128)(2,1)S(1)}, bf16[1,2,96,768]{3,2,1,0:T(8,128)(2,1)S(1)}, u32[]{:S(2)}, u32[]{:S(2)}) collective-permute-start(bf16[1,2,96,768]{3,2,1,0:T(8,128)(2,1)S(1)} %broadcast_select_fusion.4.refs_0_), channel_id=1, source_target_pairs={{1,0},{3,1},{5,3},{7,5},{6,7},{4,6},{2,4},{0,2},{9,11},{11,13},{13... | collective-permute-start | bytes 884744 | tf_op jit(solution)/shard_map/ppermute | solution.py:586
  65.5 13.8 %collective-permute-start.25 = (bf16[1,2,24,3072]{3,2,1,0:T(8,128)(2,1)}, bf16[1,2,24,3072]{3,2,1,0:T(8,128)(2,1)S(1)}, u32[]{:S(2)}, u32[]{:S(2)}) collective-permute-start(bf16[1,2,24,3072]{3,2,1,0:T(8,128)(2,1)} %collective-permute-done.18.refs_2_), channel_id=1, source_target_pairs={{1,3},{3,5},{5,7},{7,6},{6,4},{4,2},{2,0},{0,1},{9,8},{11,9},{13,1... | collective-permute-start | bytes 884744 | tf_op jit(solution)/shard_map/ppermute | solution.py:583
  67.1 12.3 %collective-permute-start.26 = (bf16[1,2,24,3072]{3,2,1,0:T(8,128)(2,1)}, bf16[1,2,24,3072]{3,2,1,0:T(8,128)(2,1)S(1)}, u32[]{:S(2)}, u32[]{:S(2)}) collective-permute-start(bf16[1,2,24,3072]{3,2,1,0:T(8,128)(2,1)} %collective-permute-done.19.refs_6_), channel_id=1, source_target_pairs={{1,0},{3,1},{5,3},{7,5},{6,7},{4,6},{2,4},{0,2},{9,11},{11,13},{13... | collective-permute-start | bytes 884744 | tf_op jit(solution)/shard_map/ppermute | solution.py:586
  67.5 14.6 %collective-permute-start.29 = (bf16[3,128,768]{2,1,0:T(8,128)(2,1)}, bf16[3,128,768]{2,1,0:T(8,128)(2,1)S(1)}, u32[]{:S(2)}, u32[]{:S(2)}) collective-permute-start(bf16[3,128,768]{2,1,0:T(8,128)(2,1)} %select_reduce_fusion.3), channel_id=1, source_target_pairs={{0,16},{16,0},{1,17},{17,1},{2,18},{18,2},{3,19},{19,3},{4,20},{20... | collective-permute-start | bytes 1769480 | tf_op jit(solution)/shard_map/ppermute | solution.py:590
  82.1 4.1 %collective-permute-start.38 = (bf16[1,2,24,3072]{3,2,1,0:T(8,128)(2,1)S(1)}, bf16[1,2,24,3072]{3,2,1,0:T(8,128)(2,1)S(1)}, u32[]{:S(2)}, u32[]{:S(2)}) collective-permute-start(bf16[1,2,24,3072]{3,2,1,0:T(8,128)(2,1)S(1)} %collective-permute-done.26.refs_7_), channel_id=1, source_target_pairs={{0,8},{8,0},{1,9},{9,1},{2,10},{10,2},{3,11},{11,3},{4,12},{12,4},... | collective-permute-start | bytes 884744 | tf_op jit(solution)/shard_map/ppermute | solution.py:590
  83.5 15.0 %collective-permute-start.34 = (bf16[1,2,24,3072]{3,2,1,0:T(8,128)(2,1)S(1)}, bf16[1,2,24,3072]{3,2,1,0:T(8,128)(2,1)S(1)}, u32[]{:S(2)}, u32[]{:S(2)}) collective-permute-start(bf16[1,2,24,3072]{3,2,1,0:T(8,128)(2,1)S(1)} %collective-permute-done.25.refs_3_), channel_id=1, source_target_pairs={{1,3},{3,5},{5,7},{7,6},{6,4},{4,2},{2,0},{0,1},{9,8},{11,9},{13,1... | collective-permute-start | bytes 884744 | tf_op jit(solution)/shard_map/ppermute | solution.py:583
  84.8 13.7 %collective-permute-start.35 = (bf16[1,2,96,768]{3,2,1,0:T(8,128)(2,1)S(1)}, bf16[1,2,96,768]{3,2,1,0:T(8,128)(2,1)S(1)}, u32[]{:S(2)}, u32[]{:S(2)}) collective-permute-start(bf16[1,2,96,768]{3,2,1,0:T(8,128)(2,1)S(1)} %collective-permute-done.27.refs_1_), channel_id=1, source_target_pairs={{1,3},{3,5},{5,7},{7,6},{6,4},{4,2},{2,0},{0,1},{9,8},{11,9},{13,1... | collective-permute-start | bytes 884744 | tf_op jit(solution)/shard_map/ppermute | solution.py:583
  86.2 12.3 %collective-permute-start.36 = (bf16[1,2,96,768]{3,2,1,0:T(8,128)(2,1)S(1)}, bf16[1,2,96,768]{3,2,1,0:T(8,128)(2,1)S(1)}, u32[]{:S(2)}, u32[]{:S(2)}) collective-permute-start(bf16[1,2,96,768]{3,2,1,0:T(8,128)(2,1)S(1)} %collective-permute-done.28.refs_5_), channel_id=1, source_target_pairs={{1,0},{3,1},{5,3},{7,5},{6,7},{4,6},{2,4},{0,2},{9,11},{11,13},{13... | collective-permute-start | bytes 884744 | tf_op jit(solution)/shard_map/ppermute | solution.py:586
  99.2 9.7 %collective-permute-start.41 = (bf16[1,2,96,768]{3,2,1,0:T(8,128)(2,1)S(1)}, bf16[1,2,96,768]{3,2,1,0:T(8,128)(2,1)S(1)}, u32[]{:S(2)}, u32[]{:S(2)}) collective-permute-start(bf16[1,2,96,768]{3,2,1,0:T(8,128)(2,1)S(1)} %collective-permute-done.35.refs_2_), channel_id=1, source_target_pairs={{1,3},{3,5},{5,7},{7,6},{6,4},{4,2},{2,0},{0,1},{9,8},{11,9},{13,1... | collective-permute-start | bytes 884744 | tf_op jit(solution)/shard_map/ppermute | solution.py:583
  100.6 8.3 %collective-permute-start.42 = (bf16[1,2,96,768]{3,2,1,0:T(8,128)(2,1)S(1)}, bf16[1,2,96,768]{3,2,1,0:T(8,128)(2,1)S(1)}, u32[]{:S(2)}, u32[]{:S(2)}) collective-permute-start(bf16[1,2,96,768]{3,2,1,0:T(8,128)(2,1)S(1)} %collective-permute-done.36.refs_6_), channel_id=1, source_target_pairs={{1,0},{3,1},{5,3},{7,5},{6,7},{4,6},{2,4},{0,2},{9,11},{11,13},{13... | collective-permute-start | bytes 884744 | tf_op jit(solution)/shard_map/ppermute | solution.py:586
  109.5 9.1 %collective-permute-start.46 = (bf16[1,2,96,768]{3,2,1,0:T(8,128)(2,1)S(1)}, bf16[1,2,96,768]{3,2,1,0:T(8,128)(2,1)S(1)}, u32[]{:S(2)}, u32[]{:S(2)}) collective-permute-start(bf16[1,2,96,768]{3,2,1,0:T(8,128)(2,1)S(1)} %collective-permute-done.41.refs_3_), channel_id=1, source_target_pairs={{1,3},{3,5},{5,7},{7,6},{6,4},{4,2},{2,0},{0,1},{9,8},{11,9},{13,1... | collective-permute-start | bytes 884744 | tf_op jit(solution)/shard_map/ppermute | solution.py:583
  136.8 17.9 %collective-permute-start.50 = (bf16[2,768,768]{2,1,0:T(8,128)(2,1)}, bf16[2,768,768]{2,1,0:T(8,128)(2,1)}, u32[]{:S(2)}, u32[]{:S(2)}) collective-permute-start(bf16[2,768,768]{2,1,0:T(8,128)(2,1)} %get-tuple-element.355), channel_id=1, source_target_pairs={{0,8},{8,0},{1,9},{9,1},{2,10},{10,2},{3,11},{11,3},{4,12},{12,4},... | collective-permute-start | bytes 7077896 | tf_op jit(solution)/shard_map/ppermute | solution.py:590
  154.3 26.9 %collective-permute-start.52 = (bf16[2,192,3072]{2,1,0:T(8,128)(2,1)}, bf16[2,192,3072]{2,1,0:T(8,128)(2,1)}, u32[]{:S(2)}, u32[]{:S(2)}) collective-permute-start(bf16[2,192,3072]{2,1,0:T(8,128)(2,1)} %get-tuple-element.363), channel_id=1, source_target_pairs={{0,8},{8,0},{1,9},{9,1},{2,10},{10,2},{3,11},{11,3},{4,12},{12,4},... | collective-permute-start | bytes 7077896 | tf_op jit(solution)/shard_map/ppermute | solution.py:590
  154.8 26.5 %collective-permute-start.53 = (bf16[3,128,768]{2,1,0:T(8,128)(2,1)S(1)}, bf16[3,128,768]{2,1,0:T(8,128)(2,1)S(1)}, u32[]{:S(2)}, u32[]{:S(2)}) collective-permute-start(bf16[3,128,768]{2,1,0:T(8,128)(2,1)S(1)} %bitcast.256), channel_id=1, source_target_pairs={{0,16},{16,0},{1,17},{17,1},{2,18},{18,2},{3,19},{19,3},{4,20},{20... | collective-permute-start | bytes 1769480 | tf_op jit(solution)/shard_map/ppermute | solution.py:590
  157.5 23.7 %collective-permute-start.51 = (bf16[1,2,96,768]{3,2,1,0:T(8,128)(2,1)S(1)}, bf16[1,2,96,768]{3,2,1,0:T(8,128)(2,1)S(1)}, u32[]{:S(2)}, u32[]{:S(2)}) collective-permute-start(bf16[1,2,96,768]{3,2,1,0:T(8,128)(2,1)S(1)} %get-tuple-element.454), channel_id=1, source_target_pairs={{1,0},{3,1},{5,3},{7,5},{6,7},{4,6},{2,4},{0,2},{9,11},{11,13},{13... | collective-permute-start | bytes 884744 | tf_op jit(solution)/shard_map/ppermute | solution.py:586
  158.3 35.3 %collective-permute-start.55 = (bf16[1,2,96,768]{3,2,1,0:T(8,128)(2,1)S(1)}, bf16[1,2,96,768]{3,2,1,0:T(8,128)(2,1)S(1)}, u32[]{:S(2)}, u32[]{:S(2)}) collective-permute-start(bf16[1,2,96,768]{3,2,1,0:T(8,128)(2,1)S(1)} %get-tuple-element.453), channel_id=1, source_target_pairs={{1,3},{3,5},{5,7},{7,6},{6,4},{4,2},{2,0},{0,1},{9,8},{11,9},{13,1... | collective-permute-start | bytes 884744 | tf_op jit(solution)/shard_map/ppermute | solution.py:583
  184.0 9.6 %collective-permute-start.56 = (bf16[1,2,24,3072]{3,2,1,0:T(8,128)(2,1)S(1)}, bf16[1,2,24,3072]{3,2,1,0:T(8,128)(2,1)}, u32[]{:S(2)}, u32[]{:S(2)}) collective-permute-start(bf16[1,2,24,3072]{3,2,1,0:T(8,128)(2,1)S(1)} %get-tuple-element.450), channel_id=1, source_target_pairs={{1,0},{3,1},{5,3},{7,5},{6,7},{4,6},{2,4},{0,2},{9,11},{11,13},{13... | collective-permute-start | bytes 884744 | tf_op jit(solution)/shard_map/ppermute | solution.py:586
  185.9 8.1 %collective-permute-start.54 = (bf16[1,2,96,768]{3,2,1,0:T(8,128)(2,1)S(1)}, bf16[1,2,96,768]{3,2,1,0:T(8,128)(2,1)}, u32[]{:S(2)}, u32[]{:S(2)}) collective-permute-start(bf16[1,2,96,768]{3,2,1,0:T(8,128)(2,1)S(1)} %fusion.18), channel_id=1, source_target_pairs={{1,0},{3,1},{5,3},{7,5},{6,7},{4,6},{2,4},{0,2},{9,11},{11,13},{13... | collective-permute-start | bytes 884744 | tf_op jit(solution)/shard_map/ppermute | solution.py:586
  194.0 16.4 %collective-permute-start.61 = (bf16[2,192,3200]{2,1,0:T(8,128)(2,1)}, bf16[2,192,3200]{2,1,0:T(8,128)(2,1)}, u32[]{:S(2)}, u32[]{:S(2)}) collective-permute-start(bf16[2,192,3200]{2,1,0:T(8,128)(2,1)} %get-tuple-element.388), channel_id=1, source_target_pairs={{0,8},{8,0},{1,9},{9,1},{2,10},{10,2},{3,11},{11,3},{4,12},{12,4},... | collective-permute-start | bytes 7372808 | tf_op jit(solution)/shard_map/ppermute | solution.py:590
  194.1 12.5 %collective-permute-start.60 = (bf16[1,2,24,3072]{3,2,1,0:T(8,128)(2,1)}, bf16[1,2,24,3072]{3,2,1,0:T(8,128)(2,1)S(1)}, u32[]{:S(2)}, u32[]{:S(2)}) collective-permute-start(bf16[1,2,24,3072]{3,2,1,0:T(8,128)(2,1)} %get-tuple-element.449), channel_id=1, source_target_pairs={{1,3},{3,5},{5,7},{7,6},{6,4},{4,2},{2,0},{0,1},{9,8},{11,9},{13,1... | collective-permute-start | bytes 884744 | tf_op jit(solution)/shard_map/ppermute | solution.py:583
  197.0 9.6 %collective-permute-start.59 = (bf16[1,2,24,3072]{3,2,1,0:T(8,128)(2,1)S(1)}, bf16[1,2,24,3072]{3,2,1,0:T(8,128)(2,1)S(1)}, u32[]{:S(2)}, u32[]{:S(2)}) collective-permute-start(bf16[1,2,24,3072]{3,2,1,0:T(8,128)(2,1)S(1)} %fusion.15), channel_id=1, source_target_pairs={{1,0},{3,1},{5,3},{7,5},{6,7},{4,6},{2,4},{0,2},{9,11},{11,13},{13... | collective-permute-start | bytes 884744 | tf_op jit(solution)/shard_map/ppermute | solution.py:586
  199.2 10.9 %collective-permute-start.57 = (bf16[1,2,96,768]{3,2,1,0:T(8,128)(2,1)S(1)}, bf16[1,2,96,768]{3,2,1,0:T(8,128)(2,1)S(1)}, u32[]{:S(2)}, u32[]{:S(2)}) collective-permute-start(bf16[1,2,96,768]{3,2,1,0:T(8,128)(2,1)S(1)} %get-tuple-element.452), channel_id=1, source_target_pairs={{1,0},{3,1},{5,3},{7,5},{6,7},{4,6},{2,4},{0,2},{9,11},{11,13},{13... | collective-permute-start | bytes 884744 | tf_op jit(solution)/shard_map/ppermute | solution.py:586
  200.5 9.9 %collective-permute-start.58 = (bf16[1,2,96,768]{3,2,1,0:T(8,128)(2,1)S(1)}, bf16[1,2,96,768]{3,2,1,0:T(8,128)(2,1)S(1)}, u32[]{:S(2)}, u32[]{:S(2)}) collective-permute-start(bf16[1,2,96,768]{3,2,1,0:T(8,128)(2,1)S(1)} %get-tuple-element.451), channel_id=1, source_target_pairs={{1,3},{3,5},{5,7},{7,6},{6,4},{4,2},{2,0},{0,1},{9,8},{11,9},{13,1... | collective-permute-start | bytes 884744 | tf_op jit(solution)/shard_map/ppermute | solution.py:583
  211.7 9.9 %collective-permute-start.64 = (bf16[1,2,24,3072]{3,2,1,0:T(8,128)(2,1)S(1)}, bf16[1,2,24,3072]{3,2,1,0:T(8,128)(2,1)S(1)}, u32[]{:S(2)}, u32[]{:S(2)}) collective-permute-start(bf16[1,2,24,3072]{3,2,1,0:T(8,128)(2,1)S(1)} %get-tuple-element.446), channel_id=1, source_target_pairs={{1,0},{3,1},{5,3},{7,5},{6,7},{4,6},{2,4},{0,2},{9,11},{11,13},{13... | collective-permute-start | bytes 884744 | tf_op jit(solution)/shard_map/ppermute | solution.py:586
  213.1 9.9 %collective-permute-start.65 = (bf16[1,2,24,3072]{3,2,1,0:T(8,128)(2,1)S(1)}, bf16[1,2,24,3072]{3,2,1,0:T(8,128)(2,1)S(1)}, u32[]{:S(2)}, u32[]{:S(2)}) collective-permute-start(bf16[1,2,24,3072]{3,2,1,0:T(8,128)(2,1)S(1)} %get-tuple-element.445), channel_id=1, source_target_pairs={{1,3},{3,5},{5,7},{7,6},{6,4},{4,2},{2,0},{0,1},{9,8},{11,9},{13,1... | collective-permute-start | bytes 884744 | tf_op jit(solution)/shard_map/ppermute | solution.py:583
  215.2 12.4 %collective-permute-start.62 = (bf16[1,2,96,768]{3,2,1,0:T(8,128)(2,1)S(1)}, bf16[1,2,96,768]{3,2,1,0:T(8,128)(2,1)S(1)}, u32[]{:S(2)}, u32[]{:S(2)}) collective-permute-start(bf16[1,2,96,768]{3,2,1,0:T(8,128)(2,1)S(1)} %get-tuple-element.448), channel_id=1, source_target_pairs={{1,0},{3,1},{5,3},{7,5},{6,7},{4,6},{2,4},{0,2},{9,11},{11,13},{13... | collective-permute-start | bytes 884744 | tf_op jit(solution)/shard_map/ppermute | solution.py:586
  216.6 12.7 %collective-permute-start.63 = (bf16[1,2,96,768]{3,2,1,0:T(8,128)(2,1)S(1)}, bf16[1,2,96,768]{3,2,1,0:T(8,128)(2,1)S(1)}, u32[]{:S(2)}, u32[]{:S(2)}) collective-permute-start(bf16[1,2,96,768]{3,2,1,0:T(8,128)(2,1)S(1)} %get-tuple-element.447), channel_id=1, source_target_pairs={{1,3},{3,5},{5,7},{7,6},{6,4},{4,2},{2,0},{0,1},{9,8},{11,9},{13,1... | collective-permute-start | bytes 884744 | tf_op jit(solution)/shard_map/ppermute | solution.py:583
  217.3 14.2 %collective-permute-start.66 = (bf16[3,128,768]{2,1,0:T(8,128)(2,1)S(1)}, bf16[3,128,768]{2,1,0:T(8,128)(2,1)S(1)}, u32[]{:S(2)}, u32[]{:S(2)}) collective-permute-start(bf16[3,128,768]{2,1,0:T(8,128)(2,1)S(1)} %bitcast.255), channel_id=1, source_target_pairs={{0,16},{16,0},{1,17},{17,1},{2,18},{18,2},{3,19},{19,3},{4,20},{20... | collective-permute-start | bytes 1769480 | tf_op jit(solution)/shard_map/ppermute | solution.py:590
  221.6 17.7 %collective-permute-start.69 = (bf16[1,2,24,3200]{3,2,1,0:T(8,128)(2,1)S(1)}, bf16[1,2,24,3200]{3,2,1,0:T(8,128)(2,1)S(1)}, u32[]{:S(2)}, u32[]{:S(2)}) collective-permute-start(bf16[1,2,24,3200]{3,2,1,0:T(8,128)(2,1)S(1)} %get-tuple-element.442), channel_id=1, source_target_pairs={{1,0},{3,1},{5,3},{7,5},{6,7},{4,6},{2,4},{0,2},{9,11},{11,13},{13... | collective-permute-start | bytes 921608 | tf_op jit(solution)/shard_map/ppermute | solution.py:586
  223.0 26.0 %collective-permute-start.72 = (bf16[1,2,24,3200]{3,2,1,0:T(8,128)(2,1)S(1)}, bf16[1,2,24,3200]{3,2,1,0:T(8,128)(2,1)S(1)}, u32[]{:S(2)}, u32[]{:S(2)}) collective-permute-start(bf16[1,2,24,3200]{3,2,1,0:T(8,128)(2,1)S(1)} %get-tuple-element.441), channel_id=1, source_target_pairs={{1,3},{3,5},{5,7},{7,6},{6,4},{4,2},{2,0},{0,1},{9,8},{11,9},{13,1... | collective-permute-start | bytes 921608 | tf_op jit(solution)/shard_map/ppermute | solution.py:583
  232.8 6.5 %collective-permute-start.70 = (bf16[96,768]{1,0:T(8,128)(2,1)S(1)}, bf16[96,768]{1,0:T(8,128)(2,1)S(1)}, u32[]{:S(2)}, u32[]{:S(2)}) collective-permute-start(bf16[96,768]{1,0:T(8,128)(2,1)S(1)} %fusion.26), channel_id=1, source_target_pairs={{0,16},{16,0},{1,17},{17,1},{2,18},{18,2},{3,19},{19,3},{4,20},{20... | collective-permute-start | bytes 442376 | tf_op jit(solution)/shard_map/ppermute | solution.py:590
  235.4 7.9 %collective-permute-start.67 = (bf16[1,2,24,3072]{3,2,1,0:T(8,128)(2,1)S(1)}, bf16[1,2,24,3072]{3,2,1,0:T(8,128)(2,1)S(1)}, u32[]{:S(2)}, u32[]{:S(2)}) collective-permute-start(bf16[1,2,24,3072]{3,2,1,0:T(8,128)(2,1)S(1)} %get-tuple-element.444), channel_id=1, source_target_pairs={{1,0},{3,1},{5,3},{7,5},{6,7},{4,6},{2,4},{0,2},{9,11},{11,13},{13... | collective-permute-start | bytes 884744 | tf_op jit(solution)/shard_map/ppermute | solution.py:586
  236.7 6.8 %collective-permute-start.68 = (bf16[1,2,24,3072]{3,2,1,0:T(8,128)(2,1)S(1)}, bf16[1,2,24,3072]{3,2,1,0:T(8,128)(2,1)S(1)}, u32[]{:S(2)}, u32[]{:S(2)}) collective-permute-start(bf16[1,2,24,3072]{3,2,1,0:T(8,128)(2,1)S(1)} %get-tuple-element.443), channel_id=1, source_target_pairs={{1,3},{3,5},{5,7},{7,6},{6,4},{4,2},{2,0},{0,1},{9,8},{11,9},{13,1... | collective-permute-start | bytes 884744 | tf_op jit(solution)/shard_map/ppermute | solution.py:583
  244.5 8.0 %collective-permute-start.71 = (bf16[1,2,24,3200]{3,2,1,0:T(8,128)(2,1)S(1)}, bf16[1,2,24,3200]{3,2,1,0:T(8,128)(2,1)S(1)}, u32[]{:S(2)}, u32[]{:S(2)}) collective-permute-start(bf16[1,2,24,3200]{3,2,1,0:T(8,128)(2,1)S(1)} %fusion.8), channel_id=1, source_target_pairs={{1,0},{3,1},{5,3},{7,5},{6,7},{4,6},{2,4},{0,2},{9,11},{11,13},{13... | collective-permute-start | bytes 921608 | tf_op jit(solution)/shard_map/ppermute | solution.py:586
  247.4 5.2 %collective-permute-start.73 = (bf16[24,3072]{1,0:T(8,128)(2,1)S(1)}, bf16[24,3072]{1,0:T(8,128)(2,1)S(1)}, u32[]{:S(2)}, u32[]{:S(2)}) collective-permute-start(bf16[24,3072]{1,0:T(8,128)(2,1)S(1)} %fusion.27), channel_id=1, source_target_pairs={{0,16},{16,0},{1,17},{17,1},{2,18},{18,2},{3,19},{19,3},{4,20},{20... | collective-permute-start | bytes 442376 | tf_op jit(solution)/shard_map/ppermute | solution.py:590
  253.9 7.2 %collective-permute-start.74 = (bf16[1,2,24,3200]{3,2,1,0:T(8,128)(2,1)S(1)}, bf16[1,2,24,3200]{3,2,1,0:T(8,128)(2,1)S(1)}, u32[]{:S(2)}, u32[]{:S(2)}) collective-permute-start(bf16[1,2,24,3200]{3,2,1,0:T(8,128)(2,1)S(1)} %get-tuple-element.440), channel_id=1, source_target_pairs={{1,0},{3,1},{5,3},{7,5},{6,7},{4,6},{2,4},{0,2},{9,11},{11,13},{13... | collective-permute-start | bytes 921608 | tf_op jit(solution)/shard_map/ppermute | solution.py:586
  255.7 7.2 %collective-permute-start.75 = (bf16[1,2,24,3200]{3,2,1,0:T(8,128)(2,1)S(1)}, bf16[1,2,24,3200]{3,2,1,0:T(8,128)(2,1)S(1)}, u32[]{:S(2)}, u32[]{:S(2)}) collective-permute-start(bf16[1,2,24,3200]{3,2,1,0:T(8,128)(2,1)S(1)} %get-tuple-element.439), channel_id=1, source_target_pairs={{1,3},{3,5},{5,7},{7,6},{6,4},{4,2},{2,0},{0,1},{9,8},{11,9},{13,1... | collective-permute-start | bytes 921608 | tf_op jit(solution)/shard_map/ppermute | solution.py:583
  264.2 6.9 %collective-permute-start.76 = (bf16[1,2,24,3200]{3,2,1,0:T(8,128)(2,1)S(1)}, bf16[1,2,24,3200]{3,2,1,0:T(8,128)(2,1)S(1)}, u32[]{:S(2)}, u32[]{:S(2)}) collective-permute-start(bf16[1,2,24,3200]{3,2,1,0:T(8,128)(2,1)S(1)} %get-tuple-element.438), channel_id=1, source_target_pairs={{1,0},{3,1},{5,3},{7,5},{6,7},{4,6},{2,4},{0,2},{9,11},{11,13},{13... | collective-permute-start | bytes 921608 | tf_op jit(solution)/shard_map/ppermute | solution.py:586
  264.6 7.0 %collective-permute-start.77 = (bf16[1,2,24,3200]{3,2,1,0:T(8,128)(2,1)S(1)}, bf16[1,2,24,3200]{3,2,1,0:T(8,128)(2,1)S(1)}, u32[]{:S(2)}, u32[]{:S(2)}) collective-permute-start(bf16[1,2,24,3200]{3,2,1,0:T(8,128)(2,1)S(1)} %get-tuple-element.437), channel_id=1, source_target_pairs={{1,3},{3,5},{5,7},{7,6},{6,4},{4,2},{2,0},{0,1},{9,8},{11,9},{13,1... | collective-permute-start | bytes 921608 | tf_op jit(solution)/shard_map/ppermute | solution.py:583
  272.8 5.3 %collective-permute-start.78 = (bf16[24,3200]{1,0:T(8,128)(2,1)S(1)}, bf16[24,3200]{1,0:T(8,128)(2,1)S(1)}, u32[]{:S(2)}, u32[]{:S(2)}) collective-permute-start(bf16[24,3200]{1,0:T(8,128)(2,1)S(1)} %fusion.25), channel_id=1, source_target_pairs={{0,16},{16,0},{1,17},{17,1},{2,18},{18,2},{3,19},{19,3},{4,20},{20... | collective-permute-start | bytes 460808 | tf_op jit(solution)/shard_map/ppermute | solution.py:590
  (65 other events, 793.1 us)

commit v2 on v1

--- a/solution.py
+++ b/solution.py
@@ -1067,10 +1067,10 @@
         _, values, back = tie(now, result, trip_result.got)
         return home(values, back)
 
-    output = slot([ring_d, ring_u, trip_rows], outputs)
+    ring_a = scatter(own_a, trip.got)
+    output = slot([ring_d, ring_u, ring_a, trip_rows], outputs)
     for _ in range(ring.long - 4):
-        slot([ring_d, ring_u])
-    ring_a = scatter(own_a, trip.got)
+        slot([ring_d, ring_u, ring_a])
     owners_d = Owners(ring_d.total, side, groups)
 
     def input_grads(now):
@@ -1081,8 +1081,6 @@
     owners_u = Owners(ring_u.total, side, groups)
     grads_d = slot([ring_a, owners_u.trip], lambda now: owners_d.by_model())
     grads_u = slot([ring_a], lambda now: owners_u.by_model())
-    for _ in range(ring.long - 3):
-        slot([ring_a])
 
     owners_a = Owners(ring_a.total, side, groups)
     slot([owners_a.trip])

time: 286 us -> 284 us (level)
  transfers between devices with their start and end apart: 79 -> 79, of which waited for: 29 -> 26; matrix products, arithmetic and copies ran while one was open for 13% -> 13% of each run, Pallas kernels for 21% -> 21%
where the time goes in v2:
time: 284 us; the launch traced here: 279 us
  starting transfers between devices  78.7 us (28%)
  Pallas kernels  76 us (27%)
  waiting for transfers between devices  70.5 us (25%)
  other arithmetic  33.8 us (12%)
  local copies, waits for them, and re-layouts  13.3 us (5%)
  matrix products  5.27 us (2%)
    ppermute x21, starting transfers between devices, forth(): return lax.ppermute(block, ('core', 'f'), self.ahead)  38.3 us
    ppermute x21, waiting for transfers between devices, forth(): return lax.ppermute(block, ('core', 'f'), self.ahead)  30 us
    ppermute x21, waiting for transfers between devices, back(): return lax.ppermute(block, ('core', 'f'), self.behind)  25.5 us
    ppermute x21, starting transfers between devices, back(): return lax.ppermute(block, ('core', 'f'), self.behind)  20.9 us
    ppermute x37, starting transfers between devices, swap(): return lax.ppermute(value, axis, SWAP)  19.5 us
    pallas_call x1, Pallas kernels, feed_back(): pl.pallas_call(back_kernel, out_shape=[jax.ShapeDtypeStruct((parts, run,...  15.7 us
    ppermute x37, waiting for transfers between devices, swap(): return lax.ppermute(value, axis, SWAP)  15.1 us
    pallas_call x3, Pallas kernels, assemble(): pl.pallas_call(functools.partial(assemble_kernel, ring, with_vectors), ou...  11.3 us
  transfers between devices with their start and end apart: 79, of which 26 were waited for; matrix products, arithmetic and copies ran while one was open for 13% of the time, Pallas kernels for 21%

profile of v2, /device:TPU:0, one launch (start us, length us, event | category | flops | bytes accessed | tf_op | source)
XLA Modules:
  0.0 279.4 jit_solution(6799357374137994599)
XLA Ops:
  0.7 1.9 pack_shard.1
  2.6 2.9 %collective-permute-start = (bf16[24,3200]{1,0:T(8,128)(2,1)}, bf16[24,3200]{1,0:T(8,128)(2,1)S(1)}, u32[]{:S(2)}, u32[]{:S(2)}) collective-permute-start(bf16[24,3200]{1,0:T(8,128)(2,1)} %get-tuple-element.221), channel_id=1, source_target_pairs={{0,16},{16,0},{1,17},{17,1},{2,18},{18,2},{3,19},{19,3},{4,20},{20... | collective-permute-start | bytes 460808 | tf_op jit(solution)/shard_map/ppermute | solution.py:590
  8.2 2.3 collective-permute-done
  11.7 2.1 collective-permute-start.1
  14.0 2.3 select_reduce_fusion.4
  16.5 4.6 %collective-permute-done.1.refs_1_ = bf16[1,2,24,3200]{3,2,1,0:T(8,128)(2,1)S(1)} collective-permute-done((bf16[1,2,24,3200]{3,2,1,0:T(8,128)(2,1)S(1)}, bf16[1,2,24,3200]{3,2,1,0:T(8,128)(2,1)S(1)}, u32[]{:S(2)}, u32[]{:S(2)}) %collective-permute-start.1) | collective-permute-done | bytes 307232 | tf_op jit(solution)/shard_map/ppermute | solution.py:583
  21.9 1.8 collective-permute-start.5
  23.8 1.6 collective-permute-start.6
  25.4 1.5 collective-permute-start.13
  27.6 1.5 collective-permute-start.12
  29.1 1.6 collective-permute-done.5.refs_2_
  30.6 2.8 %collective-permute-done.6.refs_6_ = bf16[1,2,24,3200]{3,2,1,0:T(8,128)(2,1)S(1)} collective-permute-done((bf16[1,2,24,3200]{3,2,1,0:T(8,128)(2,1)S(1)}, bf16[1,2,24,3200]{3,2,1,0:T(8,128)(2,1)S(1)}, u32[]{:S(2)}, u32[]{:S(2)}) %collective-permute-start.6) | collective-permute-done | bytes 307232 | tf_op jit(solution)/shard_map/ppermute | solution.py:586
  33.5 2.1 collective-permute-start.10
  35.6 1.4 collective-permute-done.11.refs_1_
  38.5 1.8 collective-permute-start.9
  41.2 4.1 %collective-permute-done.9.refs_3_ = bf16[1,2,24,3200]{3,2,1,0:T(8,128)(2,1)S(1)} collective-permute-done((bf16[1,2,24,3200]{3,2,1,0:T(8,128)(2,1)S(1)}, bf16[1,2,24,3200]{3,2,1,0:T(8,128)(2,1)S(1)}, u32[]{:S(2)}, u32[]{:S(2)}) %collective-permute-start.9) | collective-permute-done | bytes 307232 | tf_op jit(solution)/shard_map/ppermute | solution.py:583
  46.4 2.0 collective-permute-start.20
  48.4 1.5 collective-permute-start.17
  49.9 1.5 collective-permute-start.18
  54.6 7.1 %collective-permute-done.18.refs_2_ = bf16[1,2,24,3072]{3,2,1,0:T(8,128)(2,1)} collective-permute-done((bf16[1,2,24,3072]{3,2,1,0:T(8,128)(2,1)S(1)}, bf16[1,2,24,3072]{3,2,1,0:T(8,128)(2,1)}, u32[]{:S(2)}, u32[]{:S(2)}) %collective-permute-start.18) | collective-permute-done | bytes 294944 | tf_op jit(solution)/shard_map/ppermute | solution.py:583
  63.5 1.5 collective-permute-start.27
  65.5 1.5 collective-permute-start.25
  68.9 6.3 %assemble.3 = (bf16[1,2,2,8,24,3200]{5,4,3,2,1,0:T(8,128)(2,1)}, f32[16,768]{1,0:T(8,128)}, bf16[768,768]{1,0:T(8,128)(2,1)}) custom-call(s32[2]{0:T(128)} %pad_add_fusion.1.at_ref, bf16[1,2,24,3200]{3,2,1,0:T(8,128)(2,1)} %copy-done.29, bf16[1,2,24,3200]{3,2,1,0:T(8,128)(2,1)} %copy-done.38, bf16[1,2,24,3200]{3,2,1,0:T(8,128)(2,1)} %copy-done.41, ...), custom_call_target="tpu_custom_call" | custom-call | flops 4400000000 | bytes 1 | tf_op jit(solution)/shard_map/assemble/pallas_call | solution.py:758
  76.6 2.8 collective-permute-done.25.refs_3_
  79.4 2.8 collective-permute-done.29
  84.8 1.4 collective-permute-start.35
  86.9 9.8 %attention_forward.1 = (bf16[768,2304]{1,0:T(8,128)(2,1)S(1)}, bf16[768,768]{1,0:T(8,128)(2,1)S(1)}, f32[768,1]{1,0:T(8,128)S(1)}, bf16[768,768]{1,0:T(8,128)(2,...) custom-call(s32[6]{0:T(128)S(1)} %pad_add_fusion.lens_ref, bf16[768,768]{1,0:T(8,128)(2,1)S(1)} %bitcast.235, ...), custom_call_target="tpu_custom_call" | custom-call | flops 15399999488 | bytes 1 | tf_op jit(solution)/shard_map/attention_forward/pallas_call | solution.py:159
  96.7 1.8 copy-done.22
  99.2 1.4 collective-permute-start.41
  101.9 2.6 assemble.4
  104.5 4.4 %collective-permute-done.41.refs_3_ = bf16[1,2,96,768]{3,2,1,0:T(8,128)(2,1)S(1)} collective-permute-done((bf16[1,2,96,768]{3,2,1,0:T(8,128)(2,1)S(1)}, bf16[1,2,96,768]{3,2,1,0:T(8,128)(2,1)S(1)}, u32[]{:S(2)}, u32[]{:S(2)}) %collective-permute-start.41) | collective-permute-done | bytes 294944 | tf_op jit(solution)/shard_map/ppermute | solution.py:583
  109.5 1.6 collective-permute-start.46
  111.0 7.5 %up_gelu.1 = (bf16[768,3072]{1,0:T(8,128)(2,1)S(1)}, bf16[768,3072]{1,0:T(8,128)(2,1)S(1)}) custom-call(bf16[768,768]{1,0:T(8,128)(2,1)S(1)} %get-tuple-element.338.low_ref, bf16[768,3072]{1,0:T(8,128)(2,1)S(1)} %bitcast.241, bf16[768,3200]{1,0:T(8,128)(2,1)S(1)} %bitcast.240), custom_call_target="tpu_custom_call" | custom-call | flops 11000000512 | bytes 1 | tf_op jit(solution)/shard_map/up_gelu/pallas_call | solution.py:271
  118.7 1.5 collective-permute-done.49.refs_12_
  120.2 2.4 assemble.5
  122.6 6.2 %down_norm.1 = (bf16[768,768]{1,0:T(8,128)(2,1)S(1)}, bf16[768,768]{1,0:T(8,128)(2,1)S(1)}, f32[8,768]{1,0:T(8,128)S(1)}) custom-call(bf16[768,3072]{1,0:T(8,128)(2,1)S(1)} %get-tuple-element.342.active_ref.left_ref, bf16[3072,768]{1,0:T(8,128)(2,1)S(1)} %bitcast.243, bf16[768,768]{1,0:T(8,128)(2,1)S(1)} %get-tuple-element.351.unit_ref, ...), custom_call_target="tpu_custom_call" | custom-call | flops 11000000512 | bytes 1 | tf_op jit(solution)/shard_map/down_norm/pallas_call | solution.py:314
  128.8 6.5 %down_gradient.1 = (bf16[2,768,768]{2,1,0:T(8,128)(2,1)}, bf16[2,768,768]{2,1,0:T(8,128)(2,1)S(1)}) custom-call(s32[1]{0:T(128)} %bitcast.core_ref, bf16[768,3072]{1,0:T(8,128)(2,1)S(1)} %get-tuple-element.342.active_ref.left_ref, bf16[768,768]{1,0:T(8,128)(2,1)S(1)} %get-tuple-element.353.right_ref.df_ref), custom_call_target="tpu_custom_call" | custom-call | flops 5500000256 | bytes 1 | tf_op jit(solution)/shard_map/down_gradient/pallas_call | solution.py:871
  135.3 1.5 copy-done.2
  136.9 15.7 %feed_forward_back.1 = (bf16[2,192,3072]{2,1,0:T(8,128)(2,1)}, bf16[2,192,3072]{2,1,0:T(8,128)(2,1)S(1)}, bf16[768,768]{1,0:T(8,128)(2,1)S(1)}, f32[1,3072]{1,0:T(1,128)S(1)}, f32[8,768]{1,0:T(8,128)S(1)}) custom-call(s32[1]{0:T(128)} %bitcast.core_ref, bf16[768,768]{1,0:T(8,128)(2,1)S(1)} %get-tuple-element.353.right_ref.df_ref, ...), custom_call_target="tpu_custom_call" | custom-call | flops 23100000256 | bytes 1 | tf_op jit(solution)/shard_map/feed_forward_back/pallas_call | solution.py:399
  154.8 1.4 collective-permute-start.53
  156.2 1.4 fusion.22
  158.3 10.6 %collective-permute-start.55 = (bf16[1,2,96,768]{3,2,1,0:T(8,128)(2,1)S(1)}, bf16[1,2,96,768]{3,2,1,0:T(8,128)(2,1)S(1)}, u32[]{:S(2)}, u32[]{:S(2)}) collective-permute-start(bf16[1,2,96,768]{3,2,1,0:T(8,128)(2,1)S(1)} %get-tuple-element.453), channel_id=1, source_target_pairs={{1,3},{3,5},{5,7},{7,6},{6,4},{4,2},{2,0},{0,1},{9,8},{11,9},{13,1... | collective-permute-start | bytes 884744 | tf_op jit(solution)/shard_map/ppermute | solution.py:583
  168.9 2.0 copy-done.23
  170.9 10.3 %attention_backward.1 = (bf16[768,2304]{1,0:T(8,128)(2,1)S(1)}, f32[1,2304]{1,0:T(1,128)S(1)}) custom-call(s32[6]{0:T(128)S(1)} %pad_add_fusion.lens_ref, bf16[768,2304]{1,0:T(8,128)(2,1)S(1)} %copy-done.23, bf16[768,768]{1,0:T(8,128)(2,1)S(1)} %copy-done.20, bf16[768,768]{1,0:T(8,128)(2,1)S(1)} %copy-done.21), custom_call_target="tpu_custom_call" | custom-call | flops 12099999744 | bytes 1 | tf_op jit(solution)/shard_map/attention_backward/pallas_call | solution.py:227
  181.2 2.8 fusion.24
  187.8 5.8 %attention_gradients.1 = (bf16[2,192,3200]{2,1,0:T(8,128)(2,1)}, bf16[2,192,3200]{2,1,0:T(8,128)(2,1)S(1)}) custom-call(s32[1]{0:T(128)} %bitcast.core_ref, bf16[2,2,192,768]{3,2,1,0:T(8,128)(2,1)S(1)} %bitcast.245, bf16[2,2,192,768]{3,2,1,0:T(8,128)(2,1)S(1)} %bitcast.246, bf16[768,2304]{1,0:T(8,128)(2,1)S(1)} %get-tuple-element.379.dqkv_ref, ...), custom_call_target="tpu_custom_call" | custom-call | flops 8800000000 | bytes 1 | tf_op jit(solution)/shard_map/attention_gradients/pallas_call | solution.py:820
  194.1 1.6 collective-permute-start.60
  197.7 1.5 fusion.16
  201.3 5.3 %add_convert_fusion = bf16[768,768]{1,0:T(8,128)(2,1)S(1)} fusion(bf16[768,768]{1,0:T(8,128)(2,1)} %copy-done.19, bf16[768,2304]{1,0:T(8,128)(2,1)S(1)} %copy-done.18, bf16[768,3200]{1,0:T(8,128)(2,1)} %bitcast.238), kind=kOutput, calls=%fused_computation.4 | convolution fusion | flops 2719678464 | bytes 9437184 | tf_op jit(solution)/shard_map/dot_general | solution.py:30
  206.6 3.4 %collective-permute-done.57 = bf16[1,2,96,768]{3,2,1,0:T(8,128)(2,1)S(1)} collective-permute-done((bf16[1,2,96,768]{3,2,1,0:T(8,128)(2,1)S(1)}, bf16[1,2,96,768]{3,2,1,0:T(8,128)(2,1)S(1)}, u32[]{:S(2)}, u32[]{:S(2)}) %collective-permute-start.57) | collective-permute-done | bytes 294944 | tf_op jit(solution)/shard_map/ppermute | solution.py:586
  214.3 1.6 collective-permute-start.64
  217.1 1.5 fusion.13
  221.7 1.9 collective-permute-start.63
  223.6 1.6 select_reduce_fusion.1
  225.2 2.0 collective-permute-done.65
  227.2 1.4 collective-permute-start.71
  228.6 1.7 collective-permute-done.63
  236.5 1.8 collective-permute-start.68
  238.7 1.6 select_reduce_fusion
  240.4 7.2 %collective-permute-done.68 = bf16[1,2,24,3072]{3,2,1,0:T(8,128)(2,1)S(1)} collective-permute-done((bf16[1,2,24,3072]{3,2,1,0:T(8,128)(2,1)S(1)}, bf16[1,2,24,3072]{3,2,1,0:T(8,128)(2,1)S(1)}, u32[]{:S(2)}, u32[]{:S(2)}) %collective-permute-start.68) | collective-permute-done | bytes 294944 | tf_op jit(solution)/shard_map/ppermute | solution.py:586
  254.2 3.2 %collective-permute-done.75 = bf16[24,3072]{1,0:T(8,128)(2,1)S(1)} collective-permute-done((bf16[24,3072]{1,0:T(8,128)(2,1)S(1)}, bf16[24,3072]{1,0:T(8,128)(2,1)S(1)}, u32[]{:S(2)}, u32[]{:S(2)}) %collective-permute-start.75) | collective-permute-done | bytes 147488 | tf_op jit(solution)/shard_map/ppermute | solution.py:590
  257.4 1.5 collective-permute-done.73
  263.3 6.7 %collective-permute-done.76 = bf16[1,2,24,3200]{3,2,1,0:T(8,128)(2,1)S(1)} collective-permute-done((bf16[1,2,24,3200]{3,2,1,0:T(8,128)(2,1)S(1)}, bf16[1,2,24,3200]{3,2,1,0:T(8,128)(2,1)S(1)}, u32[]{:S(2)}, u32[]{:S(2)}) %collective-permute-start.76) | collective-permute-done | bytes 307232 | tf_op jit(solution)/shard_map/ppermute | solution.py:586
  272.2 4.5 %collective-permute-done.78 = bf16[24,3200]{1,0:T(8,128)(2,1)S(1)} collective-permute-done((bf16[24,3200]{1,0:T(8,128)(2,1)S(1)}, bf16[24,3200]{1,0:T(8,128)(2,1)S(1)}, u32[]{:S(2)}, u32[]{:S(2)}) %collective-permute-start.78) | collective-permute-done | bytes 153632 | tf_op jit(solution)/shard_map/ppermute | solution.py:590
  (271 shorter events, 65.6 us)
Async XLA Ops:
  2.6 8.0 %collective-permute-start = (bf16[24,3200]{1,0:T(8,128)(2,1)}, bf16[24,3200]{1,0:T(8,128)(2,1)S(1)}, u32[]{:S(2)}, u32[]{:S(2)}) collective-permute-start(bf16[24,3200]{1,0:T(8,128)(2,1)} %get-tuple-element.221), channel_id=1, source_target_pairs={{0,16},{16,0},{1,17},{17,1},{2,18},{18,2},{3,19},{19,3},{4,20},{20... | collective-permute-start | bytes 460808 | tf_op jit(solution)/shard_map/ppermute | solution.py:590
  6.6 9.9 %collective-permute-start.3 = (bf16[24,3072]{1,0:T(8,128)(2,1)S(1)}, bf16[24,3072]{1,0:T(8,128)(2,1)S(1)}, u32[]{:S(2)}, u32[]{:S(2)}) collective-permute-start(bf16[24,3072]{1,0:T(8,128)(2,1)S(1)} %get-tuple-element.462), channel_id=1, source_target_pairs={{0,16},{16,0},{1,17},{17,1},{2,18},{18,2},{3,19},{19,3},{4,20},{20... | collective-permute-start | bytes 442376 | tf_op jit(solution)/shard_map/ppermute | solution.py:590
  11.7 4.8 %collective-permute-start.4 = (bf16[1,2,24,3200]{3,2,1,0:T(8,128)(2,1)S(1)}, bf16[1,2,24,3200]{3,2,1,0:T(8,128)(2,1)S(1)}, u32[]{:S(2)}, u32[]{:S(2)}) collective-permute-start(bf16[1,2,24,3200]{3,2,1,0:T(8,128)(2,1)S(1)} %broadcast_select_fusion.1.refs_0_), channel_id=1, source_target_pairs={{0,8},{8,0},{1,9},{9,1},{2,10},{10,2},{3,11},{11,3},{4,12},{12,4},... | collective-permute-start | bytes 921608 | tf_op jit(solution)/shard_map/ppermute | solution.py:590
  11.7 9.3 %collective-permute-start.1 = (bf16[1,2,24,3200]{3,2,1,0:T(8,128)(2,1)S(1)}, bf16[1,2,24,3200]{3,2,1,0:T(8,128)(2,1)S(1)}, u32[]{:S(2)}, u32[]{:S(2)}) collective-permute-start(bf16[1,2,24,3200]{3,2,1,0:T(8,128)(2,1)S(1)} %broadcast_select_fusion.1.refs_0_), channel_id=1, source_target_pairs={{1,3},{3,5},{5,7},{7,6},{6,4},{4,2},{2,0},{0,1},{9,8},{11,9},{13,1... | collective-permute-start | bytes 921608 | tf_op jit(solution)/shard_map/ppermute | solution.py:583
  13.9 7.9 %collective-permute-start.2 = (bf16[1,2,24,3200]{3,2,1,0:T(8,128)(2,1)S(1)}, bf16[1,2,24,3200]{3,2,1,0:T(8,128)(2,1)S(1)}, u32[]{:S(2)}, u32[]{:S(2)}) collective-permute-start(bf16[1,2,24,3200]{3,2,1,0:T(8,128)(2,1)S(1)} %broadcast_select_fusion.1.refs_0_), channel_id=1, source_target_pairs={{1,0},{3,1},{5,3},{7,5},{6,7},{4,6},{2,4},{0,2},{9,11},{11,13},{13... | collective-permute-start | bytes 921608 | tf_op jit(solution)/shard_map/ppermute | solution.py:586
  21.8 5.2 %collective-permute-start.7 = (bf16[1,2,24,3200]{3,2,1,0:T(8,128)(2,1)S(1)}, bf16[1,2,24,3200]{3,2,1,0:T(8,128)(2,1)S(1)}, u32[]{:S(2)}, u32[]{:S(2)}) collective-permute-start(bf16[1,2,24,3200]{3,2,1,0:T(8,128)(2,1)S(1)} %collective-permute-done.1.refs_1_), channel_id=1, source_target_pairs={{0,8},{8,0},{1,9},{9,1},{2,10},{10,2},{3,11},{11,3},{4,12},{12,4},... | collective-permute-start | bytes 921608 | tf_op jit(solution)/shard_map/ppermute | solution.py:590
  21.9 8.7 %collective-permute-start.5 = (bf16[1,2,24,3200]{3,2,1,0:T(8,128)(2,1)S(1)}, bf16[1,2,24,3200]{3,2,1,0:T(8,128)(2,1)S(1)}, u32[]{:S(2)}, u32[]{:S(2)}) collective-permute-start(bf16[1,2,24,3200]{3,2,1,0:T(8,128)(2,1)S(1)} %collective-permute-done.1.refs_1_), channel_id=1, source_target_pairs={{1,3},{3,5},{5,7},{7,6},{6,4},{4,2},{2,0},{0,1},{9,8},{11,9},{13,1... | collective-permute-start | bytes 921608 | tf_op jit(solution)/shard_map/ppermute | solution.py:583
  23.8 9.7 %collective-permute-start.6 = (bf16[1,2,24,3200]{3,2,1,0:T(8,128)(2,1)S(1)}, bf16[1,2,24,3200]{3,2,1,0:T(8,128)(2,1)S(1)}, u32[]{:S(2)}, u32[]{:S(2)}) collective-permute-start(bf16[1,2,24,3200]{3,2,1,0:T(8,128)(2,1)S(1)} %collective-permute-done.2.refs_5_), channel_id=1, source_target_pairs={{1,0},{3,1},{5,3},{7,5},{6,7},{4,6},{2,4},{0,2},{9,11},{11,13},{13... | collective-permute-start | bytes 921608 | tf_op jit(solution)/shard_map/ppermute | solution.py:586
  25.4 20.0 %collective-permute-start.13 = (bf16[3,144,768]{2,1,0:T(8,128)(2,1)S(1)}, bf16[3,144,768]{2,1,0:T(8,128)(2,1)S(1)}, u32[]{:S(2)}, u32[]{:S(2)}) collective-permute-start(bf16[3,144,768]{2,1,0:T(8,128)(2,1)S(1)} %pad_maximum_fusion.4), channel_id=1, source_target_pairs={{0,16},{16,0},{1,17},{17,1},{2,18},{18,2},{3,19},{19,3},{4,20},{20... | collective-permute-start | bytes 1990664 | tf_op jit(solution)/shard_map/ppermute | solution.py:590
  27.0 10.0 %collective-permute-start.11 = (bf16[1,2,24,3072]{3,2,1,0:T(8,128)(2,1)S(1)}, bf16[1,2,24,3072]{3,2,1,0:T(8,128)(2,1)S(1)}, u32[]{:S(2)}, u32[]{:S(2)}) collective-permute-start(bf16[1,2,24,3072]{3,2,1,0:T(8,128)(2,1)S(1)} %broadcast_select_fusion.5.refs_0_), channel_id=1, source_target_pairs={{1,3},{3,5},{5,7},{7,6},{6,4},{4,2},{2,0},{0,1},{9,8},{11,9},{13,1... | collective-permute-start | bytes 884744 | tf_op jit(solution)/shard_map/ppermute | solution.py:583
  27.6 10.3 %collective-permute-start.12 = (bf16[1,2,24,3072]{3,2,1,0:T(8,128)(2,1)S(1)}, bf16[1,2,24,3072]{3,2,1,0:T(8,128)(2,1)S(1)}, u32[]{:S(2)}, u32[]{:S(2)}) collective-permute-start(bf16[1,2,24,3072]{3,2,1,0:T(8,128)(2,1)S(1)} %broadcast_select_fusion.5.refs_0_), channel_id=1, source_target_pairs={{1,0},{3,1},{5,3},{7,5},{6,7},{4,6},{2,4},{0,2},{9,11},{11,13},{13... | collective-permute-start | bytes 884744 | tf_op jit(solution)/shard_map/ppermute | solution.py:586
  30.6 7.8 %collective-permute-start.16 = (bf16[1,2,24,3072]{3,2,1,0:T(8,128)(2,1)S(1)}, bf16[1,2,24,3072]{3,2,1,0:T(8,128)(2,1)S(1)}, u32[]{:S(2)}, u32[]{:S(2)}) collective-permute-start(bf16[1,2,24,3072]{3,2,1,0:T(8,128)(2,1)S(1)} %broadcast_select_fusion.5.refs_0_), channel_id=1, source_target_pairs={{0,8},{8,0},{1,9},{9,1},{2,10},{10,2},{3,11},{11,3},{4,12},{12,4},... | collective-permute-start | bytes 884744 | tf_op jit(solution)/shard_map/ppermute | solution.py:590
  33.5 7.7 %collective-permute-start.10 = (bf16[1,2,24,3200]{3,2,1,0:T(8,128)(2,1)S(1)}, bf16[1,2,24,3200]{3,2,1,0:T(8,128)(2,1)S(1)}, u32[]{:S(2)}, u32[]{:S(2)}) collective-permute-start(bf16[1,2,24,3200]{3,2,1,0:T(8,128)(2,1)S(1)} %collective-permute-done.6.refs_6_), channel_id=1, source_target_pairs={{1,0},{3,1},{5,3},{7,5},{6,7},{4,6},{2,4},{0,2},{9,11},{11,13},{13... | collective-permute-start | bytes 921608 | tf_op jit(solution)/shard_map/ppermute | solution.py:586
  37.0 4.2 %collective-permute-start.15 = (bf16[1,2,24,3200]{3,2,1,0:T(8,128)(2,1)S(1)}, bf16[1,2,24,3200]{3,2,1,0:T(8,128)(2,1)S(1)}, u32[]{:S(2)}, u32[]{:S(2)}) collective-permute-start(bf16[1,2,24,3200]{3,2,1,0:T(8,128)(2,1)S(1)} %collective-permute-done.6.refs_6_), channel_id=1, source_target_pairs={{0,8},{8,0},{1,9},{9,1},{2,10},{10,2},{3,11},{11,3},{4,12},{12,4},... | collective-permute-start | bytes 921608 | tf_op jit(solution)/shard_map/ppermute | solution.py:590
  38.5 6.9 %collective-permute-start.9 = (bf16[1,2,24,3200]{3,2,1,0:T(8,128)(2,1)S(1)}, bf16[1,2,24,3200]{3,2,1,0:T(8,128)(2,1)S(1)}, u32[]{:S(2)}, u32[]{:S(2)}) collective-permute-start(bf16[1,2,24,3200]{3,2,1,0:T(8,128)(2,1)S(1)} %collective-permute-done.5.refs_2_), channel_id=1, source_target_pairs={{1,3},{3,5},{5,7},{7,6},{6,4},{4,2},{2,0},{0,1},{9,8},{11,9},{13,1... | collective-permute-start | bytes 921608 | tf_op jit(solution)/shard_map/ppermute | solution.py:583
  45.3 6.1 %collective-permute-start.21 = (bf16[1,2,24,3200]{3,2,1,0:T(8,128)(2,1)S(1)}, bf16[1,2,24,3200]{3,2,1,0:T(8,128)(2,1)S(1)}, u32[]{:S(2)}, u32[]{:S(2)}) collective-permute-start(bf16[1,2,24,3200]{3,2,1,0:T(8,128)(2,1)S(1)} %collective-permute-done.9.refs_3_), channel_id=1, source_target_pairs={{0,8},{8,0},{1,9},{9,1},{2,10},{10,2},{3,11},{11,3},{4,12},{12,4},... | collective-permute-start | bytes 921608 | tf_op jit(solution)/shard_map/ppermute | solution.py:590
  45.4 6.6 %collective-permute-start.22 = (bf16[1,2,24,3200]{3,2,1,0:T(8,128)(2,1)S(1)}, bf16[1,2,24,3200]{3,2,1,0:T(8,128)(2,1)S(1)}, u32[]{:S(2)}, u32[]{:S(2)}) collective-permute-start(bf16[1,2,24,3200]{3,2,1,0:T(8,128)(2,1)S(1)} %collective-permute-done.10.refs_7_), channel_id=1, source_target_pairs={{0,8},{8,0},{1,9},{9,1},{2,10},{10,2},{3,11},{11,3},{4,12},{12,4},... | collective-permute-start | bytes 921608 | tf_op jit(solution)/shard_map/ppermute | solution.py:590
  46.4 8.2 %collective-permute-start.20 = (bf16[96,768]{1,0:T(8,128)(2,1)S(1)}, bf16[96,768]{1,0:T(8,128)(2,1)S(1)}, u32[]{:S(2)}, u32[]{:S(2)}) collective-permute-start(bf16[96,768]{1,0:T(8,128)(2,1)S(1)} %get-tuple-element.460), channel_id=1, source_target_pairs={{0,16},{16,0},{1,17},{17,1},{2,18},{18,2},{3,19},{19,3},{4,20},{20... | collective-permute-start | bytes 442376 | tf_op jit(solution)/shard_map/ppermute | solution.py:590
  48.4 13.3 %collective-permute-start.17 = (bf16[1,2,24,3200]{3,2,1,0:T(8,128)(2,1)S(1)}, bf16[1,2,24,3200]{3,2,1,0:T(8,128)(2,1)}, u32[]{:S(2)}, u32[]{:S(2)}) collective-permute-start(bf16[1,2,24,3200]{3,2,1,0:T(8,128)(2,1)S(1)} %collective-permute-done.9.refs_3_), channel_id=1, source_target_pairs={{1,3},{3,5},{5,7},{7,6},{6,4},{4,2},{2,0},{0,1},{9,8},{11,9},{13,1... | collective-permute-start | bytes 921608 | tf_op jit(solution)/shard_map/ppermute | solution.py:583
  49.9 11.7 %collective-permute-start.18 = (bf16[1,2,24,3072]{3,2,1,0:T(8,128)(2,1)S(1)}, bf16[1,2,24,3072]{3,2,1,0:T(8,128)(2,1)}, u32[]{:S(2)}, u32[]{:S(2)}) collective-permute-start(bf16[1,2,24,3072]{3,2,1,0:T(8,128)(2,1)S(1)} %collective-permute-done.11.refs_1_), channel_id=1, source_target_pairs={{1,3},{3,5},{5,7},{7,6},{6,4},{4,2},{2,0},{0,1},{9,8},{11,9},{13,1... | collective-permute-start | bytes 884744 | tf_op jit(solution)/shard_map/ppermute | solution.py:583
  51.5 10.2 %collective-permute-start.19 = (bf16[1,2,24,3072]{3,2,1,0:T(8,128)(2,1)S(1)}, bf16[1,2,24,3072]{3,2,1,0:T(8,128)(2,1)}, u32[]{:S(2)}, u32[]{:S(2)}) collective-permute-start(bf16[1,2,24,3072]{3,2,1,0:T(8,128)(2,1)S(1)} %collective-permute-done.12.refs_5_), channel_id=1, source_target_pairs={{1,0},{3,1},{5,3},{7,5},{6,7},{4,6},{2,4},{0,2},{9,11},{11,13},{13... | collective-permute-start | bytes 884744 | tf_op jit(solution)/shard_map/ppermute | solution.py:586
  61.7 5.9 %collective-permute-start.33 = (bf16[1,2,24,3200]{3,2,1,0:T(8,128)(2,1)}, bf16[1,2,24,3200]{3,2,1,0:T(8,128)(2,1)}, u32[]{:S(2)}, u32[]{:S(2)}) collective-permute-start(bf16[1,2,24,3200]{3,2,1,0:T(8,128)(2,1)} %collective-permute-done.17.refs_4_), channel_id=1, source_target_pairs={{0,8},{8,0},{1,9},{9,1},{2,10},{10,2},{3,11},{11,3},{4,12},{12,4},... | collective-permute-start | bytes 921608 | tf_op jit(solution)/shard_map/ppermute | solution.py:590
  62.5 4.6 %collective-permute-start.31 = (bf16[1,2,24,3072]{3,2,1,0:T(8,128)(2,1)}, bf16[1,2,24,3072]{3,2,1,0:T(8,128)(2,1)}, u32[]{:S(2)}, u32[]{:S(2)}) collective-permute-start(bf16[1,2,24,3072]{3,2,1,0:T(8,128)(2,1)} %collective-permute-done.19.refs_6_), channel_id=1, source_target_pairs={{0,8},{8,0},{1,9},{9,1},{2,10},{10,2},{3,11},{11,3},{4,12},{12,4},... | collective-permute-start | bytes 884744 | tf_op jit(solution)/shard_map/ppermute | solution.py:590
  63.5 13.1 %collective-permute-start.27 = (bf16[1,2,96,768]{3,2,1,0:T(8,128)(2,1)S(1)}, bf16[1,2,96,768]{3,2,1,0:T(8,128)(2,1)S(1)}, u32[]{:S(2)}, u32[]{:S(2)}) collective-permute-start(bf16[1,2,96,768]{3,2,1,0:T(8,128)(2,1)S(1)} %broadcast_select_fusion.4.refs_0_), channel_id=1, source_target_pairs={{1,3},{3,5},{5,7},{7,6},{6,4},{4,2},{2,0},{0,1},{9,8},{11,9},{13,1... | collective-permute-start | bytes 884744 | tf_op jit(solution)/shard_map/ppermute | solution.py:583
  65.0 11.6 %collective-permute-start.28 = (bf16[1,2,96,768]{3,2,1,0:T(8,128)(2,1)S(1)}, bf16[1,2,96,768]{3,2,1,0:T(8,128)(2,1)S(1)}, u32[]{:S(2)}, u32[]{:S(2)}) collective-permute-start(bf16[1,2,96,768]{3,2,1,0:T(8,128)(2,1)S(1)} %broadcast_select_fusion.4.refs_0_), channel_id=1, source_target_pairs={{1,0},{3,1},{5,3},{7,5},{6,7},{4,6},{2,4},{0,2},{9,11},{11,13},{13... | collective-permute-start | bytes 884744 | tf_op jit(solution)/shard_map/ppermute | solution.py:586
  65.5 13.8 %collective-permute-start.25 = (bf16[1,2,24,3072]{3,2,1,0:T(8,128)(2,1)}, bf16[1,2,24,3072]{3,2,1,0:T(8,128)(2,1)S(1)}, u32[]{:S(2)}, u32[]{:S(2)}) collective-permute-start(bf16[1,2,24,3072]{3,2,1,0:T(8,128)(2,1)} %collective-permute-done.18.refs_2_), channel_id=1, source_target_pairs={{1,3},{3,5},{5,7},{7,6},{6,4},{4,2},{2,0},{0,1},{9,8},{11,9},{13,1... | collective-permute-start | bytes 884744 | tf_op jit(solution)/shard_map/ppermute | solution.py:583
  67.1 12.3 %collective-permute-start.26 = (bf16[1,2,24,3072]{3,2,1,0:T(8,128)(2,1)}, bf16[1,2,24,3072]{3,2,1,0:T(8,128)(2,1)S(1)}, u32[]{:S(2)}, u32[]{:S(2)}) collective-permute-start(bf16[1,2,24,3072]{3,2,1,0:T(8,128)(2,1)} %collective-permute-done.19.refs_6_), channel_id=1, source_target_pairs={{1,0},{3,1},{5,3},{7,5},{6,7},{4,6},{2,4},{0,2},{9,11},{11,13},{13... | collective-permute-start | bytes 884744 | tf_op jit(solution)/shard_map/ppermute | solution.py:586
  67.5 14.6 %collective-permute-start.29 = (bf16[3,128,768]{2,1,0:T(8,128)(2,1)}, bf16[3,128,768]{2,1,0:T(8,128)(2,1)S(1)}, u32[]{:S(2)}, u32[]{:S(2)}) collective-permute-start(bf16[3,128,768]{2,1,0:T(8,128)(2,1)} %select_reduce_fusion.3), channel_id=1, source_target_pairs={{0,16},{16,0},{1,17},{17,1},{2,18},{18,2},{3,19},{19,3},{4,20},{20... | collective-permute-start | bytes 1769480 | tf_op jit(solution)/shard_map/ppermute | solution.py:590
  82.1 4.1 %collective-permute-start.38 = (bf16[1,2,24,3072]{3,2,1,0:T(8,128)(2,1)S(1)}, bf16[1,2,24,3072]{3,2,1,0:T(8,128)(2,1)S(1)}, u32[]{:S(2)}, u32[]{:S(2)}) collective-permute-start(bf16[1,2,24,3072]{3,2,1,0:T(8,128)(2,1)S(1)} %collective-permute-done.26.refs_7_), channel_id=1, source_target_pairs={{0,8},{8,0},{1,9},{9,1},{2,10},{10,2},{3,11},{11,3},{4,12},{12,4},... | collective-permute-start | bytes 884744 | tf_op jit(solution)/shard_map/ppermute | solution.py:590
  83.5 15.0 %collective-permute-start.34 = (bf16[1,2,24,3072]{3,2,1,0:T(8,128)(2,1)S(1)}, bf16[1,2,24,3072]{3,2,1,0:T(8,128)(2,1)S(1)}, u32[]{:S(2)}, u32[]{:S(2)}) collective-permute-start(bf16[1,2,24,3072]{3,2,1,0:T(8,128)(2,1)S(1)} %collective-permute-done.25.refs_3_), channel_id=1, source_target_pairs={{1,3},{3,5},{5,7},{7,6},{6,4},{4,2},{2,0},{0,1},{9,8},{11,9},{13,1... | collective-permute-start | bytes 884744 | tf_op jit(solution)/shard_map/ppermute | solution.py:583
  84.8 13.7 %collective-permute-start.35 = (bf16[1,2,96,768]{3,2,1,0:T(8,128)(2,1)S(1)}, bf16[1,2,96,768]{3,2,1,0:T(8,128)(2,1)S(1)}, u32[]{:S(2)}, u32[]{:S(2)}) collective-permute-start(bf16[1,2,96,768]{3,2,1,0:T(8,128)(2,1)S(1)} %collective-permute-done.27.refs_1_), channel_id=1, source_target_pairs={{1,3},{3,5},{5,7},{7,6},{6,4},{4,2},{2,0},{0,1},{9,8},{11,9},{13,1... | collective-permute-start | bytes 884744 | tf_op jit(solution)/shard_map/ppermute | solution.py:583
  86.2 12.3 %collective-permute-start.36 = (bf16[1,2,96,768]{3,2,1,0:T(8,128)(2,1)S(1)}, bf16[1,2,96,768]{3,2,1,0:T(8,128)(2,1)S(1)}, u32[]{:S(2)}, u32[]{:S(2)}) collective-permute-start(bf16[1,2,96,768]{3,2,1,0:T(8,128)(2,1)S(1)} %collective-permute-done.28.refs_5_), channel_id=1, source_target_pairs={{1,0},{3,1},{5,3},{7,5},{6,7},{4,6},{2,4},{0,2},{9,11},{11,13},{13... | collective-permute-start | bytes 884744 | tf_op jit(solution)/shard_map/ppermute | solution.py:586
  99.2 9.7 %collective-permute-start.41 = (bf16[1,2,96,768]{3,2,1,0:T(8,128)(2,1)S(1)}, bf16[1,2,96,768]{3,2,1,0:T(8,128)(2,1)S(1)}, u32[]{:S(2)}, u32[]{:S(2)}) collective-permute-start(bf16[1,2,96,768]{3,2,1,0:T(8,128)(2,1)S(1)} %collective-permute-done.35.refs_2_), channel_id=1, source_target_pairs={{1,3},{3,5},{5,7},{7,6},{6,4},{4,2},{2,0},{0,1},{9,8},{11,9},{13,1... | collective-permute-start | bytes 884744 | tf_op jit(solution)/shard_map/ppermute | solution.py:583
  100.6 8.3 %collective-permute-start.42 = (bf16[1,2,96,768]{3,2,1,0:T(8,128)(2,1)S(1)}, bf16[1,2,96,768]{3,2,1,0:T(8,128)(2,1)S(1)}, u32[]{:S(2)}, u32[]{:S(2)}) collective-permute-start(bf16[1,2,96,768]{3,2,1,0:T(8,128)(2,1)S(1)} %collective-permute-done.36.refs_6_), channel_id=1, source_target_pairs={{1,0},{3,1},{5,3},{7,5},{6,7},{4,6},{2,4},{0,2},{9,11},{11,13},{13... | collective-permute-start | bytes 884744 | tf_op jit(solution)/shard_map/ppermute | solution.py:586
  109.5 9.1 %collective-permute-start.46 = (bf16[1,2,96,768]{3,2,1,0:T(8,128)(2,1)S(1)}, bf16[1,2,96,768]{3,2,1,0:T(8,128)(2,1)S(1)}, u32[]{:S(2)}, u32[]{:S(2)}) collective-permute-start(bf16[1,2,96,768]{3,2,1,0:T(8,128)(2,1)S(1)} %collective-permute-done.41.refs_3_), channel_id=1, source_target_pairs={{1,3},{3,5},{5,7},{7,6},{6,4},{4,2},{2,0},{0,1},{9,8},{11,9},{13,1... | collective-permute-start | bytes 884744 | tf_op jit(solution)/shard_map/ppermute | solution.py:583
  136.8 17.9 %collective-permute-start.50 = (bf16[2,768,768]{2,1,0:T(8,128)(2,1)}, bf16[2,768,768]{2,1,0:T(8,128)(2,1)}, u32[]{:S(2)}, u32[]{:S(2)}) collective-permute-start(bf16[2,768,768]{2,1,0:T(8,128)(2,1)} %get-tuple-element.355), channel_id=1, source_target_pairs={{0,8},{8,0},{1,9},{9,1},{2,10},{10,2},{3,11},{11,3},{4,12},{12,4},... | collective-permute-start | bytes 7077896 | tf_op jit(solution)/shard_map/ppermute | solution.py:590
  154.3 26.9 %collective-permute-start.52 = (bf16[2,192,3072]{2,1,0:T(8,128)(2,1)}, bf16[2,192,3072]{2,1,0:T(8,128)(2,1)}, u32[]{:S(2)}, u32[]{:S(2)}) collective-permute-start(bf16[2,192,3072]{2,1,0:T(8,128)(2,1)} %get-tuple-element.363), channel_id=1, source_target_pairs={{0,8},{8,0},{1,9},{9,1},{2,10},{10,2},{3,11},{11,3},{4,12},{12,4},... | collective-permute-start | bytes 7077896 | tf_op jit(solution)/shard_map/ppermute | solution.py:590
  154.8 26.5 %collective-permute-start.53 = (bf16[3,128,768]{2,1,0:T(8,128)(2,1)S(1)}, bf16[3,128,768]{2,1,0:T(8,128)(2,1)S(1)}, u32[]{:S(2)}, u32[]{:S(2)}) collective-permute-start(bf16[3,128,768]{2,1,0:T(8,128)(2,1)S(1)} %bitcast.256), channel_id=1, source_target_pairs={{0,16},{16,0},{1,17},{17,1},{2,18},{18,2},{3,19},{19,3},{4,20},{20... | collective-permute-start | bytes 1769480 | tf_op jit(solution)/shard_map/ppermute | solution.py:590
  157.5 23.7 %collective-permute-start.51 = (bf16[1,2,96,768]{3,2,1,0:T(8,128)(2,1)S(1)}, bf16[1,2,96,768]{3,2,1,0:T(8,128)(2,1)S(1)}, u32[]{:S(2)}, u32[]{:S(2)}) collective-permute-start(bf16[1,2,96,768]{3,2,1,0:T(8,128)(2,1)S(1)} %get-tuple-element.454), channel_id=1, source_target_pairs={{1,0},{3,1},{5,3},{7,5},{6,7},{4,6},{2,4},{0,2},{9,11},{11,13},{13... | collective-permute-start | bytes 884744 | tf_op jit(solution)/shard_map/ppermute | solution.py:586
  158.3 35.3 %collective-permute-start.55 = (bf16[1,2,96,768]{3,2,1,0:T(8,128)(2,1)S(1)}, bf16[1,2,96,768]{3,2,1,0:T(8,128)(2,1)S(1)}, u32[]{:S(2)}, u32[]{:S(2)}) collective-permute-start(bf16[1,2,96,768]{3,2,1,0:T(8,128)(2,1)S(1)} %get-tuple-element.453), channel_id=1, source_target_pairs={{1,3},{3,5},{5,7},{7,6},{6,4},{4,2},{2,0},{0,1},{9,8},{11,9},{13,1... | collective-permute-start | bytes 884744 | tf_op jit(solution)/shard_map/ppermute | solution.py:583
  184.0 9.6 %collective-permute-start.56 = (bf16[1,2,24,3072]{3,2,1,0:T(8,128)(2,1)S(1)}, bf16[1,2,24,3072]{3,2,1,0:T(8,128)(2,1)}, u32[]{:S(2)}, u32[]{:S(2)}) collective-permute-start(bf16[1,2,24,3072]{3,2,1,0:T(8,128)(2,1)S(1)} %get-tuple-element.450), channel_id=1, source_target_pairs={{1,0},{3,1},{5,3},{7,5},{6,7},{4,6},{2,4},{0,2},{9,11},{11,13},{13... | collective-permute-start | bytes 884744 | tf_op jit(solution)/shard_map/ppermute | solution.py:586
  185.9 8.1 %collective-permute-start.54 = (bf16[1,2,96,768]{3,2,1,0:T(8,128)(2,1)S(1)}, bf16[1,2,96,768]{3,2,1,0:T(8,128)(2,1)}, u32[]{:S(2)}, u32[]{:S(2)}) collective-permute-start(bf16[1,2,96,768]{3,2,1,0:T(8,128)(2,1)S(1)} %fusion.18), channel_id=1, source_target_pairs={{1,0},{3,1},{5,3},{7,5},{6,7},{4,6},{2,4},{0,2},{9,11},{11,13},{13... | collective-permute-start | bytes 884744 | tf_op jit(solution)/shard_map/ppermute | solution.py:586
  194.0 16.4 %collective-permute-start.61 = (bf16[2,192,3200]{2,1,0:T(8,128)(2,1)}, bf16[2,192,3200]{2,1,0:T(8,128)(2,1)}, u32[]{:S(2)}, u32[]{:S(2)}) collective-permute-start(bf16[2,192,3200]{2,1,0:T(8,128)(2,1)} %get-tuple-element.388), channel_id=1, source_target_pairs={{0,8},{8,0},{1,9},{9,1},{2,10},{10,2},{3,11},{11,3},{4,12},{12,4},... | collective-permute-start | bytes 7372808 | tf_op jit(solution)/shard_map/ppermute | solution.py:590
  194.1 12.5 %collective-permute-start.60 = (bf16[1,2,24,3072]{3,2,1,0:T(8,128)(2,1)}, bf16[1,2,24,3072]{3,2,1,0:T(8,128)(2,1)S(1)}, u32[]{:S(2)}, u32[]{:S(2)}) collective-permute-start(bf16[1,2,24,3072]{3,2,1,0:T(8,128)(2,1)} %get-tuple-element.449), channel_id=1, source_target_pairs={{1,3},{3,5},{5,7},{7,6},{6,4},{4,2},{2,0},{0,1},{9,8},{11,9},{13,1... | collective-permute-start | bytes 884744 | tf_op jit(solution)/shard_map/ppermute | solution.py:583
  197.0 9.7 %collective-permute-start.59 = (bf16[1,2,24,3072]{3,2,1,0:T(8,128)(2,1)S(1)}, bf16[1,2,24,3072]{3,2,1,0:T(8,128)(2,1)S(1)}, u32[]{:S(2)}, u32[]{:S(2)}) collective-permute-start(bf16[1,2,24,3072]{3,2,1,0:T(8,128)(2,1)S(1)} %fusion.15), channel_id=1, source_target_pairs={{1,0},{3,1},{5,3},{7,5},{6,7},{4,6},{2,4},{0,2},{9,11},{11,13},{13... | collective-permute-start | bytes 884744 | tf_op jit(solution)/shard_map/ppermute | solution.py:586
  199.2 10.9 %collective-permute-start.57 = (bf16[1,2,96,768]{3,2,1,0:T(8,128)(2,1)S(1)}, bf16[1,2,96,768]{3,2,1,0:T(8,128)(2,1)S(1)}, u32[]{:S(2)}, u32[]{:S(2)}) collective-permute-start(bf16[1,2,96,768]{3,2,1,0:T(8,128)(2,1)S(1)} %get-tuple-element.452), channel_id=1, source_target_pairs={{1,0},{3,1},{5,3},{7,5},{6,7},{4,6},{2,4},{0,2},{9,11},{11,13},{13... | collective-permute-start | bytes 884744 | tf_op jit(solution)/shard_map/ppermute | solution.py:586
  200.5 9.9 %collective-permute-start.58 = (bf16[1,2,96,768]{3,2,1,0:T(8,128)(2,1)S(1)}, bf16[1,2,96,768]{3,2,1,0:T(8,128)(2,1)S(1)}, u32[]{:S(2)}, u32[]{:S(2)}) collective-permute-start(bf16[1,2,96,768]{3,2,1,0:T(8,128)(2,1)S(1)} %get-tuple-element.451), channel_id=1, source_target_pairs={{1,3},{3,5},{5,7},{7,6},{6,4},{4,2},{2,0},{0,1},{9,8},{11,9},{13,1... | collective-permute-start | bytes 884744 | tf_op jit(solution)/shard_map/ppermute | solution.py:583
  211.6 18.7 %collective-permute-start.66 = (bf16[1,2,24,3200]{3,2,1,0:T(8,128)(2,1)S(1)}, bf16[1,2,24,3200]{3,2,1,0:T(8,128)(2,1)S(1)}, u32[]{:S(2)}, u32[]{:S(2)}) collective-permute-start(bf16[1,2,24,3200]{3,2,1,0:T(8,128)(2,1)S(1)} %get-tuple-element.442), channel_id=1, source_target_pairs={{1,0},{3,1},{5,3},{7,5},{6,7},{4,6},{2,4},{0,2},{9,11},{11,13},{13... | collective-permute-start | bytes 921608 | tf_op jit(solution)/shard_map/ppermute | solution.py:586
  214.3 7.4 %collective-permute-start.64 = (bf16[1,2,24,3072]{3,2,1,0:T(8,128)(2,1)S(1)}, bf16[1,2,24,3072]{3,2,1,0:T(8,128)(2,1)S(1)}, u32[]{:S(2)}, u32[]{:S(2)}) collective-permute-start(bf16[1,2,24,3072]{3,2,1,0:T(8,128)(2,1)S(1)} %get-tuple-element.446), channel_id=1, source_target_pairs={{1,0},{3,1},{5,3},{7,5},{6,7},{4,6},{2,4},{0,2},{9,11},{11,13},{13... | collective-permute-start | bytes 884744 | tf_op jit(solution)/shard_map/ppermute | solution.py:586
  215.9 15.1 %collective-permute-start.67 = (bf16[3,128,768]{2,1,0:T(8,128)(2,1)S(1)}, bf16[3,128,768]{2,1,0:T(8,128)(2,1)S(1)}, u32[]{:S(2)}, u32[]{:S(2)}) collective-permute-start(bf16[3,128,768]{2,1,0:T(8,128)(2,1)S(1)} %bitcast.255), channel_id=1, source_target_pairs={{0,16},{16,0},{1,17},{17,1},{2,18},{18,2},{3,19},{19,3},{4,20},{20... | collective-permute-start | bytes 1769480 | tf_op jit(solution)/shard_map/ppermute | solution.py:590
  218.6 10.0 %collective-permute-start.62 = (bf16[1,2,96,768]{3,2,1,0:T(8,128)(2,1)S(1)}, bf16[1,2,96,768]{3,2,1,0:T(8,128)(2,1)S(1)}, u32[]{:S(2)}, u32[]{:S(2)}) collective-permute-start(bf16[1,2,96,768]{3,2,1,0:T(8,128)(2,1)S(1)} %get-tuple-element.448), channel_id=1, source_target_pairs={{1,0},{3,1},{5,3},{7,5},{6,7},{4,6},{2,4},{0,2},{9,11},{11,13},{13... | collective-permute-start | bytes 884744 | tf_op jit(solution)/shard_map/ppermute | solution.py:586
  219.8 7.4 %collective-permute-start.65 = (bf16[1,2,24,3072]{3,2,1,0:T(8,128)(2,1)S(1)}, bf16[1,2,24,3072]{3,2,1,0:T(8,128)(2,1)S(1)}, u32[]{:S(2)}, u32[]{:S(2)}) collective-permute-start(bf16[1,2,24,3072]{3,2,1,0:T(8,128)(2,1)S(1)} %get-tuple-element.445), channel_id=1, source_target_pairs={{1,3},{3,5},{5,7},{7,6},{6,4},{4,2},{2,0},{0,1},{9,8},{11,9},{13,1... | collective-permute-start | bytes 884744 | tf_op jit(solution)/shard_map/ppermute | solution.py:583
  221.7 8.6 %collective-permute-start.63 = (bf16[1,2,96,768]{3,2,1,0:T(8,128)(2,1)S(1)}, bf16[1,2,96,768]{3,2,1,0:T(8,128)(2,1)S(1)}, u32[]{:S(2)}, u32[]{:S(2)}) collective-permute-start(bf16[1,2,96,768]{3,2,1,0:T(8,128)(2,1)S(1)} %get-tuple-element.447), channel_id=1, source_target_pairs={{1,3},{3,5},{5,7},{7,6},{6,4},{4,2},{2,0},{0,1},{9,8},{11,9},{13,1... | collective-permute-start | bytes 884744 | tf_op jit(solution)/shard_map/ppermute | solution.py:583
  227.2 13.2 %collective-permute-start.71 = (bf16[1,2,24,3200]{3,2,1,0:T(8,128)(2,1)S(1)}, bf16[1,2,24,3200]{3,2,1,0:T(8,128)(2,1)S(1)}, u32[]{:S(2)}, u32[]{:S(2)}) collective-permute-start(bf16[1,2,24,3200]{3,2,1,0:T(8,128)(2,1)S(1)} %get-tuple-element.441), channel_id=1, source_target_pairs={{1,3},{3,5},{5,7},{7,6},{6,4},{4,2},{2,0},{0,1},{9,8},{11,9},{13,1... | collective-permute-start | bytes 921608 | tf_op jit(solution)/shard_map/ppermute | solution.py:583
  233.3 7.1 %collective-permute-start.72 = (bf16[96,768]{1,0:T(8,128)(2,1)S(1)}, bf16[96,768]{1,0:T(8,128)(2,1)S(1)}, u32[]{:S(2)}, u32[]{:S(2)}) collective-permute-start(bf16[96,768]{1,0:T(8,128)(2,1)S(1)} %fusion.26), channel_id=1, source_target_pairs={{0,16},{16,0},{1,17},{17,1},{2,18},{18,2},{3,19},{19,3},{4,20},{20... | collective-permute-start | bytes 442376 | tf_op jit(solution)/shard_map/ppermute | solution.py:590
  234.4 13.2 %collective-permute-start.70 = (bf16[1,2,24,3200]{3,2,1,0:T(8,128)(2,1)S(1)}, bf16[1,2,24,3200]{3,2,1,0:T(8,128)(2,1)S(1)}, u32[]{:S(2)}, u32[]{:S(2)}) collective-permute-start(bf16[1,2,24,3200]{3,2,1,0:T(8,128)(2,1)S(1)} %fusion.8), channel_id=1, source_target_pairs={{1,0},{3,1},{5,3},{7,5},{6,7},{4,6},{2,4},{0,2},{9,11},{11,13},{13... | collective-permute-start | bytes 921608 | tf_op jit(solution)/shard_map/ppermute | solution.py:586
  236.5 11.1 %collective-permute-start.68 = (bf16[1,2,24,3072]{3,2,1,0:T(8,128)(2,1)S(1)}, bf16[1,2,24,3072]{3,2,1,0:T(8,128)(2,1)S(1)}, u32[]{:S(2)}, u32[]{:S(2)}) collective-permute-start(bf16[1,2,24,3072]{3,2,1,0:T(8,128)(2,1)S(1)} %get-tuple-element.444), channel_id=1, source_target_pairs={{1,0},{3,1},{5,3},{7,5},{6,7},{4,6},{2,4},{0,2},{9,11},{11,13},{13... | collective-permute-start | bytes 884744 | tf_op jit(solution)/shard_map/ppermute | solution.py:586
  238.3 9.3 %collective-permute-start.69 = (bf16[1,2,24,3072]{3,2,1,0:T(8,128)(2,1)S(1)}, bf16[1,2,24,3072]{3,2,1,0:T(8,128)(2,1)S(1)}, u32[]{:S(2)}, u32[]{:S(2)}) collective-permute-start(bf16[1,2,24,3072]{3,2,1,0:T(8,128)(2,1)S(1)} %get-tuple-element.443), channel_id=1, source_target_pairs={{1,3},{3,5},{5,7},{7,6},{6,4},{4,2},{2,0},{0,1},{9,8},{11,9},{13,1... | collective-permute-start | bytes 884744 | tf_op jit(solution)/shard_map/ppermute | solution.py:583
  248.9 10.0 %collective-permute-start.73 = (bf16[1,2,24,3200]{3,2,1,0:T(8,128)(2,1)S(1)}, bf16[1,2,24,3200]{3,2,1,0:T(8,128)(2,1)S(1)}, u32[]{:S(2)}, u32[]{:S(2)}) collective-permute-start(bf16[1,2,24,3200]{3,2,1,0:T(8,128)(2,1)S(1)} %get-tuple-element.440), channel_id=1, source_target_pairs={{1,0},{3,1},{5,3},{7,5},{6,7},{4,6},{2,4},{0,2},{9,11},{11,13},{13... | collective-permute-start | bytes 921608 | tf_op jit(solution)/shard_map/ppermute | solution.py:586
  249.7 9.2 %collective-permute-start.74 = (bf16[1,2,24,3200]{3,2,1,0:T(8,128)(2,1)S(1)}, bf16[1,2,24,3200]{3,2,1,0:T(8,128)(2,1)S(1)}, u32[]{:S(2)}, u32[]{:S(2)}) collective-permute-start(bf16[1,2,24,3200]{3,2,1,0:T(8,128)(2,1)S(1)} %get-tuple-element.439), channel_id=1, source_target_pairs={{1,3},{3,5},{5,7},{7,6},{6,4},{4,2},{2,0},{0,1},{9,8},{11,9},{13,1... | collective-permute-start | bytes 921608 | tf_op jit(solution)/shard_map/ppermute | solution.py:583
  252.2 5.2 %collective-permute-start.75 = (bf16[24,3072]{1,0:T(8,128)(2,1)S(1)}, bf16[24,3072]{1,0:T(8,128)(2,1)S(1)}, u32[]{:S(2)}, u32[]{:S(2)}) collective-permute-start(bf16[24,3072]{1,0:T(8,128)(2,1)S(1)} %fusion.27), channel_id=1, source_target_pairs={{0,16},{16,0},{1,17},{17,1},{2,18},{18,2},{3,19},{19,3},{4,20},{20... | collective-permute-start | bytes 442376 | tf_op jit(solution)/shard_map/ppermute | solution.py:590
  260.3 9.7 %collective-permute-start.76 = (bf16[1,2,24,3200]{3,2,1,0:T(8,128)(2,1)S(1)}, bf16[1,2,24,3200]{3,2,1,0:T(8,128)(2,1)S(1)}, u32[]{:S(2)}, u32[]{:S(2)}) collective-permute-start(bf16[1,2,24,3200]{3,2,1,0:T(8,128)(2,1)S(1)} %get-tuple-element.438), channel_id=1, source_target_pairs={{1,0},{3,1},{5,3},{7,5},{6,7},{4,6},{2,4},{0,2},{9,11},{11,13},{13... | collective-permute-start | bytes 921608 | tf_op jit(solution)/shard_map/ppermute | solution.py:586
  261.1 8.8 %collective-permute-start.77 = (bf16[1,2,24,3200]{3,2,1,0:T(8,128)(2,1)S(1)}, bf16[1,2,24,3200]{3,2,1,0:T(8,128)(2,1)S(1)}, u32[]{:S(2)}, u32[]{:S(2)}) collective-permute-start(bf16[1,2,24,3200]{3,2,1,0:T(8,128)(2,1)S(1)} %get-tuple-element.437), channel_id=1, source_target_pairs={{1,3},{3,5},{5,7},{7,6},{6,4},{4,2},{2,0},{0,1},{9,8},{11,9},{13,1... | collective-permute-start | bytes 921608 | tf_op jit(solution)/shard_map/ppermute | solution.py:583
  271.1 5.6 %collective-permute-start.78 = (bf16[24,3200]{1,0:T(8,128)(2,1)S(1)}, bf16[24,3200]{1,0:T(8,128)(2,1)S(1)}, u32[]{:S(2)}, u32[]{:S(2)}) collective-permute-start(bf16[24,3200]{1,0:T(8,128)(2,1)S(1)} %fusion.25), channel_id=1, source_target_pairs={{0,16},{16,0},{1,17},{17,1},{2,18},{18,2},{3,19},{19,3},{4,20},{20... | collective-permute-start | bytes 460808 | tf_op jit(solution)/shard_map/ppermute | solution.py:590
  (65 other events, 786.4 us)
